TPU v7x, 32 devices: a whole 2x2x4 slice. The times are simulated.
32 devices in a mesh: dp: 4 (over y, x), expert: 8 (over z, core).
Axes of the slice: x: 2, y: 2, z: 4, core: 2. Of those that a mesh axis runs over, the one named last changes fastest.
Arguments:
- tokens: bfloat16 [4096, 2048], P(('dp', 'expert')), may hold values from -6 to 6
- target: bfloat16 [4096, 2048], P(('dp', 'expert')), may hold values from -6 to 6
- valid: int32 [4096], P(('dp', 'expert')), may hold values from 0 to 1, as said below
- routes: int32 [4096, 6], P('dp'), may hold values from 0 to 15, all different within a row; in each aligned block of 128 rows (0 to 127, 128 to 255, ...) at most 64 rows name the same one
- lengths: int32 [1, 4], replicated, may hold values from 1 to 2048, 4096 in all within a row
- first_gain_vector: float32 [2048], replicated, may hold values from 0.5 to 1.5
- second_gain_vector: float32 [2048], replicated, may hold values from 0.5 to 1.5
- latent_gain_vector: float32 [512], replicated, may hold values from 0.5 to 1.5
- latent_compress_weight: bfloat16 [2048, 576], replicated, may hold values from -0.125 to 0.125
- query_weight: bfloat16 [2048, 3072], P(None, 'expert'), may hold values from -0.125 to 0.125
- latent_expand_weight: bfloat16 [512, 4096], P(None, 'expert'), may hold values from -0.25 to 0.25
- output_weight: bfloat16 [2048, 2048], P('expert'), may hold values from -1.5 to 1.5
- router_weight: bfloat16 [2048, 16], replicated, may hold values from -0.0625 to 0.0625
- shared_gate_weight: bfloat16 [2048, 2816], P(None, 'expert'), may hold values from -0.125 to 0.125
- shared_up_weight: bfloat16 [2048, 2816], P(None, 'expert'), may hold values from -0.125 to 0.125
- shared_down_weight: bfloat16 [2816, 2048], P('expert'), may hold values from -0.109375 to 0.109375
- expert_gate_weight: bfloat16 [16, 2048, 1408], P('expert', 'dp'), may hold values from -0.125 to 0.125
- expert_up_weight: bfloat16 [16, 2048, 1408], P('expert', 'dp'), may hold values from -0.125 to 0.125
- expert_down_weight: bfloat16 [16, 1408, 2048], P('expert', None, 'dp'), may hold values from -0.3125 to 0.3125
Outputs:
- output: bfloat16 [4096, 2048], P(('dp', 'expert'))
- loss: float32 [], replicated
- grad_tokens: float32 [4096, 2048], P(('dp', 'expert'))
- grad_norm1: float32 [2048], replicated
- grad_norm2: float32 [2048], replicated
- grad_latent_gain: float32 [512], replicated
- grad_kva: float32 [2048, 576], replicated
- query_weight_gradient: float32 [2048, 3072], P('dp', 'expert')
- latent_expand_gradient: float32 [512, 4096], P('dp', 'expert')
- output_weight_gradient: float32 [2048, 2048], P('expert', 'dp')
- grad_router: float32 [2048, 16], replicated
- shared_gate_gradient: float32 [2048, 2816], P('dp', 'expert')
- shared_up_gradient: float32 [2048, 2816], P('dp', 'expert')
- shared_down_gradient: float32 [2816, 2048], P('expert', 'dp')
- expert_gate_gradient: float32 [16, 2048, 1408], P('expert', 'dp')
- expert_up_gradient: float32 [16, 2048, 1408], P('expert', 'dp')
- expert_down_gradient: float32 [16, 1408, 2048], P('expert', None, 'dp')
Inputs may be any that keep to these rules, and one draw needn't show every extreme that they name: `routes`: each row names 6 different experts. In each aligned block of 128 rows (the tokens of one device) no expert is named by more than 64 rows, a bound that some block reaches. Each row holds the lengths of the documents of one sequence in order; they sum to 4096, and the longest is exactly half of 4096. `valid`: the first token always counts.
All inputs are finite; a program needn't handle non-finite values.
Results may differ from a plain program's by a relative error of at most 0.025.
Values may be sent and summed in bfloat16 or wider, within the bound.
No kernel may reach another device: no remote copies, remote signals or barrier semaphores. Data moves between devices by JAX's collectives and lax.ppermute only.
A program may use at most 320 MiB of HBM per device.

v0:
```python
import jax
import jax.numpy as jnp
from jax import lax
from jax.sharding import PartitionSpec as P

NOPE = 128
ROPE = 64
VDIM = 128
LATENT = 512
SEQ = 4096
WINDOW = 1024


epsilon = 1e-06
masked_value = -1e30


def passed_along(value, axis, steps):
    count = lax.axis_size(axis)
    first, last = (max(0, -steps), min(count, count - steps))
    return lax.ppermute(value, axis, [(source, source + steps) for source in range(first, last)])


def dot_plain(left, right):
    return lax.dot_general(
        left, right, (((1,), (0,)), ((), ())), preferred_element_type=jnp.float32
    )


def dot_right_t(left, right):
    return lax.dot_general(
        left, right, (((1,), (1,)), ((), ())), preferred_element_type=jnp.float32
    )


def dot_left_t(left, right):
    return lax.dot_general(
        left, right, (((0,), (0,)), ((), ())), preferred_element_type=jnp.float32
    )


def normalize(values):
    factor = lax.rsqrt(jnp.mean(values * values, axis=-1, keepdims=True) + epsilon)
    return (values * factor, factor)


def norm_back(grad_out, unit, factor, gain):
    grad_unit = grad_out * gain
    return factor * (grad_unit - unit * jnp.mean(grad_unit * unit, axis=-1, keepdims=True))


def angles(place, half):
    freq = jnp.exp(-jnp.log(10000.0) * jnp.arange(half, dtype=jnp.float32) / half)
    angle = place.astype(jnp.float32)[:, None] * freq[None, :]
    return (jnp.cos(angle), jnp.sin(angle))


def rotate(values, cosine, sine):
    half = values.shape[-1] // 2
    first, second = (values[..., :half], values[..., half:])
    return jnp.concatenate(
        [first * cosine - second * sine, first * sine + second * cosine], axis=-1
    )


def unrotate(grads, cosine, sine):
    half = grads.shape[-1] // 2
    first, second = (grads[..., :half], grads[..., half:])
    return jnp.concatenate(
        [first * cosine + second * sine, second * cosine - first * sine], axis=-1
    )


def silu_parts(values):
    sigma = jax.nn.sigmoid(values)
    return (values * sigma, sigma * (1.0 + values * (1.0 - sigma)))


def token_meta(first, amount, lengths):
    index = first + jnp.arange(amount, dtype=jnp.int32)
    seq_id = jnp.floor_divide(index, SEQ)
    place = index - seq_id * SEQ
    bounds = jnp.cumsum(lengths, axis=1)
    labels = jnp.arange(lengths.shape[0], dtype=jnp.int32)
    hits = (seq_id[:, None, None] == labels[None, :, None]) & (
        bounds[None, :, :] <= place[:, None, None]
    )
    docs = jnp.sum(hits.astype(jnp.int32), axis=(1, 2))
    return (index, seq_id, place, docs)


def body(
    tokens,
    target,
    valid,
    routes,
    lengths,
    first_gain_vector,
    second_gain_vector,
    latent_gain_vector,
    latent_compress_weight,
    query_weight,
    latent_expand_weight,
    output_weight,
    router_weight,
    shared_gate_weight,
    shared_up_weight,
    shared_down_weight,
    expert_gate_weight,
    expert_up_weight,
    expert_down_weight,
):
    rows, width = tokens.shape
    members = lax.axis_size("expert")
    member = lax.axis_index("expert")
    group = lax.axis_index("dp")
    group_size = rows * members
    head_dim = NOPE + ROPE
    local_heads = query_weight.shape[1] // head_dim
    local_experts = expert_gate_weight.shape[0]
    route_count = routes.shape[1]
    expert_count = router_weight.shape[1]
    capacity = rows * route_count * 4 // (3 * local_experts * members)
    span = max(1, WINDOW // group_size)
    block = min(512, group_size)
    blocks = group_size // block
    score_scale = head_dim ** (-0.5)
    own_start = member * rows
    tokens_float = tokens.astype(jnp.float32)
    own_unit, own_factor = normalize(tokens_float)
    own_normed = (own_unit * first_gain_vector).astype(jnp.bfloat16)
    projected = dot_plain(own_normed, latent_compress_weight)
    own_index, own_seq, own_place, own_docs = token_meta(
        (group * members + member) * rows, rows, lengths
    )
    own_cos, own_sin = angles(own_place, ROPE // 2)
    latent_unit, latent_factor = normalize(projected[:, :LATENT])
    latent = jnp.concatenate(
        [latent_unit * latent_gain_vector, rotate(projected[:, LATENT:], own_cos, own_sin)], axis=1
    ).astype(jnp.bfloat16)
    group_tokens, group_latent = (
        lax.all_gather(tokens, "expert", axis=0, tiled=True),
        lax.all_gather(latent, "expert", axis=0, tiled=True),
    )
    back = 1
    earlier = [passed_along(group_latent, "dp", back)]
    key_latent = jnp.concatenate(earlier + [group_latent], axis=0)
    key_count = key_latent.shape[0]
    group_f = group_tokens.astype(jnp.float32)
    group_unit, group_factor = normalize(group_f)
    normed = (group_unit * first_gain_vector).astype(jnp.bfloat16)
    query_index, query_seq, query_place, query_docs = token_meta(
        group * group_size, group_size, lengths
    )
    key_index, key_seq, key_place, key_docs = token_meta(
        (group - span) * group_size, key_count, lengths
    )
    query_cos, query_sin = angles(query_place, ROPE // 2)
    query_proj = dot_plain(normed, query_weight).reshape(group_size, local_heads, head_dim)
    queries = jnp.concatenate(
        [
            query_proj[..., :NOPE],
            rotate(query_proj[..., NOPE:], query_cos[:, None, :], query_sin[:, None, :]),
        ],
        axis=-1,
    ).astype(jnp.bfloat16)
    key_value = dot_plain(key_latent[:, :LATENT], latent_expand_weight).reshape(
        key_count, local_heads, NOPE + VDIM
    )
    keys = jnp.concatenate(
        [
            key_value[..., :NOPE].astype(jnp.bfloat16),
            jnp.broadcast_to(key_latent[:, None, LATENT:], (key_count, local_heads, ROPE)),
        ],
        axis=-1,
    )
    values = key_value[..., NOPE:].astype(jnp.bfloat16)
    starts = jnp.arange(blocks, dtype=jnp.int32) * block

    def block_scores(start):
        query_block = lax.dynamic_slice_in_dim(queries, start, block, 0)
        key_start = span * group_size + start - WINDOW
        key_block = lax.dynamic_slice_in_dim(keys, key_start, WINDOW + block, 0)
        value_block = lax.dynamic_slice_in_dim(values, key_start, WINDOW + block, 0)
        row_index = lax.dynamic_slice_in_dim(query_index, start, block, 0)
        row_seq = lax.dynamic_slice_in_dim(query_seq, start, block, 0)
        row_doc = lax.dynamic_slice_in_dim(query_docs, start, block, 0)
        col_index = lax.dynamic_slice_in_dim(key_index, key_start, WINDOW + block, 0)
        col_seq = lax.dynamic_slice_in_dim(key_seq, key_start, WINDOW + block, 0)
        col_doc = lax.dynamic_slice_in_dim(key_docs, key_start, WINDOW + block, 0)
        allowed = (
            (col_index[None, :] >= 0)
            & (row_seq[:, None] == col_seq[None, :])
            & (row_doc[:, None] == col_doc[None, :])
        )
        allowed = (
            allowed
            & (row_index[:, None] >= col_index[None, :])
            & (row_index[:, None] - col_index[None, :] < WINDOW)
        )
        scores = (
            jnp.einsum("qhd,khd->hqk", query_block, key_block, preferred_element_type=jnp.float32)
            * score_scale
        )
        scores = jnp.where(allowed[None], scores, masked_value)
        return (query_block, key_block, value_block, scores, key_start)

    def forward_block(start):
        query_block, key_block, value_block, scores, key_start = block_scores(start)
        top = jnp.max(scores, axis=-1, keepdims=True)
        raised = jnp.exp(scores - top)
        total = jnp.sum(raised, axis=-1, keepdims=True)
        probs = (raised / total).astype(jnp.bfloat16)
        mixed = jnp.einsum("hqk,khd->qhd", probs, value_block, preferred_element_type=jnp.float32)
        return (mixed, (top + jnp.log(total))[..., 0])

    mixed_all, log_totals = lax.map(forward_block, starts)
    heads_out = mixed_all.reshape(group_size, local_heads * VDIM).astype(jnp.bfloat16)
    attention = lax.psum(dot_plain(heads_out, output_weight).astype(jnp.bfloat16), "expert").astype(
        jnp.float32
    )
    hidden = group_f + attention
    hidden_unit, hidden_factor = normalize(hidden)
    branch_in = (hidden_unit * second_gain_vector).astype(jnp.bfloat16)
    logits = dot_plain(branch_in, router_weight)
    route_hot = (
        routes[:, :, None] == jnp.arange(expert_count, dtype=jnp.int32)[None, None, :]
    ).astype(jnp.float32)
    chosen = jnp.sum(route_hot * logits[:, None, :], axis=-1)
    raised_gate = jnp.exp(chosen - jnp.max(chosen, axis=1, keepdims=True))
    gates = raised_gate / jnp.sum(raised_gate, axis=1, keepdims=True)
    shared_gate = dot_plain(branch_in, shared_gate_weight)
    shared_up = dot_plain(branch_in, shared_up_weight)
    shared_act, shared_slope = silu_parts(shared_gate)
    shared_hidden = (shared_act * shared_up).astype(jnp.bfloat16)
    shared_part = dot_plain(shared_hidden, shared_down_weight)
    owner_routes = routes.reshape(members, rows * route_count)
    owner_hot = (
        owner_routes[:, :, None] == jnp.arange(expert_count, dtype=jnp.int32)[None, None, :]
    ).astype(jnp.int32)
    ranks = jnp.sum((jnp.cumsum(owner_hot, axis=1) - 1) * owner_hot, axis=2).reshape(
        group_size, route_count
    )
    local_id = routes - member * local_experts
    local_id = jnp.where((local_id >= 0) & (local_id < local_experts), local_id, local_experts)
    sender = jnp.broadcast_to(
        (jnp.arange(group_size, dtype=jnp.int32) // rows)[:, None], routes.shape
    )
    entries = jnp.arange(group_size * route_count, dtype=jnp.int32).reshape(group_size, route_count)
    lookup_table = jnp.full((local_experts, members, capacity), group_size * route_count, jnp.int32)
    lookup_table = (
        lookup_table.at[local_id, sender, ranks]
        .set(entries, mode="drop")
        .reshape(local_experts, members * capacity)
    )
    slot_token = lookup_table // route_count
    padded_in = jnp.concatenate([branch_in, jnp.zeros((1, width), jnp.bfloat16)], axis=0)
    slot_in = padded_in[slot_token]
    gate_pad = jnp.concatenate([gates.reshape(-1), jnp.zeros((1,), jnp.float32)])
    slot_gate = gate_pad[lookup_table]
    full_gate, full_up, full_down = (
        lax.all_gather(expert_gate_weight, "dp", axis=1, tiled=True),
        lax.all_gather(expert_up_weight, "dp", axis=1, tiled=True),
        lax.all_gather(expert_down_weight, "dp", axis=2, tiled=True),
    )
    expert_gate = jnp.einsum("erd,edf->erf", slot_in, full_gate, preferred_element_type=jnp.float32)
    expert_up = jnp.einsum("erd,edf->erf", slot_in, full_up, preferred_element_type=jnp.float32)
    expert_act, expert_slope = silu_parts(expert_gate)
    expert_hidden = (expert_act * expert_up).astype(jnp.bfloat16)
    expert_out = jnp.einsum(
        "erf,efd->erd", expert_hidden, full_down, preferred_element_type=jnp.float32
    ).astype(jnp.bfloat16)
    own_routes = lax.dynamic_slice_in_dim(routes, own_start, rows, 0)
    own_ranks = lax.dynamic_slice_in_dim(ranks, own_start, rows, 0)
    own_gates = lax.dynamic_slice_in_dim(gates, own_start, rows, 0)
    returned = lax.all_to_all(
        expert_out.reshape(local_experts, members, capacity, width),
        "expert",
        split_axis=1,
        concat_axis=1,
        tiled=True,
    )
    picked = returned[own_routes % local_experts, own_routes // local_experts, own_ranks]
    routed_own = jnp.sum(own_gates[:, :, None] * picked.astype(jnp.float32), axis=1)
    branch_own = lax.psum_scatter(
        shared_part.astype(jnp.bfloat16), "expert", scatter_dimension=0, tiled=True
    ).astype(jnp.float32)
    hidden_own = lax.dynamic_slice_in_dim(hidden, own_start, rows, 0)
    result = hidden_own + branch_own + routed_own
    difference = result - target.astype(jnp.float32)
    counted = valid.astype(jnp.float32)
    count, squares = lax.psum(
        (jnp.sum(counted), jnp.sum(counted[:, None] * difference * difference)), ("dp", "expert")
    )
    loss = squares / (count * width)
    total_tokens = rows * members * lax.axis_size("dp")
    grad_out = total_tokens / count * counted[:, None] * difference
    grad_group = lax.all_gather(grad_out.astype(jnp.bfloat16), "expert", axis=0, tiled=True).astype(
        grad_out.dtype
    )
    grad_low = grad_group.astype(jnp.bfloat16)
    shared_down_gradient = dot_left_t(shared_hidden, grad_low)
    grad_shared_hidden = dot_right_t(grad_low, shared_down_weight)
    grad_shared_gate = (grad_shared_hidden * shared_up * shared_slope).astype(jnp.bfloat16)
    grad_shared_up = (grad_shared_hidden * shared_act).astype(jnp.bfloat16)
    shared_gate_gradient = dot_left_t(branch_in, grad_shared_gate)
    shared_up_gradient = dot_left_t(branch_in, grad_shared_up)
    grad_branch = dot_right_t(grad_shared_gate, shared_gate_weight) + dot_right_t(
        grad_shared_up, shared_up_weight
    )
    padded_grad = jnp.concatenate([grad_group, jnp.zeros((1, width), jnp.float32)], axis=0)
    slot_grad = padded_grad[slot_token]
    gate_grad_slot = jnp.sum(slot_grad * expert_out.astype(jnp.float32), axis=-1)
    grad_expert_out = (slot_gate[:, :, None] * slot_grad).astype(jnp.bfloat16)
    grad_expert_hidden = jnp.einsum(
        "erd,efd->erf", grad_expert_out, full_down, preferred_element_type=jnp.float32
    )
    expert_down_gradient = jnp.einsum(
        "erf,erd->efd", expert_hidden, grad_expert_out, preferred_element_type=jnp.float32
    )
    grad_expert_gate = (grad_expert_hidden * expert_up * expert_slope).astype(jnp.bfloat16)
    grad_expert_up = (grad_expert_hidden * expert_act).astype(jnp.bfloat16)
    expert_gate_gradient = jnp.einsum(
        "erd,erf->edf", slot_in, grad_expert_gate, preferred_element_type=jnp.float32
    )
    expert_up_gradient = jnp.einsum(
        "erd,erf->edf", slot_in, grad_expert_up, preferred_element_type=jnp.float32
    )
    grad_slot_in = (
        jnp.einsum("erf,edf->erd", grad_expert_gate, full_gate, preferred_element_type=jnp.float32)
        + jnp.einsum("erf,edf->erd", grad_expert_up, full_up, preferred_element_type=jnp.float32)
    ).astype(jnp.bfloat16)
    gate_grad = (
        jnp.zeros((group_size * route_count + 1,), jnp.float32)
        .at[lookup_table.reshape(-1)]
        .add(gate_grad_slot.reshape(-1))
    )
    gate_grad = gate_grad[: group_size * route_count].reshape(group_size, route_count)
    chosen_grad = gates * (gate_grad - jnp.sum(gates * gate_grad, axis=1, keepdims=True))
    logit_grad = jnp.sum(route_hot * chosen_grad[:, :, None], axis=1)
    grad_router = jnp.einsum("td,te->de", branch_in, logit_grad, preferred_element_type=jnp.float32)
    grad_branch = grad_branch + jnp.einsum(
        "te,de->td",
        logit_grad,
        router_weight.astype(jnp.float32),
        preferred_element_type=jnp.float32,
    )
    came_back = lax.all_to_all(
        grad_slot_in.reshape(local_experts, members, capacity, width),
        "expert",
        split_axis=1,
        concat_axis=1,
        tiled=True,
    )
    picked_grad = came_back[own_routes % local_experts, own_routes // local_experts, own_ranks]
    own_part = lax.dynamic_slice_in_dim(grad_branch, own_start, rows, 0) + jnp.sum(
        picked_grad.astype(jnp.float32), axis=1
    )
    grad_branch = lax.dynamic_update_slice_in_dim(grad_branch, own_part, own_start, 0)
    grad_branch = lax.psum(grad_branch.astype(jnp.bfloat16), "expert").astype(jnp.float32)
    grad_hidden = grad_group + norm_back(
        grad_branch, hidden_unit, hidden_factor, second_gain_vector
    )
    own_branch_grad = lax.dynamic_slice_in_dim(grad_branch, own_start, rows, 0)
    own_hidden_unit = lax.dynamic_slice_in_dim(hidden_unit, own_start, rows, 0)
    grad_norm2 = jnp.sum(own_branch_grad * own_hidden_unit, axis=0)
    grad_attention = grad_hidden.astype(jnp.bfloat16)
    output_weight_gradient = dot_left_t(heads_out, grad_attention)
    grad_heads = (
        dot_right_t(grad_attention, output_weight)
        .astype(jnp.bfloat16)
        .reshape(blocks, block, local_heads, VDIM)
    )

    def backward_block(carry, items):
        key_grad, value_grad = carry
        start, grad_mixed, log_total = items
        query_block, key_block, value_block, scores, key_start = block_scores(start)
        probs = jnp.exp(scores - log_total[..., None])
        prob_grad = jnp.einsum(
            "qhd,khd->hqk", grad_mixed, value_block, preferred_element_type=jnp.float32
        )
        value_piece = jnp.einsum(
            "hqk,qhd->khd",
            probs.astype(jnp.bfloat16),
            grad_mixed,
            preferred_element_type=jnp.float32,
        )
        score_grad = (
            probs * (prob_grad - jnp.sum(probs * prob_grad, axis=-1, keepdims=True))
        ).astype(jnp.bfloat16)
        query_piece = (
            jnp.einsum("hqk,khd->qhd", score_grad, key_block, preferred_element_type=jnp.float32)
            * score_scale
        )
        key_piece = (
            jnp.einsum("hqk,qhd->khd", score_grad, query_block, preferred_element_type=jnp.float32)
            * score_scale
        )
        key_grad = lax.dynamic_update_slice_in_dim(
            key_grad,
            lax.dynamic_slice_in_dim(key_grad, key_start, WINDOW + block, 0) + key_piece,
            key_start,
            0,
        )
        value_grad = lax.dynamic_update_slice_in_dim(
            value_grad,
            lax.dynamic_slice_in_dim(value_grad, key_start, WINDOW + block, 0) + value_piece,
            key_start,
            0,
        )
        return ((key_grad, value_grad), query_piece)

    initial = (
        jnp.zeros((key_count, local_heads, head_dim), jnp.float32),
        jnp.zeros((key_count, local_heads, VDIM), jnp.float32),
    )
    (key_grad, value_grad), query_grad = lax.scan(
        backward_block, initial, (starts, grad_heads, log_totals)
    )
    query_grad = query_grad.reshape(group_size, local_heads, head_dim)
    query_proj_grad = jnp.concatenate(
        [
            query_grad[..., :NOPE],
            unrotate(query_grad[..., NOPE:], query_cos[:, None, :], query_sin[:, None, :]),
        ],
        axis=-1,
    )
    query_proj_grad = query_proj_grad.reshape(group_size, local_heads * head_dim).astype(
        jnp.bfloat16
    )
    query_weight_gradient = dot_left_t(normed, query_proj_grad)
    grad_normed = dot_right_t(query_proj_grad, query_weight)
    grad_kv = (
        jnp.concatenate([key_grad[..., :NOPE], value_grad], axis=-1)
        .reshape(key_count, local_heads * (NOPE + VDIM))
        .astype(jnp.bfloat16)
    )
    latent_expand_gradient = dot_left_t(key_latent[:, :LATENT], grad_kv)
    grad_key_latent = jnp.concatenate(
        [dot_right_t(grad_kv, latent_expand_weight), jnp.sum(key_grad[..., NOPE:], axis=1)], axis=1
    )
    own_latent_grad = grad_key_latent[span * group_size :]
    back = 1
    piece = grad_key_latent[(span - back) * group_size : (span - back + 1) * group_size]
    own_latent_grad = own_latent_grad + passed_along(
        piece.astype(jnp.bfloat16), "dp", -back
    ).astype(piece.dtype)
    grad_normed_own, grad_latent_own = (
        lax.psum_scatter(
            grad_normed.astype(jnp.bfloat16), "expert", scatter_dimension=0, tiled=True
        ).astype(jnp.float32),
        lax.psum_scatter(
            own_latent_grad.astype(jnp.bfloat16), "expert", scatter_dimension=0, tiled=True
        ).astype(jnp.float32),
    )
    grad_latent_gain = jnp.sum(grad_latent_own[:, :LATENT] * latent_unit, axis=0)
    grad_projected = jnp.concatenate(
        [
            norm_back(grad_latent_own[:, :LATENT], latent_unit, latent_factor, latent_gain_vector),
            unrotate(grad_latent_own[:, LATENT:], own_cos, own_sin),
        ],
        axis=1,
    ).astype(jnp.bfloat16)
    grad_kva = dot_left_t(own_normed, grad_projected)
    grad_normed_own = grad_normed_own + dot_right_t(grad_projected, latent_compress_weight)
    grad_norm1 = jnp.sum(grad_normed_own * own_unit, axis=0)
    grad_tokens = lax.dynamic_slice_in_dim(grad_hidden, own_start, rows, 0) + norm_back(
        grad_normed_own, own_unit, own_factor, first_gain_vector
    )
    (
        query_weight_gradient,
        latent_expand_gradient,
        output_weight_gradient,
        shared_gate_gradient,
        shared_up_gradient,
        shared_down_gradient,
        expert_gate_gradient,
        expert_up_gradient,
        expert_down_gradient,
    ) = (
        lax.psum_scatter(
            query_weight_gradient.astype(jnp.bfloat16), "dp", scatter_dimension=0, tiled=True
        ).astype(jnp.float32),
        lax.psum_scatter(
            latent_expand_gradient.astype(jnp.bfloat16), "dp", scatter_dimension=0, tiled=True
        ).astype(jnp.float32),
        lax.psum_scatter(
            output_weight_gradient.astype(jnp.bfloat16), "dp", scatter_dimension=1, tiled=True
        ).astype(jnp.float32),
        lax.psum_scatter(
            shared_gate_gradient.astype(jnp.bfloat16), "dp", scatter_dimension=0, tiled=True
        ).astype(jnp.float32),
        lax.psum_scatter(
            shared_up_gradient.astype(jnp.bfloat16), "dp", scatter_dimension=0, tiled=True
        ).astype(jnp.float32),
        lax.psum_scatter(
            shared_down_gradient.astype(jnp.bfloat16), "dp", scatter_dimension=1, tiled=True
        ).astype(jnp.float32),
        lax.psum_scatter(
            expert_gate_gradient.astype(jnp.bfloat16), "dp", scatter_dimension=1, tiled=True
        ).astype(jnp.float32),
        lax.psum_scatter(
            expert_up_gradient.astype(jnp.bfloat16), "dp", scatter_dimension=1, tiled=True
        ).astype(jnp.float32),
        lax.psum_scatter(
            expert_down_gradient.astype(jnp.bfloat16), "dp", scatter_dimension=2, tiled=True
        ).astype(jnp.float32),
    )
    grad_norm1, grad_norm2, grad_latent_gain, grad_kva, grad_router = lax.psum(
        (grad_norm1, grad_norm2, grad_latent_gain, grad_kva, grad_router), ("dp", "expert")
    )
    return (
        result.astype(jnp.bfloat16),
        loss,
        grad_tokens,
        grad_norm1,
        grad_norm2,
        grad_latent_gain,
        grad_kva,
        query_weight_gradient,
        latent_expand_gradient,
        output_weight_gradient,
        grad_router,
        shared_gate_gradient,
        shared_up_gradient,
        shared_down_gradient,
        expert_gate_gradient,
        expert_up_gradient,
        expert_down_gradient,
    )


def solution(mesh):
    placed = (
        P(("dp", "expert"), None),
        P(("dp", "expert"), None),
        P(("dp", "expert")),
        P("dp", None),
        P(),
        P(),
        P(),
        P(),
        P(),
        P(None, "expert"),
        P(None, "expert"),
        P("expert", None),
        P(),
        P(None, "expert"),
        P(None, "expert"),
        P("expert", None),
        P("expert", "dp", None),
        P("expert", "dp", None),
        P("expert", None, "dp"),
    )
    return jax.shard_map(
        body,
        mesh=mesh,
        in_specs=placed,
        out_specs=(
            P(("dp", "expert"), None),
            P(),
            P(("dp", "expert"), None),
            P(),
            P(),
            P(),
            P(),
            P("dp", "expert"),
            P("dp", "expert"),
            P("expert", "dp"),
            P(),
            P("dp", "expert"),
            P("dp", "expert"),
            P("expert", "dp"),
            P("expert", "dp", None),
            P("expert", "dp", None),
            P("expert", None, "dp"),
        ),
        check_vma=False,
    )
```

profile of v0, /device:TPU:0, one launch (start us, length us, event | category | flops | bytes accessed | tf_op | source)
XLA Modules:
  0.0 1841.2 jit_solution(18379527574127889507)
XLA Ops:
  15.4 26.3 %all-gather.9.cloned.1.call-done = bf16[1024,576]{0,1:T(8,128)(2,1)} async-done(((bf16[128,576]{0,1:T(8,128)(2,1)}), bf16[1024,576]{0,1:T(8,128)(2,1)}) %all-gather.9.cloned.1.call-update) | async-done | bytes 1179664 | tf_op jit(solution)/shard_map/all_gather | solution.py:143
  51.7 18.2 collective-permute-done
  80.3 8.9 all-gather.7.cloned.1.call-done
  97.4 31.3 %while.34 = (s32[]{:T(128)}, bf16[2,512,2,128]{1,3,2,0:T(8,128)(2,1)}, f32[2,2,512]{2,1,0:T(2,128)}, s32[2]{0:T(128)S(1)}, bf16[2048,2,128]{2,0,1:T(8,128)(2,1)S...) while((s32[]{:T(128)}, ...), condition=%wide.region_9.10_spmd, body=%wide.region_6.9_spmd.sunk | while | flops 1032585728 | bytes 25014536 | solution.py:217
  139.2 24.2 %reduce-window.18 = s32[8,16,6,128]{3,1,2,0:T(8,128)S(1)} reduce-window(s32[8,16,6,128]{3,1,2,0:T(8,128)} %fusion.79, s32[]{:T(128)} %constant.309.clone.1), window={size=1x1x1x128 pad=0_0x0_0x0_0x127_0}, to_apply=%region_16.17 | reduce-window | flops 12484608 | bytes 786436 | tf_op jit(solution)/shard_map/reduce-window
  169.8 23.0 %scatter_custom_fusion.1 = s32[1024]{0:T(1024)S(1)} fusion(s32[6144]{0:T(1024)S(1)} %reshape.1109, s32[6144]{0:T(1024)S(1)} %reshape.1111, s32[]{:T(128)} %constant.329.clone.1), kind=kCustom, calls=%fused_computation.273 | custom fusion | bytes 4100
  193.4 37.7 %all-reduce.8.cloned.1.call-done = bf16[1024,2048]{1,0:T(8,128)(2,1)} async-done(((bf16[1024,2048]{1,0:T(8,128)(2,1)}), bf16[1024,2048]{1,0:T(8,128)(2,1)}) %all-reduce.8.cloned.1.call-update) | async-done | bytes 4194320 | tf_op jit(solution)/shard_map/psum | solution.py:219
  231.1 8.2 convert_add_fusion
  248.5 11.6 gather_fusion
  274.5 13.4 fusion.140
  287.9 78.0 %all-gather.13.cloned.1.call-done = bf16[2,2048,1408]{2,1,0:T(8,128)(2,1)} async-done(((bf16[2,512,1408]{2,1,0:T(8,128)(2,1)}), bf16[2,2048,1408]{2,1,0:T(8,128)(2,1)}) %all-gather.13.cloned.1.call-update) | async-done | bytes 11534352 | tf_op jit(solution)/shard_map/all_gather | solution.py:263
  365.8 15.0 multiply_convert_fusion.5
  380.8 100.2 %all-gather.15.cloned.1.call-done = bf16[2,1408,2048]{2,1,0:T(8,128)(2,1)} async-done(((bf16[2,1408,512]{2,1,0:T(8,128)(2,1)}), bf16[2,1408,2048]{2,1,0:T(8,128)(2,1)}) %all-gather.15.cloned.1.call-update) | async-done | bytes 11534352 | tf_op jit(solution)/shard_map/all_gather | solution.py:264
  481.0 10.4 convolution_convert_fusion.3
  501.2 112.7 %psum.65 = f32[]{:T(128)} all-reduce(f32[]{:T(128)} %convert_reduce_fusion.2), channel_id=1, replica_groups=mesh['dp'=4,'expert'=8] {'dp','expert'}, use_global_device_ids=true, to_apply=%region_24.25 | all-reduce | flops 1 | bytes 8 | tf_op jit(solution)/shard_map/psum | solution.py:292
  625.9 15.5 gather_fusion.1
  641.4 6.5 reshape.1118
  647.9 6.5 multiply_reduce_fusion.3
  664.3 41.4 %all-gather.17.cloned.1.call-done = bf16[1024,2048]{1,0:T(8,128)(2,1)} async-done(((bf16[128,2048]{1,0:T(8,128)(2,1)}), bf16[1024,2048]{1,0:T(8,128)(2,1)}) %all-gather.17.cloned.1.call-update) | async-done | bytes 4194320 | tf_op jit(solution)/shard_map/all_gather | solution.py:298
  705.7 6.6 concatenate.52
  712.3 12.7 gather_fusion.2
  725.0 15.8 multiply_convert_fusion.3
  740.9 12.5 fusion.143
  753.3 11.6 add_convert_fusion
  777.8 7.7 scatter_custom_fusion
  801.5 64.8 %all-to-all-done.1 = bf16[2,8,64,2048]{3,2,0,1:T(8,128)(2,1)} async-done(((bf16[2,8,64,2048]{3,2,0,1:T(8,128)(2,1)}), bf16[2,8,64,2048]{3,2,0,1:T(8,128)(2,1)}, u32[]{:S(2)}, u32[]{:S(2)}) %all-to-all-start.1) | async-done | bytes 4194336 | tf_op jit(solution)/shard_map/all_to_all | solution.py:348
  871.1 15.6 gather_fusion.4
  907.7 95.4 %all-reduce.10.cloned.1.call-done = bf16[1024,2048]{1,0:T(8,128)(2,1)} async-done(((bf16[1024,2048]{1,0:T(8,128)(2,1)}), bf16[1024,2048]{1,0:T(8,128)(2,1)}) %all-reduce.10.cloned.1.call-update) | async-done | bytes 4194320 | tf_op jit(solution)/shard_map/psum | solution.py:360
  1026.6 132.2 %while.35 = (s32[]{:T(128)}, f32[2048,2,192]{0,2,1:T(8,128)}, f32[2048,2,128]{0,2,1:T(8,128)}, f32[2,512,2,192]{1,0,3,2:T(2,128)}, s32[2]{0:T(128)S(1)}, /*index...) while((s32[]{:T(128)}, f32[2048,2,192]{0,2,1:T(8,128)}, ...), condition=%wide.region_34.35_spmd, body=%wide.region_32.34_spmd.sunk | while | flops 2640249344 | bytes 158432752 | solution.py:418
  1049.8 10.8 dynamic_update_slice.62
  1065.0 15.0 dynamic_update_slice.64
  1085.1 8.3 dynamic_update_slice.63
  1116.2 10.4 dynamic_update_slice.62
  1130.8 15.0 dynamic_update_slice.64
  1151.0 7.8 dynamic_update_slice.63
  1165.4 28.1 %collective-permute-done.1 = bf16[1024,576]{0,1:T(8,128)(2,1)S(1)} collective-permute-done((bf16[1024,576]{0,1:T(8,128)(2,1)S(1)}, bf16[1024,576]{0,1:T(8,128)(2,1)S(1)}, u32[]{:S(2)}, u32[]{:S(2)}) %collective-permute-start.1) | collective-permute-done | bytes 1179680 | tf_op jit(solution)/shard_map/ppermute | solution.py:21
  1240.3 12.3 convolution_convert_fusion
  1252.7 11.9 convolution_convert_fusion.2
  1264.9 11.8 convolution_convert_fusion.1
  1296.6 32.5 %reduce-scatter.27.cloned.1.call-done = bf16[512,352]{0,1:T(8,128)(2,1)} async-done(((bf16[2048,352]{0,1:T(8,128)(2,1)}), bf16[512,352]{0,1:T(8,128)(2,1)}) %reduce-scatter.27.cloned.1.call-update) | async-done | bytes 360464 | tf_op jit(solution)/shard_map/reduce_scatter | solution.py:494
  1335.7 21.9 %reduce-scatter.21.cloned.1.call-done = bf16[128,512]{1,0:T(8,128)(2,1)} async-done(((bf16[512,512]{1,0:T(8,128)(2,1)}), bf16[128,512]{1,0:T(8,128)(2,1)}) %reduce-scatter.21.cloned.1.call-update) | async-done | bytes 131088 | tf_op jit(solution)/shard_map/reduce_scatter | solution.py:485
  1359.2 29.0 %reduce-scatter.23.cloned.1.call-done = bf16[256,512]{1,0:T(8,128)(2,1)} async-done(((bf16[256,2048]{1,0:T(8,128)(2,1)}), bf16[256,512]{1,0:T(8,128)(2,1)}) %reduce-scatter.23.cloned.1.call-update) | async-done | bytes 262160 | tf_op jit(solution)/shard_map/reduce_scatter | solution.py:488
  1390.1 33.6 %reduce-scatter.19.cloned.1.call-done = bf16[512,384]{1,0:T(8,128)(2,1)} async-done(((bf16[2048,384]{1,0:T(8,128)(2,1)}), bf16[512,384]{1,0:T(8,128)(2,1)}) %reduce-scatter.19.cloned.1.call-update) | async-done | bytes 393232 | tf_op jit(solution)/shard_map/reduce_scatter | solution.py:482
  1425.6 51.0 %reduce-scatter.17.cloned.1.call-done = bf16[128,2048]{1,0:T(8,128)(2,1)} async-done(((bf16[1024,2048]{1,0:T(8,128)(2,1)}), bf16[128,2048]{1,0:T(8,128)(2,1)}) %reduce-scatter.17.cloned.1.call-update) | async-done | bytes 524304 | tf_op jit(solution)/shard_map/reduce_scatter | solution.py:450
  1479.4 38.7 %all-reduce.2 = (f32[]{:T(128)}, f32[2048]{0:T(1024)}, f32[2048]{0:T(1024)}, f32[512]{0:T(512)}) all-reduce(f32[]{:T(128)} %get-tuple-element.829, f32[2048]{0:T(1024)S(1)} %get-tuple-element.737, f32[2048]{0:T(1024)S(1)} %multiply_reduce_fusion.5, f32[512]{0:T(512)S(1)} %copy-done.71), channel_id=1, replica_groups=mesh['dp'=4,'expert'=8] {'dp','expert'}, use_global_device_ids=true, to_apply=%region_22.23 | all-reduce | flops 4609 | bytes 36872 | tf_op jit(solution)/shard_map/psum | solution.py:292
  1521.7 69.4 %reduce-scatter.35.cloned.1.call-done = bf16[2,1408,512]{2,1,0:T(8,128)(2,1)} async-done(((bf16[2,1408,2048]{2,1,0:T(8,128)(2,1)}), bf16[2,1408,512]{2,1,0:T(8,128)(2,1)}) %reduce-scatter.35.cloned.1.call-update) | async-done | bytes 2883600 | tf_op jit(solution)/shard_map/reduce_scatter | solution.py:506
  1596.2 110.3 %reduce-scatter.31.cloned.1.call-done = bf16[2,512,1408]{2,1,0:T(8,128)(2,1)} async-done(((bf16[2,2048,1408]{2,1,0:T(8,128)(2,1)}), bf16[2,512,1408]{2,1,0:T(8,128)(2,1)}) %reduce-scatter.31.cloned.1.call-update) | async-done | bytes 2883600 | tf_op jit(solution)/shard_map/reduce_scatter | solution.py:500
  1711.2 110.7 %reduce-scatter.33.cloned.1.call-done = bf16[2,512,1408]{2,1,0:T(8,128)(2,1)} async-done(((bf16[2,2048,1408]{2,1,0:T(8,128)(2,1)}), bf16[2,512,1408]{2,1,0:T(8,128)(2,1)}) %reduce-scatter.33.cloned.1.call-update) | async-done | bytes 2883600 | tf_op jit(solution)/shard_map/reduce_scatter | solution.py:503
  (477 shorter events, 378.3 us)
Async XLA Ops:
  8.0 36.6 %copy-start.88 = (s32[1,4]{1,0:T(1,128)S(1)}, s32[1,4]{1,0:T(1,128)}, u32[]{:S(2)}) copy-start(s32[1,4]{1,0:T(1,128)} %param.27) | copy-start | bytes 52
  8.0 33.6 %all-gather.9.cloned.1.call-start = ((), (), s32[]{:S(2)}) async-start(), calls=%async_computation.15 | async-start | bytes 1327104 | tf_op jit(solution)/shard_map/all_gather | solution.py:143
  14.0 75.2 %all-gather.7.cloned.1.call-start = ((), (), s32[]{:S(2)}) async-start(), calls=%async_computation.14 | async-start | bytes 4718592 | tf_op jit(solution)/shard_map/all_gather | solution.py:142
  14.8 216.3 %all-reduce.8.cloned.1.call-start = ((), (), s32[]{:S(2)}) async-start(), calls=%async_computation.16 | async-start | bytes 8388608 | tf_op jit(solution)/shard_map/psum | solution.py:219
  41.6 28.3 %collective-permute-start = (bf16[1024,576]{0,1:T(8,128)(2,1)}, bf16[1024,576]{0,1:T(8,128)(2,1)S(1)}, u32[]{:S(2)}, u32[]{:S(2)}) collective-permute-start(bf16[1024,576]{0,1:T(8,128)(2,1)} %all-gather.9.cloned.1.call-done), channel_id=1, source_target_pairs={{0,8},{8,16},{16,24},{1,9},{9,17},{17,25},{2,10},{10,18},{18,26},{... | collective-permute-start | bytes 3538952 | tf_op jit(solution)/shard_map/ppermute | solution.py:21
  45.3 26.8 %copy-start.44 = (bf16[512,512]{1,0:T(8,128)(2,1)S(1)}, bf16[512,512]{1,0:T(8,128)(2,1)}, u32[]{:S(2)}) copy-start(bf16[512,512]{1,0:T(8,128)(2,1)} %param.33) | copy-start | bytes 1572868
  76.7 15.8 copy-start.56
  135.7 138.8 %all-gather.11.cloned.1.call-start = ((), (), s32[]{:S(2)}) async-start(), calls=%async_computation.18 | async-start | bytes 14417920 | tf_op jit(solution)/shard_map/all_gather | solution.py:262
  136.3 229.5 %all-gather.13.cloned.1.call-start = ((), (), s32[]{:S(2)}) async-start(), calls=%async_computation.19 | async-start | bytes 14417920 | tf_op jit(solution)/shard_map/all_gather | solution.py:263
  136.9 31.7 %copy-start.69 = (s32[1024]{0:T(1024)S(1)}, s32[1024]{0:T(1024)}, u32[]{:S(2)}) copy-start(s32[1024]{0:T(1024)} %get-tuple-element.847) | copy-start | bytes 12292
  136.9 31.7 %copy-start.70 = (s32[1024]{0:T(1024)S(1)}, s32[1024]{0:T(1024)}, u32[]{:S(2)}) copy-start(s32[1024]{0:T(1024)} %get-tuple-element.844) | copy-start | bytes 12292
  136.9 31.7 %copy-start.82 = (pred[1024]{0:T(1024)(128)(4,1)S(1)}, pred[1024]{0:T(1024)(128)(4,1)}, u32[]{:S(2)}) copy-start(pred[1024]{0:T(1024)(128)(4,1)} %get-tuple-element.849) | copy-start | bytes 3076
  136.9 344.1 %all-gather.15.cloned.1.call-start = ((), (), s32[]{:S(2)}) async-start(), calls=%async_computation.20 | async-start | bytes 14417920 | tf_op jit(solution)/shard_map/all_gather | solution.py:264
  137.5 31.2 %copy-start.86 = (s32[3]{0:T(128)S(1)}, s32[3]{0:T(128)}, u32[]{:S(2)}) copy-start(s32[3]{0:T(128)} %constant.347) | copy-start | bytes 40
  137.5 31.3 %copy-start.85 = (s32[3]{0:T(128)S(1)}, s32[3]{0:T(128)}, u32[]{:S(2)}) copy-start(s32[3]{0:T(128)} %constant.350) | copy-start | bytes 40
  137.5 517.0 %reduce-scatter.15.cloned.1.call-start = ((), (), s32[]{:S(2)}) async-start(), calls=%async_computation.17 | async-start | bytes 4718592 | tf_op jit(solution)/shard_map/reduce_scatter | solution.py:285
  193.4 45.9 %copy-start.59 = (f32[2048]{0:T(1024)S(1)}, f32[2048]{0:T(1024)}, u32[]{:S(2)}) copy-start(f32[2048]{0:T(1024)} %param.29) | copy-start | bytes 24580
  231.1 8.2 copy-start.11
  231.1 8.2 copy-start.16
  495.8 121.0 %copy-start.48 = (bf16[2048,16]{0,1:T(8,128)(2,1)S(1)}, bf16[2048,16]{0,1:T(8,128)(2,1)}, u32[]{:S(2)}) copy-start(bf16[2048,16]{0,1:T(8,128)(2,1)} %param.35) | copy-start | bytes 196612
  495.8 125.3 %all-to-all-start = ((bf16[2,8,64,2048]{3,2,0,1:T(8,128)(2,1)}), bf16[2,8,64,2048]{3,2,0,1:T(8,128)(2,1)}, u32[]{:S(2)}, u32[]{:S(2)}) async-start(bf16[2,8,64,2048]{3,2,0,1:T(8,128)(2,1)} %copy.120), calls=%async_computation.1 | async-start | bytes 8388608 | tf_op jit(solution)/shard_map/all_to_all | solution.py:276
  500.5 205.2 %all-gather.17.cloned.1.call-start = ((), (), s32[]{:S(2)}) async-start(), calls=%async_computation.21 | async-start | bytes 4718592 | tf_op jit(solution)/shard_map/all_gather | solution.py:298
  664.3 60.7 %copy-start.80 = (f32[2,512]{1,0:T(2,128)}, f32[2,512]{1,0:T(2,128)S(1)}, u32[]{:S(2)}) copy-start(f32[2,512]{1,0:T(2,128)S(1)} %reshape.1088) | copy-start | bytes 12292
  767.5 98.8 %all-to-all-start.1 = ((bf16[2,8,64,2048]{3,2,0,1:T(8,128)(2,1)}), bf16[2,8,64,2048]{3,2,0,1:T(8,128)(2,1)}, u32[]{:S(2)}, u32[]{:S(2)}) async-start(bf16[2,8,64,2048]{3,2,0,1:T(8,128)(2,1)} %copy.126), calls=%async_computation.2 | async-start | bytes 8388608 | tf_op jit(solution)/shard_map/all_to_all | solution.py:348
  772.3 230.8 %all-reduce.10.cloned.1.call-start = ((), (), s32[]{:S(2)}) async-start(), calls=%async_computation.22 | async-start | bytes 8388608 | tf_op jit(solution)/shard_map/psum | solution.py:360
  786.3 10.5 copy-start.46
  907.6 95.5 %copy-start.60 = (f32[2048]{0:T(1024)S(1)}, f32[2048]{0:T(1024)}, u32[]{:S(2)}) copy-start(f32[2048]{0:T(1024)} %param.29) | copy-start | bytes 24580
  907.6 373.5 %reduce-scatter.37.cloned.1.call-start = ((), (), s32[]{:S(2)}) async-start(), calls=%async_computation.33 | async-start | bytes 1474560
  1010.1 8.7 copy-start.24
  1039.9 7.6 copy-start.5
  1080.0 13.5 copy-start.19
  1106.3 7.6 copy-start.5
  1145.8 13.0 copy-start.19
  1163.9 29.5 %collective-permute-start.1 = (bf16[1024,576]{0,1:T(8,128)(2,1)S(1)}, bf16[1024,576]{0,1:T(8,128)(2,1)S(1)}, u32[]{:S(2)}, u32[]{:S(2)}) collective-permute-start(bf16[1024,576]{0,1:T(8,128)(2,1)S(1)} %fusion.43), channel_id=1, source_target_pairs={{8,0},{16,8},{24,16},{9,1},{17,9},{25,17},{10,2},{18,10},{26,18},{... | collective-permute-start | bytes 3538952 | tf_op jit(solution)/shard_map/ppermute | solution.py:21
  1195.3 97.4 %reduce-scatter.29.cloned.1.call-start = ((), (), s32[]{:S(2)}) async-start(), calls=%async_computation.29 | async-start | bytes 1802240 | tf_op jit(solution)/shard_map/reduce_scatter | solution.py:497
  1200.6 94.1 %reduce-scatter.25.cloned.1.call-start = ((), (), s32[]{:S(2)}) async-start(), calls=%async_computation.27 | async-start | bytes 1802240 | tf_op jit(solution)/shard_map/reduce_scatter | solution.py:491
  1206.0 123.1 %reduce-scatter.27.cloned.1.call-start = ((), (), s32[]{:S(2)}) async-start(), calls=%async_computation.28 | async-start | bytes 1802240 | tf_op jit(solution)/shard_map/reduce_scatter | solution.py:494
  1211.2 146.4 %reduce-scatter.21.cloned.1.call-start = ((), (), s32[]{:S(2)}) async-start(), calls=%async_computation.25 | async-start | bytes 655360 | tf_op jit(solution)/shard_map/reduce_scatter | solution.py:485
  1215.6 172.7 %reduce-scatter.23.cloned.1.call-start = ((), (), s32[]{:S(2)}) async-start(), calls=%async_computation.26 | async-start | bytes 1310720 | tf_op jit(solution)/shard_map/reduce_scatter | solution.py:488
  1221.4 202.3 %reduce-scatter.19.cloned.1.call-start = ((), (), s32[]{:S(2)}) async-start(), calls=%async_computation.24 | async-start | bytes 1966080 | tf_op jit(solution)/shard_map/reduce_scatter | solution.py:482
  1233.6 243.0 %reduce-scatter.17.cloned.1.call-start = ((), (), s32[]{:S(2)}) async-start(), calls=%async_computation.23 | async-start | bytes 4718592 | tf_op jit(solution)/shard_map/reduce_scatter | solution.py:450
  1239.7 351.4 %reduce-scatter.35.cloned.1.call-start = ((), (), s32[]{:S(2)}) async-start(), calls=%async_computation.32 | async-start | bytes 14417920 | tf_op jit(solution)/shard_map/reduce_scatter | solution.py:506
  1252.7 453.8 %reduce-scatter.31.cloned.1.call-start = ((), (), s32[]{:S(2)}) async-start(), calls=%async_computation.30 | async-start | bytes 14417920 | tf_op jit(solution)/shard_map/reduce_scatter | solution.py:500
  1264.6 557.3 %reduce-scatter.33.cloned.1.call-start = ((), (), s32[]{:S(2)}) async-start(), calls=%async_computation.31 | async-start | bytes 14417920 | tf_op jit(solution)/shard_map/reduce_scatter | solution.py:503
  1276.9 549.8 %all-reduce.12.cloned.1.call-start = ((), (), s32[]{:S(2)}) async-start(), calls=%async_computation.34 | async-start | bytes 9699328 | tf_op jit(solution)/shard_map/psum | solution.py:510
  1334.3 142.3 %copy-start.62 = (bf16[128,32]{0,1:T(8,128)(2,1)S(1)}, bf16[128,32]{0,1:T(8,128)(2,1)}, u32[]{:S(2)}) copy-start(bf16[128,32]{0,1:T(8,128)(2,1)} %copy-done.61) | copy-start | bytes 24580
  1334.3 142.3 %copy-start.73 = (f32[128]{0:T(128)S(1)}, f32[128]{0:T(128)}, u32[]{:S(2)}) copy-start(f32[128]{0:T(128)} %copy-done.72) | copy-start | bytes 1540
  1334.3 145.1 %copy-start.71 = (f32[512]{0:T(512)S(1)}, f32[512]{0:T(512)}, u32[]{:S(2)}) copy-start(f32[512]{0:T(512)} %get-tuple-element.739) | copy-start | bytes 6148
  (77 other events, 330.5 us)
Sparse Core Ops, SparseCore 0:
  14.1 27.4 all-gather.8
  43.2 45.9 all-gather.6
  135.8 95.2 all-reduce.7
  274.6 50.1 reduce-scatter.14
  657.6 48.0 all-gather.16
  907.7 95.2 all-reduce.9
  1195.4 33.5 reduce-scatter.36
  1231.9 27.9 reduce-scatter.28
  1263.2 30.0 reduce-scatter.24
  1296.1 32.9 reduce-scatter.26
  1332.7 24.8 reduce-scatter.20
  1360.3 27.8 reduce-scatter.22
  1392.1 31.5 reduce-scatter.18
  1426.5 50.0 reduce-scatter.16
  1479.9 111.1 reduce-scatter.34
  1594.3 112.1 reduce-scatter.30
  1709.8 112.1 reduce-scatter.32
Sparse Core Ops, SparseCore 1:
  138.0 112.4 all-gather.10
  252.2 113.6 all-gather.12
  367.5 113.4 all-gather.14
  1287.7 151.7 all-reduce.11
where the time goes:
time: 1850 us; the launch traced here: 1840 us
  waiting for transfers between devices  960 us (52%)
  matrix products  255 us (14%)
  local copies, waits for them, and re-layouts  251 us (14%)
  other arithmetic  175 us (9%)
  blocking collectives  151 us (8%)
  between operations  20.5 us (1%)
    psum x2, blocking collectives, body(): lax.psum((jnp.sum(counted), jnp.sum(counted[:, None] * difference * diffe...  151 us
    reduce_scatter x1, waiting for transfers between devices, body(): lax.psum_scatter(expert_up_gradient.astype(jnp.bfloat16), 'dp', scatter_d...  111 us
    reduce_scatter x1, waiting for transfers between devices, body(): lax.psum_scatter(expert_gate_gradient.astype(jnp.bfloat16), 'dp', scatter...  110 us
    all_gather x1, waiting for transfers between devices, body(): lax.all_gather(expert_down_weight, 'dp', axis=2, tiled=True)  100 us
    psum x1, waiting for transfers between devices, body(): lax.psum(grad_branch.astype(jnp.bfloat16), 'expert').astype(jnp.float32)  95.4 us
    all_gather x1, waiting for transfers between devices, body(): lax.all_gather(expert_up_weight, 'dp', axis=1, tiled=True)  78 us
    reduce_scatter x1, waiting for transfers between devices, body(): lax.psum_scatter(expert_down_gradient.astype(jnp.bfloat16), 'dp', scatter...  69.4 us
    all_to_all x1, waiting for transfers between devices, body(): lax.all_to_all(grad_slot_in.reshape(local_experts, members, capacity, wid...  64.8 us
  transfers between devices with their start and end apart: 25, of which 18 were waited for; matrix products, arithmetic and copies ran while one was open for 20% of the time, Pallas kernels for 0%

commit v1 on v0

v1 whole, which is shorter than its diff:
```python
import functools

import jax
import jax.numpy as jnp
from jax import lax
from jax.experimental import pallas as pl
from jax.experimental.pallas import tpu as pltpu
from jax.sharding import PartitionSpec as P

NOPE = 128
ROPE = 64
VDIM = 128
LATENT = 512
SEQ = 4096
WINDOW = 1024
QUERY_BLOCK = 256

epsilon = 1e-06
masked_value = -1e30
score_scale = (NOPE + ROPE) ** (-0.5)
bf16 = jnp.bfloat16
f32 = jnp.float32


def dot_plain(left, right):
    return lax.dot_general(left, right, (((1,), (0,)), ((), ())), preferred_element_type=f32)


def dot_right_t(left, right):
    return lax.dot_general(left, right, (((1,), (1,)), ((), ())), preferred_element_type=f32)


def dot_left_t(left, right):
    return lax.dot_general(left, right, (((0,), (0,)), ((), ())), preferred_element_type=f32)


def normalize(values):
    factor = lax.rsqrt(jnp.mean(values * values, axis=-1, keepdims=True) + epsilon)
    return (values * factor, factor)


def norm_back(grad_out, unit, factor, gain):
    grad_unit = grad_out * gain
    return factor * (grad_unit - unit * jnp.mean(grad_unit * unit, axis=-1, keepdims=True))


def angles(place, half):
    freq = jnp.exp(-jnp.log(10000.0) * jnp.arange(half, dtype=f32) / half)
    angle = place.astype(f32)[:, None] * freq[None, :]
    return (jnp.cos(angle), jnp.sin(angle))


def rotate(values, cosine, sine):
    half = values.shape[-1] // 2
    first, second = (values[..., :half], values[..., half:])
    return jnp.concatenate(
        [first * cosine - second * sine, first * sine + second * cosine], axis=-1
    )


def unrotate(grads, cosine, sine):
    half = grads.shape[-1] // 2
    first, second = (grads[..., :half], grads[..., half:])
    return jnp.concatenate(
        [first * cosine + second * sine, second * cosine - first * sine], axis=-1
    )


def silu_parts(values):
    sigma = jax.nn.sigmoid(values)
    return (values * sigma, sigma * (1.0 + values * (1.0 - sigma)))


def head_lanes(block, head):
    lane = lax.broadcasted_iota(jnp.int32, (block, 2 * ROPE), 1)
    return (lane // (ROPE // 2)) % 2 == head


def allowed_keys(low, block, span):
    row = lax.broadcasted_iota(jnp.int32, (block, span), 0)
    col = lax.broadcasted_iota(jnp.int32, (block, span), 1)
    return (col <= row + WINDOW) & (col >= low)


def read_chunks(refs, first, last):
    return jnp.concatenate([ref[:, first:last] for ref in refs], axis=0)


def head_parts(query, lanes, kv, rope, head):
    turned = jnp.where(lanes, query[:, 2 * NOPE :], 0)
    query_head = jnp.concatenate([query[:, head * NOPE : (head + 1) * NOPE], turned], axis=1)
    base = head * (NOPE + VDIM)
    key_head = jnp.concatenate([read_chunks(kv, base, base + NOPE), rope], axis=1)
    return (query_head, key_head, read_chunks(kv, base + NOPE, base + NOPE + VDIM))


def attend_kernel(chunks, normed, cosine, sine, low, query_w, out_w, *refs):
    kv, key_rope = refs[:chunks], refs[chunks : 2 * chunks]
    query_out, mixed_out, log_out, part_out = refs[2 * chunks :]
    block = normed.shape[0]
    proj = dot_plain(normed[...], query_w[...])
    turned = proj[:, 2 * NOPE :]
    turned = turned * cosine[...] + pltpu.roll(turned, ROPE, 1) * sine[...]
    query = jnp.concatenate([proj[:, : 2 * NOPE], turned], axis=1).astype(bf16)
    query_out[...] = query
    mask = allowed_keys(low[...], block, WINDOW + block)
    rope = read_chunks(key_rope, 0, 2 * ROPE)
    mixed, logs = [], []
    for head in range(2):
        query_head, key_head, value_head = head_parts(query, head_lanes(block, head), kv, rope, head)
        scores = jnp.where(mask, dot_right_t(query_head, key_head) * score_scale, masked_value)
        top = jnp.max(scores, axis=1, keepdims=True)
        raised = jnp.exp(scores - top)
        total = jnp.sum(raised, axis=1, keepdims=True)
        probs = (raised * (1.0 / total)).astype(bf16)
        mixed.append(dot_plain(probs, value_head))
        logs.append(top + jnp.log(total))
    lane = lax.broadcasted_iota(jnp.int32, (block, 128), 1)
    log_out[...] = jnp.where(lane == 0, logs[0], logs[1])
    mixed = jnp.concatenate(mixed, axis=1).astype(bf16)
    mixed_out[...] = mixed
    part_out[...] = dot_plain(mixed, out_w[...]).astype(bf16)


def by_rows(block, cols, offset=0):
    return pl.BlockSpec((block, cols), lambda i: (i + offset, 0))


def whole(shape):
    return pl.BlockSpec(shape, lambda i: (0, 0))


def attend(normed, cosine, sine, low, query_w, kv, key_rope, out_w):
    rows, width = normed.shape
    block = QUERY_BLOCK
    chunks = 1 + WINDOW // block
    query_cols = query_w.shape[1]
    rows_of = functools.partial(by_rows, block)
    return pl.pallas_call(
        functools.partial(attend_kernel, chunks),
        grid=(rows // block,),
        in_specs=[
            rows_of(width),
            rows_of(2 * ROPE),
            rows_of(2 * ROPE),
            rows_of(1),
            whole(query_w.shape),
            whole(out_w.shape),
        ]
        + [rows_of(kv.shape[1], chunk) for chunk in range(chunks)]
        + [rows_of(key_rope.shape[1], chunk) for chunk in range(chunks)],
        out_specs=[rows_of(query_cols), rows_of(2 * VDIM), rows_of(128), rows_of(width)],
        out_shape=[
            jax.ShapeDtypeStruct((rows, query_cols), bf16),
            jax.ShapeDtypeStruct((rows, 2 * VDIM), bf16),
            jax.ShapeDtypeStruct((rows, 128), f32),
            jax.ShapeDtypeStruct((rows, width), bf16),
        ],
        compiler_params=pltpu.CompilerParams(vmem_limit_bytes=50 * 1024 * 1024),
        cost_estimate=pl.CostEstimate(
            flops=2 * rows * (width * (query_cols + 2 * VDIM) + 2 * (WINDOW + block) * 384),
            bytes_accessed=20 * 1024 * 1024,
            transcendentals=2 * rows * (WINDOW + block),
        ),
        name="attend",
    )(normed, cosine, sine, low, query_w, out_w, *([kv] * chunks), *([key_rope] * chunks))


def attend_back_kernel(
    chunks, grad, query_in, logs, cosine, sine, low, query_w, out_w, *refs
):
    kv, key_rope = refs[:chunks], refs[chunks : 2 * chunks]
    query_grad_out, part_out = refs[2 * chunks : 2 * chunks + 2]
    kv_past, rope_past, kv_own, rope_own, kv_sum, rope_sum = refs[2 * chunks + 2 :]
    block = grad.shape[0]

    @pl.when(pl.program_id(0) == 0)
    def clear():
        kv_sum[...] = jnp.zeros_like(kv_sum)
        rope_sum[...] = jnp.zeros_like(rope_sum)

    def add(total, past, cols, piece):
        for chunk in range(chunks):
            part = piece[chunk * block : (chunk + 1) * block]
            if chunk < chunks - 1:
                part = part + total[chunk * block : (chunk + 1) * block, cols]
            if chunk == 0:
                past[:, cols] = part.astype(past.dtype)
            else:
                total[(chunk - 1) * block : chunk * block, cols] = part

    mixed_grad = dot_right_t(grad[...], out_w[...]).astype(bf16)
    mask = allowed_keys(low[...], block, WINDOW + block)
    rope = read_chunks(key_rope, 0, 2 * ROPE)
    query = query_in[...]
    plain, turned, rope_piece = [], 0.0, 0.0
    for head in range(2):
        lanes = head_lanes(block, head)
        query_head, key_head, value_head = head_parts(query, lanes, kv, rope, head)
        base = head * (NOPE + VDIM)
        grad_head = mixed_grad[:, head * VDIM : (head + 1) * VDIM]
        scores = jnp.where(mask, dot_right_t(query_head, key_head) * score_scale, masked_value)
        probs = jnp.exp(scores - logs[:, head : head + 1])
        prob_grad = dot_right_t(grad_head, value_head)
        shift = jnp.sum(probs * prob_grad, axis=1, keepdims=True)
        score_grad = (probs * (prob_grad - shift)).astype(bf16)
        key_piece = dot_left_t(score_grad, query_head) * score_scale
        add(kv_sum, kv_past, slice(base, base + NOPE), key_piece[:, :NOPE])
        value_piece = dot_left_t(probs.astype(bf16), grad_head)
        add(kv_sum, kv_past, slice(base + NOPE, base + NOPE + VDIM), value_piece)
        rope_piece = rope_piece + key_piece[:, NOPE:]
        query_piece = dot_plain(score_grad, key_head) * score_scale
        plain.append(query_piece[:, :NOPE])
        turned = turned + jnp.where(lanes, query_piece[:, NOPE:], 0.0)
    add(rope_sum, rope_past, slice(0, 2 * ROPE), rope_piece)
    turned = turned * cosine[...] - pltpu.roll(turned, ROPE, 1) * sine[...]
    query_grad = jnp.concatenate(plain + [turned], axis=1).astype(bf16)
    query_grad_out[...] = query_grad
    part_out[...] = dot_right_t(query_grad, query_w[...]).astype(bf16)

    @pl.when(pl.program_id(0) == pl.num_programs(0) - 1)
    def finish():
        kv_own[...] = kv_sum[...].astype(bf16)
        rope_own[...] = rope_sum[...]


def attend_back(grad, query, logs, cosine, sine, low, query_w, kv, key_rope, out_w):
    rows, width = grad.shape
    block = QUERY_BLOCK
    chunks = 1 + WINDOW // block
    query_cols = query_w.shape[1]
    rows_of = functools.partial(by_rows, block)
    kv_cols, rope_cols = kv.shape[1], key_rope.shape[1]
    return pl.pallas_call(
        functools.partial(attend_back_kernel, chunks),
        grid=(rows // block,),
        in_specs=[
            rows_of(width),
            rows_of(query_cols),
            rows_of(128),
            rows_of(2 * ROPE),
            rows_of(2 * ROPE),
            rows_of(1),
            whole(query_w.shape),
            whole(out_w.shape),
        ]
        + [rows_of(kv_cols, chunk) for chunk in range(chunks)]
        + [rows_of(rope_cols, chunk) for chunk in range(chunks)],
        out_specs=[
            rows_of(query_cols),
            rows_of(width),
            rows_of(kv_cols),
            rows_of(rope_cols),
            whole((WINDOW, kv_cols)),
            whole((WINDOW, rope_cols)),
        ],
        out_shape=[
            jax.ShapeDtypeStruct((rows, query_cols), bf16),
            jax.ShapeDtypeStruct((rows, width), bf16),
            jax.ShapeDtypeStruct((rows, kv_cols), bf16),
            jax.ShapeDtypeStruct((rows, rope_cols), f32),
            jax.ShapeDtypeStruct((WINDOW, kv_cols), bf16),
            jax.ShapeDtypeStruct((WINDOW, rope_cols), f32),
        ],
        scratch_shapes=[pltpu.VMEM((WINDOW, kv_cols), f32), pltpu.VMEM((WINDOW, rope_cols), f32)],
        compiler_params=pltpu.CompilerParams(vmem_limit_bytes=50 * 1024 * 1024),
        cost_estimate=pl.CostEstimate(
            flops=2 * rows * (width * (query_cols + 2 * VDIM) + 2 * (WINDOW + block) * 1024),
            bytes_accessed=30 * 1024 * 1024,
            transcendentals=2 * rows * (WINDOW + block),
        ),
        name="attend_back",
    )(
        grad, query, logs, cosine, sine, low, query_w, out_w, *([kv] * chunks), *([key_rope] * chunks)
    )


def split_query_columns(weight):
    head = NOPE + ROPE
    half = ROPE // 2
    pieces = [weight[:, :NOPE], weight[:, head : head + NOPE]]
    for part in range(2):
        for index in range(2):
            first = index * head + NOPE + part * half
            pieces.append(weight[:, first : first + half])
    return jnp.concatenate(pieces, axis=1)


def join_query_columns(grad):
    half = ROPE // 2
    base = 2 * NOPE
    pieces = []
    for index in range(2):
        pieces.append(grad[:, index * NOPE : (index + 1) * NOPE])
        for part in range(2):
            first = base + part * ROPE + index * half
            pieces.append(grad[:, first : first + half])
    return jnp.concatenate(pieces, axis=1)


class Pairing:
    def __init__(self, groups, members):
        self.groups = groups
        self.members = members
        self.bits = groups.bit_length() - 1
        top = self.bits - 1
        self.partner = (1 << top, 1)
        self.others = (
            [1 << bit for bit in range(top)],
            [1 << (bit + 1) for bit in range(top)],
        )
        self.group = lax.axis_index("dp")
        self.odd = lax.axis_index("expert") % 2

    def chosen(self, masks):
        return jnp.where(self.odd == 1, masks[1], masks[0])

    def place(self, masks):
        return self.group ^ self.chosen(masks)

    def bit(self):
        return jnp.where(self.group & self.chosen(self.partner), 1, 0)

    def swap(self, value, masks):
        pairs = []
        for group in range(self.groups):
            for member in range(self.members):
                other = group ^ masks[member % 2]
                pairs.append((group * self.members + member, other * self.members + member))
        return lax.ppermute(value, ("dp", "expert"), pairs)

    def swap_partner(self, value):
        return self.swap(value, self.partner)

    def gather(self, kept, given):
        masks = [(0, 0), self.partner]
        held = jnp.stack([kept, self.swap_partner(given)])
        for step in zip(*self.others):
            held = jnp.concatenate([held, self.swap(held, step)])
            masks = masks + [(even ^ step[0], odd ^ step[1]) for even, odd in masks]
        out = jnp.zeros((self.groups,) + kept.shape, kept.dtype)
        for index, mask in enumerate(masks):
            out = lax.dynamic_update_slice_in_dim(
                out, held[index : index + 1], self.place(mask), 0
            )
        return out

    def scatter(self, grad):
        masks = [(0, 0), self.partner]
        for step in zip(*self.others):
            masks = masks + [(even ^ step[0], odd ^ step[1]) for even, odd in masks]
        held = [lax.dynamic_index_in_dim(grad, self.place(mask), 0, False) for mask in masks]
        for step in reversed(list(zip(*self.others))):
            half = len(held) // 2
            arrived = self.swap(jnp.stack(held[half:]), step)
            held = [
                (held[index].astype(f32) + arrived[index].astype(f32)).astype(bf16)
                for index in range(half)
            ]
        return (held[0], self.swap_partner(held[1]))

    def total(self, value):
        for bit in range(self.bits):
            value = value + self.swap(value, (1 << bit, 1 << bit))
        return value


def body(
    tokens,
    target,
    valid,
    routes,
    lengths,
    first_gain_vector,
    second_gain_vector,
    latent_gain_vector,
    latent_compress_weight,
    query_weight,
    latent_expand_weight,
    output_weight,
    router_weight,
    shared_gate_weight,
    shared_up_weight,
    shared_down_weight,
    expert_gate_weight,
    expert_up_weight,
    expert_down_weight,
):
    rows, width = tokens.shape
    members = lax.axis_size("expert")
    groups = lax.axis_size("dp")
    member = lax.axis_index("expert")
    group = lax.axis_index("dp")
    group_size = rows * members
    local_experts = expert_gate_weight.shape[0]
    route_count = routes.shape[1]
    expert_count = router_weight.shape[1]
    hidden_width = expert_gate_weight.shape[2]
    capacity = rows * route_count * 4 // (3 * local_experts * members)
    pairing = Pairing(groups, members)
    bit = pairing.bit()

    def pick(weight, index):
        return lax.dynamic_index_in_dim(weight, index, 0, False)

    down_t = jnp.swapaxes(expert_down_weight, 1, 2)
    gate_w, up_w, down_w = [
        pairing.gather(pick(weight, bit), pick(weight, 1 - bit)).reshape(width, hidden_width)
        for weight in (expert_gate_weight, expert_up_weight, down_t)
    ]

    counted = valid.astype(f32)
    count = lax.psum(jnp.sum(counted), ("dp", "expert"))

    tokens_float = tokens.astype(f32)
    own_unit, own_factor = normalize(tokens_float)
    own_normed = (own_unit * first_gain_vector).astype(bf16)
    projected = dot_plain(own_normed, latent_compress_weight)
    own_first = (group * members + member) * rows
    own_place = (own_first + jnp.arange(rows, dtype=jnp.int32)) % SEQ
    own_cos, own_sin = angles(own_place, ROPE // 2)
    latent_unit, latent_factor = normalize(projected[:, :LATENT])
    latent = jnp.concatenate(
        [latent_unit * latent_gain_vector, rotate(projected[:, LATENT:], own_cos, own_sin)], axis=1
    ).astype(bf16)
    group_latent = lax.all_gather(latent, "expert", axis=0, tiled=True)
    normed = lax.all_gather(own_normed, "expert", axis=0, tiled=True)
    previous = lax.ppermute(group_latent, "dp", [(i, i + 1) for i in range(groups - 1)])
    key_latent = jnp.concatenate([previous, group_latent], axis=0)

    index = group * group_size + jnp.arange(group_size, dtype=jnp.int32)
    seq_id = jnp.floor_divide(index, SEQ)
    place = index - seq_id * SEQ
    bounds = lax.dynamic_slice_in_dim(
        jnp.cumsum(lengths, axis=1), group * group_size // SEQ, 1, 0
    )
    doc_start = jnp.max(jnp.where(bounds <= place[:, None], bounds, 0), axis=1)
    in_block = jnp.arange(group_size, dtype=jnp.int32) % QUERY_BLOCK
    low = jnp.maximum(doc_start - place + WINDOW + in_block, in_block + 1)[:, None]
    cosine, sine = angles(place, ROPE // 2)
    cosine = jnp.concatenate([cosine] * 4, axis=1)
    sine = jnp.concatenate([-sine, -sine, sine, sine], axis=1)

    hot = jnp.any(routes[:, :, None] == jnp.arange(expert_count, dtype=jnp.int32), axis=1)
    routes_t = routes.T.reshape(route_count, members, rows)
    order = jnp.arange(rows, dtype=jnp.int32)
    earlier = (order[:, None] < order[None, :]).astype(bf16)
    mine = member * local_experts + bit
    other = member * local_experts + 1 - bit

    def slots_of(expert):
        hit = jnp.any(routes_t == expert, axis=0)
        rank = dot_plain(hit.astype(bf16), earlier).astype(jnp.int32)
        slot = jnp.arange(capacity, dtype=jnp.int32)[None, :, None]
        return (hit[:, None, :] & (rank[:, None, :] == slot)).astype(bf16)

    slots_mine, slots_other = slots_of(mine), slots_of(other)

    def to_slots(slots, values):
        return jnp.einsum(
            "bst,btd->bsd", slots, values.reshape(members, rows, -1), preferred_element_type=f32
        )

    def from_slots(slots, values):
        return jnp.einsum(
            "bst,bsd->btd", slots, values, preferred_element_type=f32
        ).reshape(group_size, -1)

    query_w = split_query_columns(query_weight)
    kv = dot_plain(key_latent[:, :LATENT], latent_expand_weight).astype(bf16)
    half = LATENT + ROPE // 2
    key_rope = jnp.concatenate(
        [key_latent[:, LATENT:half]] * 2 + [key_latent[:, half:]] * 2, axis=1
    )
    query, mixed, logs, attention_part = attend(
        normed, cosine, sine, low, query_w, kv, key_rope, output_weight
    )
    attention = lax.psum_scatter(attention_part, "expert", scatter_dimension=0, tiled=True)
    hidden = tokens_float + attention.astype(f32)
    hidden_unit, hidden_factor = normalize(hidden)
    own_branch = (hidden_unit * second_gain_vector).astype(bf16)
    branch = lax.all_gather(own_branch, "expert", axis=0, tiled=True)

    logits = jnp.where(hot, dot_plain(branch, router_weight), masked_value)
    top = jnp.max(logits, axis=1, keepdims=True)
    raised = jnp.where(hot, jnp.exp(logits - top), 0.0)
    gates = raised / jnp.sum(raised, axis=1, keepdims=True)
    experts = jnp.arange(expert_count, dtype=jnp.int32)[None, :]
    gate_mine = jnp.sum(jnp.where(experts == mine, gates, 0.0), axis=1, keepdims=True)
    gate_other = jnp.sum(jnp.where(experts == other, gates, 0.0), axis=1, keepdims=True)

    in_other = to_slots(slots_other, branch).astype(bf16)
    in_arrived = pairing.swap_partner(in_other)
    in_mine = to_slots(slots_mine, branch).astype(bf16)

    def expert_forward(slot_in):
        flat = slot_in.reshape(-1, width)
        gate = dot_plain(flat, gate_w)
        up = dot_plain(flat, up_w)
        act, slope = silu_parts(gate)
        inner = (act * up).astype(bf16)
        out = dot_right_t(inner, down_w).astype(bf16).reshape(slot_in.shape)
        return (flat, act.astype(bf16), (up * slope).astype(bf16), inner, out)

    flat_m, act_m, slope_m, inner_m, out_mine = expert_forward(in_mine)
    shared_gate = dot_plain(branch, shared_gate_weight)
    shared_up = dot_plain(branch, shared_up_weight)
    shared_act, shared_slope = silu_parts(shared_gate)
    shared_hidden = (shared_act * shared_up).astype(bf16)
    flat_a, act_a, slope_a, inner_a, out_arrived = expert_forward(in_arrived)
    out_other = pairing.swap_partner(out_arrived)
    branch_part = (
        dot_plain(shared_hidden, shared_down_weight)
        + gate_mine * from_slots(slots_mine, out_mine)
        + gate_other * from_slots(slots_other, out_other)
    ).astype(bf16)
    branch_sum = lax.psum_scatter(branch_part, "expert", scatter_dimension=0, tiled=True)
    result = hidden + branch_sum.astype(f32)
    difference = result - target.astype(f32)
    squares = jnp.sum(counted[:, None] * difference * difference)
    total_tokens = rows * members * groups
    grad_out = total_tokens / count * counted[:, None] * difference

    grad_low = lax.all_gather(grad_out.astype(bf16), "expert", axis=0, tiled=True)

    def slot_gates(slots, gate):
        return jnp.sum(slots.astype(f32) * gate.reshape(members, 1, rows), axis=2)

    def out_grads(slots, gate, out):
        grads = to_slots(slots, grad_low)
        gate_grad = jnp.sum(grads * out.astype(f32), axis=2)
        gate_grad = jnp.sum(slots.astype(f32) * gate_grad[:, :, None], axis=1).reshape(group_size, 1)
        return ((slot_gates(slots, gate)[:, :, None] * grads).astype(bf16), gate_grad)

    out_grad_other, gate_grad_other = out_grads(slots_other, gate_other, out_other)
    out_grad_arrived = pairing.swap_partner(out_grad_other)
    out_grad_mine, gate_grad_mine = out_grads(slots_mine, gate_mine, out_mine)

    def expert_backward(out_grad, act, slope):
        flat = out_grad.reshape(-1, width)
        inner_grad = dot_plain(flat, down_w)
        gate_grad = (inner_grad * slope.astype(f32)).astype(bf16)
        up_grad = (inner_grad * act.astype(f32)).astype(bf16)
        in_grad = (dot_right_t(gate_grad, gate_w) + dot_right_t(up_grad, up_w)).astype(bf16)
        return (flat, gate_grad, up_grad, in_grad.reshape(out_grad.shape))

    flat_gm, gate_gm, up_gm, in_grad_mine = expert_backward(out_grad_mine, act_m, slope_m)
    grad_hidden = dot_right_t(grad_low, shared_down_weight)
    grad_shared_gate = (grad_hidden * shared_up * shared_slope).astype(bf16)
    grad_shared_up = (grad_hidden * shared_act).astype(bf16)
    flat_ga, gate_ga, up_ga, in_grad_arrived = expert_backward(out_grad_arrived, act_a, slope_a)
    in_grad_other = pairing.swap_partner(in_grad_arrived)

    gate_grads = jnp.where(experts == mine, gate_grad_mine, 0.0) + jnp.where(
        experts == other, gate_grad_other, 0.0
    )
    logit_grad = gates * (gate_grads - jnp.sum(gates * gate_grads, axis=1, keepdims=True))
    grad_router = dot_left_t(branch, logit_grad.astype(bf16))
    branch_grad_part = (
        dot_right_t(grad_shared_gate, shared_gate_weight)
        + dot_right_t(grad_shared_up, shared_up_weight)
        + dot_right_t(logit_grad.astype(bf16), router_weight)
        + from_slots(slots_mine, in_grad_mine)
        + from_slots(slots_other, in_grad_other)
    ).astype(bf16)
    branch_grad = lax.psum_scatter(
        branch_grad_part, "expert", scatter_dimension=0, tiled=True
    ).astype(f32)

    def weight_grad(left_m, left_a, right_m, right_a):
        left = jnp.concatenate([left_m, left_a])
        right = jnp.concatenate([right_m, right_a])
        grad = dot_left_t(left, right).astype(bf16).reshape(groups, -1, hidden_width)
        own, others = pairing.scatter(grad)
        own, others = own.astype(f32), others.astype(f32)
        return jnp.where(bit == 0, jnp.stack([own, others]), jnp.stack([others, own]))

    expert_down_gradient = jnp.swapaxes(weight_grad(flat_gm, flat_ga, inner_m, inner_a), 1, 2)
    expert_gate_gradient = weight_grad(flat_m, flat_a, gate_gm, gate_ga)
    expert_up_gradient = weight_grad(flat_m, flat_a, up_gm, up_ga)

    def sum_groups(grad):
        return lax.psum_scatter(grad, "dp", scatter_dimension=0, tiled=True).astype(f32)

    shared_cols = shared_gate.shape[1]
    shared_grads = sum_groups(
        jnp.concatenate(
            [
                dot_left_t(branch, grad_shared_gate).astype(bf16),
                dot_left_t(branch, grad_shared_up).astype(bf16),
                dot_left_t(grad_low, shared_hidden).astype(bf16),
            ],
            axis=1,
        )
    )
    shared_gate_gradient = shared_grads[:, :shared_cols]
    shared_up_gradient = shared_grads[:, shared_cols : 2 * shared_cols]
    shared_down_gradient = shared_grads[:, 2 * shared_cols :].T

    grad_norm2 = jnp.sum(branch_grad * hidden_unit, axis=0)
    grad_hidden_own = grad_out + norm_back(
        branch_grad, hidden_unit, hidden_factor, second_gain_vector
    )
    grad_attention = lax.all_gather(grad_hidden_own.astype(bf16), "expert", axis=0, tiled=True)
    query_grad, normed_grad_part, kv_past, rope_past, kv_own, rope_own = attend_back(
        grad_attention, query, logs, cosine, sine, low, query_w, kv, key_rope, output_weight
    )

    def latent_back(kv_grad, rope_grad):
        half = ROPE // 2
        first = rope_grad[:, :half] + rope_grad[:, half:ROPE]
        second = rope_grad[:, ROPE : ROPE + half] + rope_grad[:, ROPE + half :]
        return jnp.concatenate(
            [dot_right_t(kv_grad, latent_expand_weight), first, second], axis=1
        )

    back = lax.ppermute(
        latent_back(kv_past, rope_past).astype(bf16),
        "dp",
        [(i + 1, i) for i in range(groups - 1)],
    )
    latent_grad = lax.psum_scatter(
        (latent_back(kv_own, rope_own) + back.astype(f32)).astype(bf16),
        "expert",
        scatter_dimension=0,
        tiled=True,
    ).astype(f32)
    normed_grad = lax.psum_scatter(
        normed_grad_part, "expert", scatter_dimension=0, tiled=True
    ).astype(f32)

    expand_grad = (
        dot_left_t(previous[:, :LATENT], kv_past) + dot_left_t(group_latent[:, :LATENT], kv_own)
    ).astype(bf16)
    expand_shape = expand_grad.shape
    query_cols = query_w.shape[1]
    attention_grads = sum_groups(
        jnp.concatenate(
            [
                dot_left_t(normed, query_grad).astype(bf16),
                dot_left_t(grad_attention, mixed).astype(bf16),
                expand_grad.reshape(width, -1),
            ],
            axis=1,
        )
    )
    query_weight_gradient = join_query_columns(attention_grads[:, :query_cols])
    output_weight_gradient = attention_grads[:, query_cols : query_cols + 2 * VDIM].T
    latent_expand_gradient = attention_grads[:, query_cols + 2 * VDIM :].reshape(
        expand_shape[0] // groups, expand_shape[1]
    )

    grad_latent_gain = jnp.sum(latent_grad[:, :LATENT] * latent_unit, axis=0)
    grad_projected = jnp.concatenate(
        [
            norm_back(latent_grad[:, :LATENT], latent_unit, latent_factor, latent_gain_vector),
            unrotate(latent_grad[:, LATENT:], own_cos, own_sin),
        ],
        axis=1,
    ).astype(bf16)
    group_projected = lax.all_gather(grad_projected, "expert", axis=0, tiled=True)
    slice_cols = width // members
    normed_slice = lax.dynamic_slice_in_dim(normed, member * slice_cols, slice_cols, 1)
    compress_slice = pairing.total(dot_left_t(normed_slice, group_projected))
    grad_kva = lax.all_gather(
        compress_slice.astype(bf16), "expert", axis=0, tiled=True
    ).astype(f32)
    normed_grad = normed_grad + dot_right_t(grad_projected, latent_compress_weight)
    grad_norm1 = jnp.sum(normed_grad * own_unit, axis=0)
    grad_tokens = grad_hidden_own + norm_back(
        normed_grad, own_unit, own_factor, first_gain_vector
    )
    squares, grad_norm1, grad_norm2, grad_latent_gain, grad_router = lax.psum(
        (squares, grad_norm1, grad_norm2, grad_latent_gain, grad_router), ("dp", "expert")
    )
    return (
        result.astype(bf16),
        squares / (count * width),
        grad_tokens,
        grad_norm1,
        grad_norm2,
        grad_latent_gain,
        grad_kva,
        query_weight_gradient,
        latent_expand_gradient,
        output_weight_gradient,
        grad_router,
        shared_gate_gradient,
        shared_up_gradient,
        shared_down_gradient,
        expert_gate_gradient,
        expert_up_gradient,
        expert_down_gradient,
    )


def solution(mesh):
    placed = (
        P(("dp", "expert"), None),
        P(("dp", "expert"), None),
        P(("dp", "expert")),
        P("dp", None),
        P(),
        P(),
        P(),
        P(),
        P(),
        P(None, "expert"),
        P(None, "expert"),
        P("expert", None),
        P(),
        P(None, "expert"),
        P(None, "expert"),
        P("expert", None),
        P("expert", "dp", None),
        P("expert", "dp", None),
        P("expert", None, "dp"),
    )
    return jax.shard_map(
        body,
        mesh=mesh,
        in_specs=placed,
        out_specs=(
            P(("dp", "expert"), None),
            P(),
            P(("dp", "expert"), None),
            P(),
            P(),
            P(),
            P(),
            P("dp", "expert"),
            P("dp", "expert"),
            P("expert", "dp"),
            P(),
            P("dp", "expert"),
            P("dp", "expert"),
            P("expert", "dp"),
            P("expert", "dp", None),
            P("expert", "dp", None),
            P("expert", None, "dp"),
        ),
        check_vma=False,
    )
```

time: 1850 us -> 1160 us (0.63)
  waiting for transfers between devices: 960 us -> 501 us
  local copies, waits for them, and re-layouts: 251 us -> 149 us
  other arithmetic: 175 us -> 104 us
  matrix products: 255 us -> 196 us
  blocking collectives: 151 us -> 108 us
  Pallas kernels: 0 us -> 37.4 us
    reduce_scatter x11 -> x7, waiting for transfers between devices: 458 us -> 124 us  [the longest x1 48.3 us: body(): lax.psum_scatter(branch_grad_part, 'expert', scatter_dimension=0, tiled=T...]
    ppermute x2 -> x20, waiting for transfers between devices: 46.3 us -> 226 us  [the longest x18 188 us: swap(): return lax.ppermute(value, ('dp', 'expert'), pairs)]
    dot_general x25 -> x8, matrix products: 169 us -> 21.1 us  [the longest x4 11.9 us: from_slots(): jnp.einsum('bst,bsd->btd', slots, values, preferred_element_type=f32)]
    all_gather x6 -> x7, waiting for transfers between devices: 255 us -> 121 us  [the longest x1 45.4 us: body(): lax.all_gather(grad_hidden_own.astype(bf16), 'expert', axis=0, tiled=True)]
    psum x3 -> x1, waiting for transfers between devices: 133 us -> 29 us  [body(): lax.psum((squares, grad_norm1, grad_norm2, grad_latent_gain, grad_router)...]
    all_to_all x2 -> x0, waiting for transfers between devices: 64.8 us -> none  [the longest x1 64.8 us: body(): lax.all_to_all(grad_slot_in.reshape(local_experts, members, capacity, wid...]
    gather x6 -> x0, local copies, waits for them, and re-layouts: 61.5 us -> none  [the longest x1 15.6 us: body(): came_back[own_routes % local_experts, own_routes // local_experts, own_ra...]
    dot_general x7 -> x13, matrix products: 22.4 us -> 68 us  [dot_right_t(): lax.dot_general(left, right, (((1,), (1,)), ((), ())), preferred_element_...]
  transfers between devices with their start and end apart: 25 -> 35, of which waited for: 18 -> 24; matrix products, arithmetic and copies ran while one was open for 20% -> 29% of each run, Pallas kernels for 0% -> 0%
where the time goes in v1:
time: 1160 us; the launch traced here: 1150 us
  waiting for transfers between devices  501 us (43%)
  matrix products  196 us (17%)
  local copies, waits for them, and re-layouts  149 us (13%)
  blocking collectives  108 us (9%)
  other arithmetic  104 us (9%)
  Pallas kernels  37.4 us (3%)
  starting transfers between devices  31.3 us (3%)
  between operations  19.3 us (2%)
    ppermute x18, waiting for transfers between devices, swap(): return lax.ppermute(value, ('dp', 'expert'), pairs)  188 us
    unnamed x299, local copies, waits for them, and re-layouts  71.7 us
    dot_general x13, matrix products, dot_right_t(): lax.dot_general(left, right, (((1,), (1,)), ((), ())), preferred_element_...  68 us
    psum x1, blocking collectives, body(): lax.psum((squares, grad_norm1, grad_norm2, grad_latent_gain, grad_router)...  65.8 us
    dot_general x14, matrix products, dot_plain(): lax.dot_general(left, right, (((1,), (0,)), ((), ())), preferred_element_...  56.7 us
    dot_general x12, matrix products, dot_left_t(): lax.dot_general(left, right, (((0,), (0,)), ((), ())), preferred_element_...  49.9 us
    reduce_scatter x1, waiting for transfers between devices, body(): lax.psum_scatter(branch_grad_part, 'expert', scatter_dimension=0, tiled=T...  48.3 us
    all_gather x1, waiting for transfers between devices, body(): lax.all_gather(grad_hidden_own.astype(bf16), 'expert', axis=0, tiled=True)  45.4 us
  transfers between devices with their start and end apart: 35, of which 24 were waited for; matrix products, arithmetic and copies ran while one was open for 29% of the time, Pallas kernels for 0%

profile of v1, /device:TPU:0, one launch (start us, length us, event | category | flops | bytes accessed | tf_op | source)
XLA Modules:
  0.0 1146.1 jit_solution(2671495619261246)
XLA Ops:
  17.9 20.8 %all-gather.10.cloned.1.call-done = bf16[1024,576]{1,0:T(8,128)(2,1)} async-done(((bf16[128,576]{1,0:T(8,128)(2,1)}), bf16[1024,576]{1,0:T(8,128)(2,1)}) %all-gather.10.cloned.1.call-update) | async-done | bytes 1179664 | tf_op jit(solution)/shard_map/all_gather | solution.py:426
  47.2 5.4 concatenate.57.query_w
  57.5 12.9 %collective-permute-done = bf16[1024,576]{0,1:T(8,128)(2,1)} collective-permute-done((bf16[1024,576]{0,1:T(8,128)(2,1)}, bf16[1024,576]{0,1:T(8,128)(2,1)}, u32[]{:S(2)}, u32[]{:S(2)}) %collective-permute-start) | collective-permute-done | bytes 1179680 | tf_op jit(solution)/shard_map/ppermute | solution.py:428
  78.5 9.1 all-gather.8.cloned.1.call-done.normed
  89.6 15.6 %attend.1 = (bf16[1024,384]{1,0:T(8,128)(2,1)S(1)}, bf16[1024,256]{1,0:T(8,128)(2,1)S(1)}, f32[1024,128]{1,0:T(8,128)S(1)}, bf16[1024,2048]{1,0:T(8,128)(2,1)}) custom-call(bf16[1024,2048]{1,0:T(8,128)(2,1)} %all-gather.8.cloned.1.call-done.normed, f32[1024,128]{1,0:T(8,128)S(1)} %copy-done.3, f32[1024,128]{1,0:T(8,128)S(1)} %pad_maximum_fusion.13.sine, ...), custom_call_target="tpu_custom_call" | custom-call | flops 4697620480 | bytes 20971520 | tf_op jit(solution)/shard_map/attend/pallas_call | solution.py:139
  119.3 37.3 %reduce-scatter.8.cloned.1.call-done = bf16[128,2048]{1,0:T(8,128)(2,1)} async-done(((bf16[1024,2048]{1,0:T(8,128)(2,1)}), bf16[128,2048]{1,0:T(8,128)(2,1)}) %reduce-scatter.8.cloned.1.call-update) | async-done | bytes 524304 | tf_op jit(solution)/shard_map/reduce_scatter | solution.py:478
  183.6 12.3 %collective-permute-done.1 = bf16[512,1408]{1,0:T(8,128)(2,1)} collective-permute-done((bf16[512,1408]{1,0:T(8,128)(2,1)}, bf16[512,1408]{1,0:T(8,128)(2,1)}, u32[]{:S(2)}, u32[]{:S(2)}) %collective-permute-start.1) | collective-permute-done | bytes 1441824 | tf_op jit(solution)/shard_map/ppermute | solution.py:330
  212.7 30.9 %collective-permute-done.6 = bf16[2,512,1408]{2,1,0:T(8,128)(2,1)} collective-permute-done((bf16[2,512,1408]{2,1,0:T(8,128)(2,1)}, bf16[2,512,1408]{2,1,0:T(8,128)(2,1)}, u32[]{:S(2)}, u32[]{:S(2)}) %collective-permute-start.6) | collective-permute-done | bytes 2883616 | tf_op jit(solution)/shard_map/ppermute | solution.py:330
  249.8 24.7 %collective-permute-done.2 = bf16[2,512,1408]{2,1,0:T(8,128)(2,1)} collective-permute-done((bf16[2,512,1408]{2,1,0:T(8,128)(2,1)}, bf16[2,512,1408]{2,1,0:T(8,128)(2,1)}, u32[]{:S(2)}, u32[]{:S(2)}) %collective-permute-start.2) | collective-permute-done | bytes 2883616 | tf_op jit(solution)/shard_map/ppermute | solution.py:330
  287.6 6.9 fusion.156
  294.5 5.1 multiply_convert_fusion.9
  299.6 6.9 convolution_convert_fusion.7
  311.4 6.7 fusion.157
  318.1 5.2 multiply_convert_fusion.8
  323.3 6.9 convolution_convert_fusion.6
  339.4 17.0 %collective-permute-done.8 = bf16[8,64,2048]{2,1,0:T(8,128)(2,1)S(1)} collective-permute-done((bf16[8,64,2048]{2,1,0:T(8,128)(2,1)S(1)}, bf16[8,64,2048]{2,1,0:T(8,128)(2,1)S(1)}, u32[]{:S(2)}, u32[]{:S(2)}) %collective-permute-start.8) | collective-permute-done | bytes 2097184 | tf_op jit(solution)/shard_map/ppermute | solution.py:330
  357.7 5.9 fusion.2
  364.9 42.5 %psum.43 = f32[]{:T(128)} all-reduce(f32[]{:T(128)} %convert_reduce_fusion), channel_id=1, replica_groups=mesh['dp'=4,'expert'=8] {'dp','expert'}, use_global_device_ids=true, to_apply=%region_17.18 | all-reduce | flops 1 | bytes 8 | tf_op jit(solution)/shard_map/psum | solution.py:413
  409.3 6.0 reduce-scatter.10.cloned.1.call-done
  418.0 45.4 %all-gather.14.cloned.1.call-done = bf16[1024,2048]{1,0:T(8,128)(2,1)} async-done(((bf16[128,2048]{1,0:T(8,128)(2,1)}), bf16[1024,2048]{1,0:T(8,128)(2,1)}) %all-gather.14.cloned.1.call-update) | async-done | bytes 4194320 | tf_op jit(solution)/shard_map/all_gather | solution.py:524
  472.1 8.9 multiply_convert_fusion.6
  484.6 6.4 add_convert_fusion.1
  496.0 8.4 multiply_convert_fusion.3
  507.9 6.6 add_convert_fusion
  523.0 5.7 fusion.158
  528.7 5.6 fusion.159
  534.3 6.3 collective-permute-done.10
  545.3 13.8 %fusion = bf16[1024,2048]{1,0:T(8,128)(2,1)} fusion(f32[8,128,2048]{2,1,0:T(8,128)} %fusion.88, f32[8,128,2048]{2,1,0:T(8,128)} %fusion.79, f32[1024,2048]{1,0:T(8,128)} %fusion.158, f32[1024,2048]{1,0:T(8,128)} %fusion.159, bf16[2048,16]{0,1:T(8,128)(2,1)S(1)} %copy-done.67, f32[1024,16]{0,1:T(8,128)S(1)} %get-tuple-element.143, ...), kind=kOutput, calls=%fused_computation.1 | convolution fusion | flops 77692928 | bytes 37892128 | tf_op jit(solution)/shard_map/dot_general | solution.py:30
  559.8 48.3 %reduce-scatter.12.cloned.1.call-done = bf16[128,2048]{1,0:T(8,128)(2,1)} async-done(((bf16[1024,2048]{1,0:T(8,128)(2,1)}), bf16[128,2048]{1,0:T(8,128)(2,1)}) %reduce-scatter.12.cloned.1.call-update) | async-done | bytes 524304 | tf_op jit(solution)/shard_map/reduce_scatter | solution.py:566
  613.1 45.4 %all-gather.16.cloned.1.call-done.grad = bf16[1024,2048]{1,0:T(8,128)(2,1)} async-done(((bf16[128,2048]{1,0:T(8,128)(2,1)}), bf16[1024,2048]{1,0:T(8,128)(2,1)}) %all-gather.16.cloned.1.call-update) | async-done | bytes 4194320 | tf_op jit(solution)/shard_map/all_gather | solution.py:604
  662.6 21.8 %attend_back.1 = (bf16[1024,384]{1,0:T(8,128)(2,1)}, bf16[1024,2048]{1,0:T(8,128)(2,1)}, bf16[1024,512]{1,0:T(8,128)(2,1)}, f32[1024,128]{1,0:T(8,128)S(1)}, bf1...) custom-call(bf16[1024,2048]{1,0:T(8,128)(2,1)} %all-gather.16.cloned.1.call-done.grad, bf16[1024,384]{1,0:T(8,128)(2,1)} %copy-done.7, ...), custom_call_target="tpu_custom_call" | custom-call | flops 8053063680 | bytes 31457280 | tf_op jit(solution)/shard_map/attend_back/pallas_call | solution.py:234
  694.4 25.3 %collective-permute-done.11 = bf16[1024,576]{0,1:T(8,128)(2,1)} collective-permute-done((bf16[1024,576]{0,1:T(8,128)(2,1)S(1)}, bf16[1024,576]{0,1:T(8,128)(2,1)}, u32[]{:S(2)}, u32[]{:S(2)}) %collective-permute-start.11) | collective-permute-done | bytes 1179680 | tf_op jit(solution)/shard_map/ppermute | solution.py:617
  725.9 32.1 %reduce-scatter.16.cloned.1.call-done = bf16[128,576]{1,0:T(8,128)(2,1)} async-done(((bf16[1024,576]{1,0:T(8,128)(2,1)}), bf16[128,576]{1,0:T(8,128)(2,1)}) %reduce-scatter.16.cloned.1.call-update) | async-done | bytes 147472 | tf_op jit(solution)/shard_map/reduce_scatter | solution.py:622
  787.3 11.1 convolution_convert_fusion.1
  798.4 8.7 convolution_convert_fusion.2
  810.7 5.3 constant_dynamic-slice_fusion.7
  833.1 5.9 constant_dynamic-slice_fusion.11
  848.3 11.4 collective-permute-done.13
  861.8 9.4 convolution_convert_fusion
  888.6 5.8 fusion.28
  908.4 20.0 %collective-permute-done.14 = bf16[2,512,1408]{1,2,0:T(8,128)(2,1)} collective-permute-done((bf16[2,512,1408]{1,2,0:T(8,128)(2,1)}, bf16[2,512,1408]{1,2,0:T(8,128)(2,1)}, u32[]{:S(2)}, u32[]{:S(2)}) %collective-permute-start.14) | collective-permute-done | bytes 2883616 | tf_op jit(solution)/shard_map/ppermute | solution.py:330
  928.3 5.5 fusion.26
  935.3 42.0 %collective-permute-done.18 = bf16[2,512,1408]{1,2,0:T(8,128)(2,1)} collective-permute-done((bf16[2,512,1408]{1,2,0:T(8,128)(2,1)}, bf16[2,512,1408]{1,2,0:T(8,128)(2,1)}, u32[]{:S(2)}, u32[]{:S(2)}) %collective-permute-start.18) | collective-permute-done | bytes 2883616 | tf_op jit(solution)/shard_map/ppermute | solution.py:330
  988.8 6.3 copy.180
  1000.3 6.3 copy.179
  1006.5 5.8 collective-permute-done.19
  1036.5 65.8 %all-reduce = (f32[]{:T(128)}, f32[2048]{0:T(1024)}, f32[2048]{0:T(1024)}, f32[512]{0:T(512)}) all-reduce(f32[]{:T(128)} %get-tuple-element.126, f32[2048]{0:T(1024)S(1)} %get-tuple-element.124, f32[2048]{0:T(1024)S(1)} %get-tuple-element.122, f32[512]{0:T(512)S(1)} %get-tuple-element.127), channel_id=1, replica_groups=mesh['dp'=4,'expert'=8] {'dp','expert'}, use_global_device_ids=true, to_apply=%region_15.16 | all-reduce | flops 4609 | bytes 36872 | tf_op jit(solution)/shard_map/psum | solution.py:673
  1107.4 29.0 %all-reduce.3.cloned.1.call-done = f32[2048,16]{0,1:T(8,128)} async-done(((f32[2048,16]{0,1:T(8,128)}), f32[2048,16]{0,1:T(8,128)}) %all-reduce.3.cloned.1.call-update) | async-done | bytes 131088 | tf_op jit(solution)/shard_map/psum | solution.py:673
  (499 shorter events, 330.6 us)
Async XLA Ops:
  7.2 31.5 %all-gather.10.cloned.1.call-start = ((), (), s32[]{:S(2)}) async-start(), calls=%async_computation.8 | async-start | bytes 1474560 | tf_op jit(solution)/shard_map/all_gather | solution.py:426
  12.4 75.1 %all-gather.8.cloned.1.call-start = ((), (), s32[]{:S(2)}) async-start(), calls=%async_computation.7 | async-start | bytes 4718592 | tf_op jit(solution)/shard_map/all_gather | solution.py:427
  13.2 143.4 %reduce-scatter.8.cloned.1.call-start = ((), (), s32[]{:S(2)}) async-start(), calls=%async_computation.9 | async-start | bytes 4718592 | tf_op jit(solution)/shard_map/reduce_scatter | solution.py:478
  41.1 29.3 %collective-permute-start = (bf16[1024,576]{0,1:T(8,128)(2,1)}, bf16[1024,576]{0,1:T(8,128)(2,1)}, u32[]{:S(2)}, u32[]{:S(2)}) collective-permute-start(bf16[1024,576]{0,1:T(8,128)(2,1)} %copy.156), channel_id=1, source_target_pairs={{0,8},{8,16},{16,24},{1,9},{9,17},{17,25},{2,10},{10,18},{18,26},{... | collective-permute-start | bytes 3538952 | tf_op jit(solution)/shard_map/ppermute | solution.py:428
  107.8 174.5 %all-gather.12.cloned.1.call-start = ((), (), s32[]{:S(2)}) async-start(), calls=%async_computation.10 | async-start | bytes 4718592 | tf_op jit(solution)/shard_map/all_gather | solution.py:482
  111.9 58.3 %collective-permute-start.3 = (bf16[512,1408]{1,0:T(8,128)(2,1)}, bf16[512,1408]{1,0:T(8,128)(2,1)}, u32[]{:S(2)}, u32[]{:S(2)}) collective-permute-start(bf16[512,1408]{1,0:T(8,128)(2,1)} %get-tuple-element.175), channel_id=1, source_target_pairs={{0,16},{1,9},{2,18},{3,11},{4,20},{5,13},{6,22},{7,15},{8,24},{9,1... | collective-permute-start | bytes 4325384 | tf_op jit(solution)/shard_map/ppermute | solution.py:330
  117.9 57.6 %collective-permute-start.5 = (bf16[512,1408]{1,0:T(8,128)(2,1)}, bf16[512,1408]{1,0:T(8,128)(2,1)}, u32[]{:S(2)}, u32[]{:S(2)}) collective-permute-start(bf16[512,1408]{1,0:T(8,128)(2,1)} %bitcast.180), channel_id=1, source_target_pairs={{0,16},{1,9},{2,18},{3,11},{4,20},{5,13},{6,22},{7,15},{8,24},{9,1... | collective-permute-start | bytes 4325384 | tf_op jit(solution)/shard_map/ppermute | solution.py:330
  160.5 254.8 %reduce-scatter.10.cloned.1.call-start = ((), (), s32[]{:S(2)}) async-start(), calls=%async_computation.11 | async-start | bytes 4718592 | tf_op jit(solution)/shard_map/reduce_scatter | solution.py:517
  165.8 30.1 %collective-permute-start.1 = (bf16[512,1408]{1,0:T(8,128)(2,1)}, bf16[512,1408]{1,0:T(8,128)(2,1)}, u32[]{:S(2)}, u32[]{:S(2)}) collective-permute-start(bf16[512,1408]{1,0:T(8,128)(2,1)} %get-tuple-element.174), channel_id=1, source_target_pairs={{0,16},{1,9},{2,18},{3,11},{4,20},{5,13},{6,22},{7,15},{8,24},{9,1... | collective-permute-start | bytes 4325384 | tf_op jit(solution)/shard_map/ppermute | solution.py:330
  167.3 114.9 %copy-start.81 = (pred[1024]{0:T(1024)(128)(4,1)}, pred[1024]{0:T(1024)(128)(4,1)S(1)}, u32[]{:S(2)}) copy-start(pred[1024]{0:T(1024)(128)(4,1)S(1)} %get-tuple-element.132) | copy-start | bytes 3076
  167.3 119.5 %copy-start.84 = (pred[1024]{0:T(1024)(128)(4,1)}, pred[1024]{0:T(1024)(128)(4,1)S(1)}, u32[]{:S(2)}) copy-start(pred[1024]{0:T(1024)(128)(4,1)S(1)} %get-tuple-element.131) | copy-start | bytes 3076
  167.5 119.4 %copy-start.69 = (s32[8,128]{1,0:T(8,128)}, s32[8,128]{1,0:T(8,128)S(1)}, u32[]{:S(2)}) copy-start(s32[8,128]{1,0:T(8,128)S(1)} %convolution_convert_fusion.15) | copy-start | bytes 12292
  173.9 38.8 %collective-permute-start.4 = (bf16[2,512,1408]{2,1,0:T(8,128)(2,1)}, bf16[2,512,1408]{2,1,0:T(8,128)(2,1)}, u32[]{:S(2)}, u32[]{:S(2)}) collective-permute-start(bf16[2,512,1408]{2,1,0:T(8,128)(2,1)} %pad_maximum_fusion.4), channel_id=1, source_target_pairs={{0,8},{1,17},{2,10},{3,19},{4,12},{5,21},{6,14},{7,23},{8,0},{9,25... | collective-permute-start | bytes 8650760 | tf_op jit(solution)/shard_map/ppermute | solution.py:330
  178.8 64.9 %collective-permute-start.6 = (bf16[2,512,1408]{2,1,0:T(8,128)(2,1)}, bf16[2,512,1408]{2,1,0:T(8,128)(2,1)}, u32[]{:S(2)}, u32[]{:S(2)}) collective-permute-start(bf16[2,512,1408]{2,1,0:T(8,128)(2,1)} %pad_maximum_fusion.5), channel_id=1, source_target_pairs={{0,8},{1,17},{2,10},{3,19},{4,12},{5,21},{6,14},{7,23},{8,0},{9,25... | collective-permute-start | bytes 8650760 | tf_op jit(solution)/shard_map/ppermute | solution.py:330
  179.5 102.8 %copy-start.72 = (s32[8,128]{1,0:T(8,128)}, s32[8,128]{1,0:T(8,128)S(1)}, u32[]{:S(2)}) copy-start(s32[8,128]{1,0:T(8,128)S(1)} %convolution_convert_fusion.14) | copy-start | bytes 12292
  199.1 75.4 %collective-permute-start.2 = (bf16[2,512,1408]{2,1,0:T(8,128)(2,1)}, bf16[2,512,1408]{2,1,0:T(8,128)(2,1)}, u32[]{:S(2)}, u32[]{:S(2)}) collective-permute-start(bf16[2,512,1408]{2,1,0:T(8,128)(2,1)} %pad_maximum_fusion.3), channel_id=1, source_target_pairs={{0,8},{1,17},{2,10},{3,19},{4,12},{5,21},{6,14},{7,23},{8,0},{9,25... | collective-permute-start | bytes 8650760 | tf_op jit(solution)/shard_map/ppermute | solution.py:330
  285.3 26.1 %collective-permute-start.7 = (bf16[8,64,2048]{2,1,0:T(8,128)(2,1)S(1)}, bf16[8,64,2048]{2,1,0:T(8,128)(2,1)S(1)}, u32[]{:S(2)}, u32[]{:S(2)}) collective-permute-start(bf16[8,64,2048]{2,1,0:T(8,128)(2,1)S(1)} %convolution_convert_fusion.3), channel_id=1, source_target_pairs={{0,16},{1,9},{2,18},{3,11},{4,20},{5,13},{6,22},{7,15},{8,24},{9,1... | collective-permute-start | bytes 6291464 | tf_op jit(solution)/shard_map/ppermute | solution.py:330
  330.3 26.1 %collective-permute-start.8 = (bf16[8,64,2048]{2,1,0:T(8,128)(2,1)S(1)}, bf16[8,64,2048]{2,1,0:T(8,128)(2,1)S(1)}, u32[]{:S(2)}, u32[]{:S(2)}) collective-permute-start(bf16[8,64,2048]{2,1,0:T(8,128)(2,1)S(1)} %bitcast.207), channel_id=1, source_target_pairs={{0,16},{1,9},{2,18},{3,11},{4,20},{5,13},{6,22},{7,15},{8,24},{9,1... | collective-permute-start | bytes 6291464 | tf_op jit(solution)/shard_map/ppermute | solution.py:330
  363.6 99.8 %copy-start.71 = (s32[8,128]{1,0:T(8,128)S(1)}, s32[8,128]{1,0:T(8,128)}, u32[]{:S(2)}) copy-start(s32[8,128]{1,0:T(8,128)} %copy-done.69) | copy-start | bytes 12292
  363.6 99.8 %copy-start.86 = (pred[1024]{0:T(1024)(128)(4,1)S(1)}, pred[1024]{0:T(1024)(128)(4,1)}, u32[]{:S(2)}) copy-start(pred[1024]{0:T(1024)(128)(4,1)} %copy-done.84) | copy-start | bytes 3076
  363.6 99.7 %all-gather.14.cloned.1.call-start = ((), (), s32[]{:S(2)}) async-start(), calls=%async_computation.12 | async-start | bytes 4718592 | tf_op jit(solution)/shard_map/all_gather | solution.py:524
  417.9 190.1 %reduce-scatter.12.cloned.1.call-start = ((), (), s32[]{:S(2)}) async-start(), calls=%async_computation.13 | async-start | bytes 4718592 | tf_op jit(solution)/shard_map/reduce_scatter | solution.py:566
  469.6 75.7 %copy-start.77 = (f32[8,128]{1,0:T(8,128)}, f32[8,128]{1,0:T(8,128)S(1)}, u32[]{:S(2)}) copy-start(f32[8,128]{1,0:T(8,128)S(1)} %get-tuple-element.135) | copy-start | bytes 12292
  469.9 26.1 %collective-permute-start.9 = (bf16[8,64,2048]{2,1,0:T(8,128)(2,1)S(1)}, bf16[8,64,2048]{2,1,0:T(8,128)(2,1)S(1)}, u32[]{:S(2)}, u32[]{:S(2)}) collective-permute-start(bf16[8,64,2048]{2,1,0:T(8,128)(2,1)S(1)} %multiply_convert_fusion), channel_id=1, source_target_pairs={{0,16},{1,9},{2,18},{3,11},{4,20},{5,13},{6,22},{7,15},{8,24},{9,1... | collective-permute-start | bytes 6291464 | tf_op jit(solution)/shard_map/ppermute | solution.py:330
  471.7 73.6 %copy-start.79 = (f32[8,128]{1,0:T(8,128)}, f32[8,128]{1,0:T(8,128)S(1)}, u32[]{:S(2)}) copy-start(f32[8,128]{1,0:T(8,128)S(1)} %get-tuple-element.133) | copy-start | bytes 12292
  481.1 64.2 %copy-start.88 = (f32[1024]{0:T(1024)}, f32[1024]{0:T(1024)S(1)}, u32[]{:S(2)}) copy-start(f32[1024]{0:T(1024)S(1)} %multiply_reduce_fusion.6) | copy-start | bytes 12292
  514.5 26.1 %collective-permute-start.10 = (bf16[8,64,2048]{2,1,0:T(8,128)(2,1)S(1)}, bf16[8,64,2048]{2,1,0:T(8,128)(2,1)S(1)}, u32[]{:S(2)}, u32[]{:S(2)}) collective-permute-start(bf16[8,64,2048]{2,1,0:T(8,128)(2,1)S(1)} %bitcast.208), channel_id=1, source_target_pairs={{0,16},{1,9},{2,18},{3,11},{4,20},{5,13},{6,22},{7,15},{8,24},{9,1... | collective-permute-start | bytes 6291464 | tf_op jit(solution)/shard_map/ppermute | solution.py:330
  559.1 48.9 %copy-start.107 = (f32[128]{0:T(128)S(1)}, f32[128]{0:T(128)}, u32[]{:S(2)}) copy-start(f32[128]{0:T(128)} %copy-done.106) | copy-start | bytes 1540
  559.1 51.9 %copy-start.112 = (f32[128]{0:T(128)S(1)}, f32[128]{0:T(128)}, u32[]{:S(2)}) copy-start(f32[128]{0:T(128)} %broadcast_multiply_fusion) | copy-start | bytes 1540
  559.1 99.3 %all-gather.16.cloned.1.call-start = ((), (), s32[]{:S(2)}) async-start(), calls=%async_computation.14 | async-start | bytes 4718592 | tf_op jit(solution)/shard_map/all_gather | solution.py:604
  613.0 145.0 %reduce-scatter.16.cloned.1.call-start = ((), (), s32[]{:S(2)}) async-start(), calls=%async_computation.16 | async-start | bytes 1474560 | tf_op jit(solution)/shard_map/reduce_scatter | solution.py:622
  689.5 30.1 %collective-permute-start.11 = (bf16[1024,576]{0,1:T(8,128)(2,1)S(1)}, bf16[1024,576]{0,1:T(8,128)(2,1)}, u32[]{:S(2)}, u32[]{:S(2)}) collective-permute-start(bf16[1024,576]{0,1:T(8,128)(2,1)S(1)} %pad_maximum_fusion.11), channel_id=1, source_target_pairs={{8,0},{16,8},{24,16},{9,1},{17,9},{25,17},{10,2},{18,10},{26,18},{... | collective-permute-start | bytes 3538952 | tf_op jit(solution)/shard_map/ppermute | solution.py:617
  725.8 81.3 %all-gather.18.cloned.1.call-start = ((), (), s32[]{:S(2)}) async-start(), calls=%async_computation.17 | async-start | bytes 1474560 | tf_op jit(solution)/shard_map/all_gather | solution.py:661
  760.5 256.9 %reduce-scatter.20.cloned.1.call-start = ((), (), s32[]{:S(2)}) async-start(), calls=%async_computation.21 | async-start | bytes 5406720 | tf_op jit(solution)/shard_map/reduce_scatter | solution.py:583
  771.3 249.9 %reduce-scatter.18.cloned.1.call-start = ((), (), s32[]{:S(2)}) async-start(), calls=%async_computation.19 | async-start | bytes 3932160 | tf_op jit(solution)/shard_map/reduce_scatter | solution.py:583
  786.4 246.7 %reduce-scatter.14.cloned.1.call-start = ((), (), s32[]{:S(2)}) async-start(), calls=%async_computation.15 | async-start | bytes 4718592 | tf_op jit(solution)/shard_map/reduce_scatter | solution.py:628
  787.2 315.7 %all-gather.20.cloned.1.call-start = ((), (), s32[]{:S(2)}) async-start(), calls=%async_computation.18 | async-start | bytes 2654208 | tf_op jit(solution)/shard_map/all_gather | solution.py:665
  809.2 20.4 %collective-permute-start.12 = (f32[256,576]{0,1:T(8,128)S(1)}, f32[256,576]{0,1:T(8,128)}, u32[]{:S(2)}, u32[]{:S(2)}) collective-permute-start(f32[256,576]{0,1:T(8,128)S(1)} %fusion.66), channel_id=1, source_target_pairs={{0,8},{1,9},{2,10},{3,11},{4,12},{5,13},{6,14},{7,15},{8,0},{9,1},... | collective-permute-start | bytes 1769480 | tf_op jit(solution)/shard_map/ppermute | solution.py:330
  824.7 63.9 %collective-permute-start.16 = (bf16[2,512,1408]{1,2,0:T(8,128)(2,1)}, bf16[2,512,1408]{1,2,0:T(8,128)(2,1)}, u32[]{:S(2)}, u32[]{:S(2)}) collective-permute-start(bf16[2,512,1408]{1,2,0:T(8,128)(2,1)} %pad_maximum_fusion.7), channel_id=1, source_target_pairs={{0,8},{1,17},{2,10},{3,19},{4,12},{5,21},{6,14},{7,23},{8,0},{9,25... | collective-permute-start | bytes 8650760 | tf_op jit(solution)/shard_map/ppermute | solution.py:330
  831.6 28.1 %collective-permute-start.13 = (f32[256,576]{0,1:T(8,128)}, f32[256,576]{0,1:T(8,128)S(1)}, u32[]{:S(2)}, u32[]{:S(2)}) collective-permute-start(f32[256,576]{0,1:T(8,128)} %add.383), channel_id=1, source_target_pairs={{0,16},{1,17},{2,18},{3,19},{4,20},{5,21},{6,22},{7,23},{8,24},{9,... | collective-permute-start | bytes 1769480 | tf_op jit(solution)/shard_map/ppermute | solution.py:330
  847.7 80.6 %collective-permute-start.14 = (bf16[2,512,1408]{1,2,0:T(8,128)(2,1)}, bf16[2,512,1408]{1,2,0:T(8,128)(2,1)}, u32[]{:S(2)}, u32[]{:S(2)}) collective-permute-start(bf16[2,512,1408]{1,2,0:T(8,128)(2,1)} %pad_maximum_fusion.6), channel_id=1, source_target_pairs={{0,8},{1,17},{2,10},{3,19},{4,12},{5,21},{6,14},{7,23},{8,0},{9,25... | collective-permute-start | bytes 8650760 | tf_op jit(solution)/shard_map/ppermute | solution.py:330
  861.6 274.8 %all-reduce.3.cloned.1.call-start = ((), (), s32[]{:S(2)}) async-start(), calls=%async_computation.20 | async-start | bytes 262144 | tf_op jit(solution)/shard_map/psum | solution.py:673
  882.8 94.6 %collective-permute-start.18 = (bf16[2,512,1408]{1,2,0:T(8,128)(2,1)}, bf16[2,512,1408]{1,2,0:T(8,128)(2,1)}, u32[]{:S(2)}, u32[]{:S(2)}) collective-permute-start(bf16[2,512,1408]{1,2,0:T(8,128)(2,1)} %pad_maximum_fusion.8), channel_id=1, source_target_pairs={{0,8},{1,17},{2,10},{3,19},{4,12},{5,21},{6,14},{7,23},{8,0},{9,25... | collective-permute-start | bytes 8650760 | tf_op jit(solution)/shard_map/ppermute | solution.py:330
  894.4 89.6 %collective-permute-start.17 = (bf16[512,1408]{0,1:T(8,128)(2,1)}, bf16[512,1408]{0,1:T(8,128)(2,1)}, u32[]{:S(2)}, u32[]{:S(2)}) collective-permute-start(bf16[512,1408]{0,1:T(8,128)(2,1)} %get-tuple-element.167), channel_id=1, source_target_pairs={{0,16},{1,9},{2,18},{3,11},{4,20},{5,13},{6,22},{7,15},{8,24},{9,1... | collective-permute-start | bytes 4325384 | tf_op jit(solution)/shard_map/ppermute | solution.py:330
  908.4 69.0 %copy-start.32 = (bf16[1,512,1408]{1,2,0:T(8,128)(2,1)S(1)}, bf16[1,512,1408]{1,2,0:T(8,128)(2,1)}, u32[]{:S(2)}) copy-start(bf16[1,512,1408]{1,2,0:T(8,128)(2,1)} %copy.193) | copy-start | bytes 4325380
  908.4 69.0 %copy-start.33 = (bf16[1,512,1408]{1,2,0:T(8,128)(2,1)S(1)}, bf16[1,512,1408]{1,2,0:T(8,128)(2,1)}, u32[]{:S(2)}) copy-start(bf16[1,512,1408]{1,2,0:T(8,128)(2,1)} %copy.196) | copy-start | bytes 4325380
  933.9 61.2 %collective-permute-start.15 = (bf16[512,1408]{0,1:T(8,128)(2,1)}, bf16[512,1408]{0,1:T(8,128)(2,1)}, u32[]{:S(2)}, u32[]{:S(2)}) collective-permute-start(bf16[512,1408]{0,1:T(8,128)(2,1)} %get-tuple-element.169), channel_id=1, source_target_pairs={{0,16},{1,9},{2,18},{3,11},{4,20},{5,13},{6,22},{7,15},{8,24},{9,1... | collective-permute-start | bytes 4325384 | tf_op jit(solution)/shard_map/ppermute | solution.py:330
  982.0 30.4 %collective-permute-start.19 = (bf16[512,1408]{0,1:T(8,128)(2,1)}, bf16[512,1408]{0,1:T(8,128)(2,1)}, u32[]{:S(2)}, u32[]{:S(2)}) collective-permute-start(bf16[512,1408]{0,1:T(8,128)(2,1)} %get-tuple-element.165), channel_id=1, source_target_pairs={{0,16},{1,9},{2,18},{3,11},{4,20},{5,13},{6,22},{7,15},{8,24},{9,1... | collective-permute-start | bytes 4325384 | tf_op jit(solution)/shard_map/ppermute | solution.py:330
  (125 other events, 1093.9 us)
Sparse Core Ops, SparseCore 0:
  12.5 26.1 all-gather.9
  40.9 46.6 all-gather.7
  107.9 48.6 reduce-scatter.7
  160.6 45.2 all-gather.11
  363.8 51.5 reduce-scatter.9
  418.0 45.2 all-gather.13
  559.3 48.7 reduce-scatter.11
  613.1 45.2 all-gather.15
  726.0 32.0 reduce-scatter.15
  760.6 21.4 all-gather.17
  785.7 74.8 reduce-scatter.19
  863.4 60.8 reduce-scatter.17
  926.6 50.0 reduce-scatter.13
  978.1 31.0 all-gather.19
  1015.1 121.2 all-reduce.2

commit v2 on v1

v2 whole, which is shorter than its diff:
```python
import functools

import jax
import jax.numpy as jnp
from jax import lax
from jax.experimental import pallas as pl
from jax.experimental.pallas import tpu as pltpu
from jax.sharding import PartitionSpec as P

NOPE = 128
ROPE = 64
VDIM = 128
LATENT = 512
SEQ = 4096
WINDOW = 1024
QUERY_BLOCK = 256

epsilon = 1e-06
masked_value = -1e30
score_scale = (NOPE + ROPE) ** (-0.5)
bf16 = jnp.bfloat16
f32 = jnp.float32
small_cost = pl.CostEstimate(flops=1, bytes_accessed=1, transcendentals=0)


def dot_plain(left, right):
    return lax.dot_general(left, right, (((1,), (0,)), ((), ())), preferred_element_type=f32)


def dot_right_t(left, right):
    return lax.dot_general(left, right, (((1,), (1,)), ((), ())), preferred_element_type=f32)


def dot_left_t(left, right):
    return lax.dot_general(left, right, (((0,), (0,)), ((), ())), preferred_element_type=f32)


def normalize(values):
    factor = lax.rsqrt(jnp.mean(values * values, axis=-1, keepdims=True) + epsilon)
    return (values * factor, factor)


def norm_back(grad_out, unit, factor, gain):
    grad_unit = grad_out * gain
    return factor * (grad_unit - unit * jnp.mean(grad_unit * unit, axis=-1, keepdims=True))


def angles(place, half):
    freq = jnp.exp(-jnp.log(10000.0) * jnp.arange(half, dtype=f32) / half)
    angle = place.astype(f32)[:, None] * freq[None, :]
    return (jnp.cos(angle), jnp.sin(angle))


def silu_parts(values):
    sigma = jax.nn.sigmoid(values)
    return (values * sigma, sigma * (1.0 + values * (1.0 - sigma)))


def head_lanes(block, head):
    lane = lax.broadcasted_iota(jnp.int32, (block, 2 * ROPE), 1)
    return (lane // (ROPE // 2)) % 2 == head


def allowed_keys(low, block, span):
    row = lax.broadcasted_iota(jnp.int32, (block, span), 0)
    col = lax.broadcasted_iota(jnp.int32, (block, span), 1)
    return (col <= row + WINDOW) & (col >= low)


def read_chunks(refs, first, last):
    return jnp.concatenate([ref[:, first:last] for ref in refs], axis=0)


def head_parts(query, lanes, kv, rope, head):
    turned = jnp.where(lanes, query[:, 2 * NOPE :], 0)
    query_head = jnp.concatenate([query[:, head * NOPE : (head + 1) * NOPE], turned], axis=1)
    base = head * (NOPE + VDIM)
    key_head = jnp.concatenate([read_chunks(kv, base, base + NOPE), rope], axis=1)
    return (query_head, key_head, read_chunks(kv, base + NOPE, base + NOPE + VDIM))


def attend_kernel(chunks, normed, cosine, sine, low, query_w, out_w, *refs):
    kv, key_rope = refs[:chunks], refs[chunks : 2 * chunks]
    query_out, mixed_out, log_out, part_out = refs[-4:]
    block = normed.shape[0]
    proj = dot_plain(normed[...], query_w[...])
    turned = proj[:, 2 * NOPE :]
    turned = turn(turned, cosine[...], sine[...])
    query = jnp.concatenate([proj[:, : 2 * NOPE], turned], axis=1).astype(bf16)
    query_out[...] = query
    mask = allowed_keys(low[...], block, WINDOW + block)
    rope = read_chunks(key_rope, 0, 2 * ROPE)
    mixed, logs = [], []
    for head in range(2):
        query_head, key_head, value_head = head_parts(query, head_lanes(block, head), kv, rope, head)
        scores = jnp.where(mask, dot_right_t(query_head, key_head) * score_scale, masked_value)
        top = jnp.max(scores, axis=1, keepdims=True)
        raised = jnp.exp(scores - top)
        total = jnp.sum(raised, axis=1, keepdims=True)
        probs = (raised * (1.0 / total)).astype(bf16)
        mixed.append(dot_plain(probs, value_head))
        logs.append(top + jnp.log(total))
    lane = lax.broadcasted_iota(jnp.int32, (block, 128), 1)
    log_out[...] = jnp.where(lane == 0, logs[0], logs[1])
    mixed = jnp.concatenate(mixed, axis=1).astype(bf16)
    mixed_out[...] = mixed
    part_out[...] = dot_plain(mixed, out_w[...]).astype(bf16)


def by_rows(block, cols, offset=0):
    return pl.BlockSpec((block, cols), lambda i: (i + offset, 0))


def whole(shape):
    return pl.BlockSpec(shape, lambda i: (0, 0))


def unread(arrays):
    return [pl.BlockSpec(memory_space=pl.ANY) for _ in arrays]


def turn(values, cosine, sine):
    return values * cosine + pltpu.roll(values, ROPE, 1) * sine


def turn_back(values, cosine, sine):
    return values * cosine - pltpu.roll(values, ROPE, 1) * sine


def own_keys_kernel(normed, cosine, sine, gain, compress, expand, *refs):
    kv, key_rope, latent = refs[-3:]
    projected = dot_right_t(normed[...], compress[...])
    unit, _ = normalize(projected[:, :LATENT])
    low = (unit * gain[...]).astype(bf16)
    latent[...] = low
    kv[...] = dot_plain(low, expand[...]).astype(bf16)
    key_rope[...] = turn(projected[:, LATENT:], cosine[...], sine[...]).astype(bf16)


def own_keys(normed, cosine, sine, gain, compress, expand, after):
    rows, width = normed.shape
    block = QUERY_BLOCK
    blocks = rows // block
    kv_cols, rope_cols = expand.shape[1], 2 * ROPE
    return pl.pallas_call(
        own_keys_kernel,
        grid=(blocks,),
        in_specs=[
            by_rows(block, width),
            by_rows(block, rope_cols),
            by_rows(block, rope_cols),
            whole((1, LATENT)),
            whole(compress.shape),
            whole(expand.shape),
        ]
        + unread(after),
        out_specs=[
            by_rows(block, kv_cols, blocks),
            by_rows(block, rope_cols, blocks),
            by_rows(block, LATENT),
        ],
        out_shape=[
            jax.ShapeDtypeStruct((2 * rows, kv_cols), bf16),
            jax.ShapeDtypeStruct((2 * rows, rope_cols), bf16),
            jax.ShapeDtypeStruct((rows, LATENT), bf16),
        ],
        compiler_params=pltpu.CompilerParams(vmem_limit_bytes=40 * 1024 * 1024),
        cost_estimate=small_cost,
        name="own_keys",
    )(normed, cosine, sine, gain[None], compress, expand, *after)


def past_keys_kernel(previous, expand, kv_in, rope_in, kv, key_rope):
    kv[...] = dot_plain(previous[:, :LATENT], expand[...]).astype(bf16)
    key_rope[...] = previous[:, LATENT:]


def past_keys(previous, expand, kv, key_rope):
    block = QUERY_BLOCK
    return pl.pallas_call(
        past_keys_kernel,
        grid=(previous.shape[0] // block,),
        in_specs=[by_rows(block, previous.shape[1]), whole(expand.shape)] + unread([kv, key_rope]),
        out_specs=[by_rows(block, kv.shape[1]), by_rows(block, key_rope.shape[1])],
        out_shape=[
            jax.ShapeDtypeStruct(kv.shape, bf16),
            jax.ShapeDtypeStruct(key_rope.shape, bf16),
        ],
        input_output_aliases={2: 0, 3: 1},
        cost_estimate=small_cost,
        name="past_keys",
    )(previous, expand, kv, key_rope)


def attend(normed, cosine, sine, low, query_w, kv, key_rope, out_w, after):
    rows, width = normed.shape
    block = QUERY_BLOCK
    chunks = 1 + WINDOW // block
    query_cols = query_w.shape[1]
    rows_of = functools.partial(by_rows, block)
    return pl.pallas_call(
        functools.partial(attend_kernel, chunks),
        grid=(rows // block,),
        in_specs=[
            rows_of(width),
            rows_of(2 * ROPE),
            rows_of(2 * ROPE),
            rows_of(1),
            whole(query_w.shape),
            whole(out_w.shape),
        ]
        + [rows_of(kv.shape[1], chunk) for chunk in range(chunks)]
        + [rows_of(key_rope.shape[1], chunk) for chunk in range(chunks)]
        + unread(after),
        out_specs=[rows_of(query_cols), rows_of(2 * VDIM), rows_of(128), rows_of(width)],
        out_shape=[
            jax.ShapeDtypeStruct((rows, query_cols), bf16),
            jax.ShapeDtypeStruct((rows, 2 * VDIM), bf16),
            jax.ShapeDtypeStruct((rows, 128), f32),
            jax.ShapeDtypeStruct((rows, width), bf16),
        ],
        compiler_params=pltpu.CompilerParams(vmem_limit_bytes=50 * 1024 * 1024),
        cost_estimate=small_cost,
        name="attend",
    )(normed, cosine, sine, low, query_w, out_w, *([kv] * chunks), *([key_rope] * chunks), *after)


def attend_back_kernel(
    chunks, grad, query_in, logs, cosine, sine, low, query_w, out_w, *refs
):
    kv, key_rope = refs[:chunks], refs[chunks : 2 * chunks]
    query_grad_out, part_out, kv_past, rope_past, kv_own, rope_own, kv_sum, rope_sum = refs[-8:]
    block = grad.shape[0]

    @pl.when(pl.program_id(0) == 0)
    def clear():
        kv_sum[...] = jnp.zeros_like(kv_sum)
        rope_sum[...] = jnp.zeros_like(rope_sum)

    def add(total, past, cols, piece):
        for chunk in range(chunks):
            part = piece[chunk * block : (chunk + 1) * block]
            if chunk < chunks - 1:
                part = part + total[chunk * block : (chunk + 1) * block, cols]
            if chunk == 0:
                past[:, cols] = part.astype(past.dtype)
            else:
                total[(chunk - 1) * block : chunk * block, cols] = part

    mixed_grad = dot_right_t(grad[...], out_w[...]).astype(bf16)
    mask = allowed_keys(low[...], block, WINDOW + block)
    rope = read_chunks(key_rope, 0, 2 * ROPE)
    query = query_in[...]
    plain, turned, rope_piece = [], 0.0, 0.0
    for head in range(2):
        lanes = head_lanes(block, head)
        query_head, key_head, value_head = head_parts(query, lanes, kv, rope, head)
        base = head * (NOPE + VDIM)
        grad_head = mixed_grad[:, head * VDIM : (head + 1) * VDIM]
        scores = jnp.where(mask, dot_right_t(query_head, key_head) * score_scale, masked_value)
        probs = jnp.exp(scores - logs[:, head : head + 1])
        prob_grad = dot_right_t(grad_head, value_head)
        shift = jnp.sum(probs * prob_grad, axis=1, keepdims=True)
        score_grad = (probs * (prob_grad - shift)).astype(bf16)
        key_piece = dot_left_t(score_grad, query_head) * score_scale
        add(kv_sum, kv_past, slice(base, base + NOPE), key_piece[:, :NOPE])
        value_piece = dot_left_t(probs.astype(bf16), grad_head)
        add(kv_sum, kv_past, slice(base + NOPE, base + NOPE + VDIM), value_piece)
        rope_piece = rope_piece + key_piece[:, NOPE:]
        query_piece = dot_plain(score_grad, key_head) * score_scale
        plain.append(query_piece[:, :NOPE])
        turned = turned + jnp.where(lanes, query_piece[:, NOPE:], 0.0)
    add(rope_sum, rope_past, slice(0, 2 * ROPE), rope_piece)
    turned = turn_back(turned, cosine[...], sine[...])
    query_grad = jnp.concatenate(plain + [turned], axis=1).astype(bf16)
    query_grad_out[...] = query_grad
    part_out[...] = dot_right_t(query_grad, query_w[...]).astype(bf16)

    @pl.when(pl.program_id(0) == pl.num_programs(0) - 1)
    def finish():
        kv_own[...] = kv_sum[...].astype(bf16)
        rope_own[...] = rope_sum[...].astype(bf16)


def attend_back(grad, query, logs, cosine, sine, low, query_w, kv, key_rope, out_w, after):
    rows, width = grad.shape
    block = QUERY_BLOCK
    chunks = 1 + WINDOW // block
    query_cols = query_w.shape[1]
    rows_of = functools.partial(by_rows, block)
    kv_cols, rope_cols = kv.shape[1], key_rope.shape[1]
    return pl.pallas_call(
        functools.partial(attend_back_kernel, chunks),
        grid=(rows // block,),
        in_specs=[
            rows_of(width),
            rows_of(query_cols),
            rows_of(128),
            rows_of(2 * ROPE),
            rows_of(2 * ROPE),
            rows_of(1),
            whole(query_w.shape),
            whole(out_w.shape),
        ]
        + [rows_of(kv_cols, chunk) for chunk in range(chunks)]
        + [rows_of(rope_cols, chunk) for chunk in range(chunks)]
        + unread(after),
        out_specs=[
            rows_of(query_cols),
            rows_of(width),
            rows_of(kv_cols),
            rows_of(rope_cols),
            whole((WINDOW, kv_cols)),
            whole((WINDOW, rope_cols)),
        ],
        out_shape=[
            jax.ShapeDtypeStruct((rows, query_cols), bf16),
            jax.ShapeDtypeStruct((rows, width), bf16),
            jax.ShapeDtypeStruct((rows, kv_cols), bf16),
            jax.ShapeDtypeStruct((rows, rope_cols), bf16),
            jax.ShapeDtypeStruct((WINDOW, kv_cols), bf16),
            jax.ShapeDtypeStruct((WINDOW, rope_cols), bf16),
        ],
        scratch_shapes=[pltpu.VMEM((WINDOW, kv_cols), f32), pltpu.VMEM((WINDOW, rope_cols), f32)],
        compiler_params=pltpu.CompilerParams(vmem_limit_bytes=50 * 1024 * 1024),
        cost_estimate=small_cost,
        name="attend_back",
    )(
        grad,
        query,
        logs,
        cosine,
        sine,
        low,
        query_w,
        out_w,
        *([kv] * chunks),
        *([key_rope] * chunks),
        *after,
    )


def norm_kernel(tokens, attention, gain, *refs):
    hidden_out, unit_out, factor_out, branch_out = refs[-4:]
    hidden = tokens[...].astype(f32) + attention[...].astype(f32)
    unit, factor = normalize(hidden)
    hidden_out[...] = hidden
    unit_out[...] = unit
    factor_out[...] = factor
    branch_out[...] = (unit * gain[...]).astype(bf16)


def norm(tokens, attention, gain, after):
    rows, width = tokens.shape
    full = whole((rows, width))
    return pl.pallas_call(
        norm_kernel,
        grid=(1,),
        in_specs=[full, full, whole((1, width))] + unread(after),
        out_specs=[full, full, whole((rows, 1)), full],
        out_shape=[
            jax.ShapeDtypeStruct((rows, width), f32),
            jax.ShapeDtypeStruct((rows, width), f32),
            jax.ShapeDtypeStruct((rows, 1), f32),
            jax.ShapeDtypeStruct((rows, width), bf16),
        ],
        cost_estimate=small_cost,
        name="norm",
    )(tokens, attention, gain[None], *after)


def norm_back_kernel(branch_grad, grad_out, unit, factor, gain, *refs):
    hidden_grad_out, low_out, gain_grad_out = refs[-3:]
    grad = branch_grad[...].astype(f32)
    hidden_grad = grad_out[...] + norm_back(grad, unit[...], factor[...], gain[...])
    hidden_grad_out[...] = hidden_grad
    low_out[...] = hidden_grad.astype(bf16)
    gain_grad_out[...] = jnp.sum(grad * unit[...], axis=0, keepdims=True)


def norm_back_rows(branch_grad, grad_out, unit, factor, gain, after):
    rows, width = unit.shape
    full, line = whole((rows, width)), whole((1, width))
    return pl.pallas_call(
        norm_back_kernel,
        grid=(1,),
        in_specs=[full, full, full, whole((rows, 1)), line] + unread(after),
        out_specs=[full, full, line],
        out_shape=[
            jax.ShapeDtypeStruct((rows, width), f32),
            jax.ShapeDtypeStruct((rows, width), bf16),
            jax.ShapeDtypeStruct((1, width), f32),
        ],
        cost_estimate=small_cost,
        name="norm_back",
    )(branch_grad, grad_out, unit, factor, gain[None], *after)


def load_all(step, pairs):
    @pl.when(step == 0)
    def start():
        for source, target, semaphore in pairs:
            pltpu.make_async_copy(source, target, semaphore).start()


def wait_for(pairs):
    for source, target, semaphore in pairs:
        pltpu.make_async_copy(source, target, semaphore).wait()


def expert_kernel(count, extra, places, slot_in, *refs):
    act_out, slope_out, inner_out, out, held, gate_sum, up_sum, semaphores = refs[count + extra :]
    step = pl.program_id(0)
    order = [(ref, item) for ref in refs[:count] for item in (0, 1)]
    order += [(ref, 2) for ref in refs[:count]]
    pairs = [
        (ref.at[item], held.at[index], semaphores.at[index])
        for index, (ref, item) in enumerate(order)
    ]
    load_all(step, pairs)
    for index in range(count):

        @pl.when(step == index)
        def add(index=index):
            wait_for(pairs[2 * index : 2 * index + 2])
            gate = dot_plain(slot_in[...], held[2 * index])
            up = dot_plain(slot_in[...], held[2 * index + 1])
            if index > 0:
                gate = gate + gate_sum[...]
                up = up + up_sum[...]
            if index < count - 1:
                gate_sum[...] = gate
                up_sum[...] = up
            else:
                act, slope = silu_parts(gate)
                act_out[...] = act.astype(bf16)
                slope_out[...] = (up * slope).astype(bf16)
                inner_out[...] = (act * up).astype(bf16)

        @pl.when(step == count + index)
        def down(index=index):
            wait_for(pairs[2 * count + index : 2 * count + index + 1])
            out[...] = dot_right_t(inner_out[...], held[2 * count + index]).astype(bf16)


def expert_back_kernel(count, extra, places, out_grad, act, slope, *refs):
    gate_out, up_out, in_grad, held, inner_sum, semaphores = refs[count + extra :]
    step = pl.program_id(0)
    order = [(ref, 2) for ref in refs[:count]]
    order += [(ref, item) for ref in refs[:count] for item in (0, 1)]
    pairs = [
        (ref.at[item], held.at[index], semaphores.at[index])
        for index, (ref, item) in enumerate(order)
    ]
    load_all(step, pairs)
    for index in range(count):

        @pl.when(step == index)
        def add(index=index):
            wait_for(pairs[index : index + 1])
            inner = dot_plain(out_grad[...], held[index])
            if index > 0:
                inner = inner + inner_sum[...]
            if index < count - 1:
                inner_sum[...] = inner
            else:
                gate_out[...] = (inner * slope[...].astype(f32)).astype(bf16)
                up_out[...] = (inner * act[...].astype(f32)).astype(bf16)

        @pl.when(step == count + index)
        def back(index=index):
            first = count + 2 * index
            wait_for(pairs[first : first + 2])
            in_grad[...] = (
                dot_right_t(gate_out[...], held[first]) + dot_right_t(up_out[...], held[first + 1])
            ).astype(bf16)


def expert_call(kernel, name, places, slots, fixed, weights, outputs, sums, after):
    count = len(weights)
    rows, width = slots.shape
    _, depth, hidden = weights[0].shape
    inner = pl.BlockSpec((rows, hidden), lambda i, places: (0, 0))
    return pl.pallas_call(
        functools.partial(kernel, count, len(after)),
        grid_spec=pltpu.PrefetchScalarGridSpec(
            num_scalar_prefetch=1,
            grid=(2 * count,),
            in_specs=[
                pl.BlockSpec((rows, depth), lambda i, places: (0, places[jnp.minimum(i, count - 1)]))
            ]
            + [inner] * len(fixed)
            + unread(weights)
            + unread(after),
            out_specs=[inner] * outputs
            + [pl.BlockSpec((rows, depth), lambda i, places: (0, places[jnp.maximum(i - count, 0)]))],
            scratch_shapes=[pltpu.VMEM((3 * count, depth, hidden), bf16)]
            + [pltpu.VMEM((rows, hidden), f32)] * sums
            + [pltpu.SemaphoreType.DMA((3 * count,))],
        ),
        out_shape=[jax.ShapeDtypeStruct((rows, hidden), bf16)] * outputs
        + [jax.ShapeDtypeStruct((rows, width), bf16)],
        compiler_params=pltpu.CompilerParams(vmem_limit_bytes=56 * 1024 * 1024),
        cost_estimate=small_cost,
        name=name,
    )(places, slots, *fixed, *weights, *after)


def weight_grad_kernel(count, plan, places, *refs):
    half = count // 2
    outs = refs[-1 - half * len(plan) :]
    step = pl.program_id(0)
    for number, segments in enumerate(plan):
        first = 0
        for terms in segments:
            grad = 0.0
            for left, right in terms:
                grad = grad + dot_left_t(refs[left][...], refs[right][...])
            last = first + grad.shape[1]
            for index in range(count):

                @pl.when(step == index)
                def store(index=index, number=number, cols=slice(first, last), grad=grad):
                    if index < half:
                        outs[0][index, number, :, cols] = grad.astype(bf16)
                    else:
                        out = outs[1 + (index - half) * len(plan) + number]
                        out[:, cols] = grad.astype(bf16)

            first = last


def weight_grads(name, places, outputs, after=()):
    count = places.shape[0]
    lefts, rights = [], []
    for segments in outputs:
        for terms in segments:
            for left, right in terms:
                if not any(left is other for other in lefts):
                    lefts.append(left)
                rights.append(right)
    plan, position, flops = [], len(lefts), 0
    for segments in outputs:
        planned, columns = [], 0
        for terms in segments:
            numbers = []
            for left, right in terms:
                numbers.append(([left is other for other in lefts].index(True), position))
                position += 1
                flops += 2 * left.shape[0] * left.shape[1] * right.shape[1]
            planned.append(numbers)
            columns += terms[0][1].shape[1]
        plan.append(planned)
    piece = (lefts[0].shape[1] // count, columns)
    shapes = [(count // 2, len(outputs)) + piece] + [piece] * (count // 2 * len(outputs))
    kept, *given = pl.pallas_call(
        functools.partial(weight_grad_kernel, count, plan),
        grid_spec=pltpu.PrefetchScalarGridSpec(
            num_scalar_prefetch=1,
            grid=(count,),
            in_specs=[
                pl.BlockSpec((left.shape[0], left.shape[1] // count), lambda i, places: (0, places[i]))
                for left in lefts
            ]
            + [pl.BlockSpec(right.shape, lambda i, places: (0, 0)) for right in rights]
            + unread(after),
            out_specs=[pl.BlockSpec(shapes[0], lambda i, places: (0, 0, 0, 0))]
            + [pl.BlockSpec(shape, lambda i, places: (0, 0)) for shape in shapes[1:]],
        ),
        out_shape=[jax.ShapeDtypeStruct(shape, bf16) for shape in shapes],
        compiler_params=pltpu.CompilerParams(vmem_limit_bytes=56 * 1024 * 1024),
        cost_estimate=small_cost,
        name=name,
    )(places, *lefts, *rights, *after)
    return kept, given


def lead(array, *indices):
    shape = (1,) * len(indices) + array.shape[-2:]
    return pl.BlockSpec(shape, lambda i, *prefetched: indices + (0, 0))


def flat(ref):
    for _ in ref.shape[2:]:
        ref = ref.at[0]
    return ref[...].astype(f32)


def finish_kernel(cuts, own, arrived, other, *refs):
    total = flat(own) + flat(arrived) + flat(other)
    outs = refs[-len(cuts) :]
    for (first, last, turned), out in zip(cuts, outs):
        part = total[:, first:last]
        out[...] = part.T[: out.shape[0]] if turned else part


def finish(name, parts, cuts, sizes, after):
    own, arrived, other = parts
    arrived, other = arrived[0], other[0]
    rows = own.shape[-2]
    shapes = [
        (size, rows) if turned else (rows, last - first)
        for (first, last, turned), size in zip(cuts, sizes)
    ]
    return pl.pallas_call(
        functools.partial(finish_kernel, cuts),
        grid=(1,),
        in_specs=[lead(own, 0, 0), lead(arrived), lead(other)] + unread(after),
        out_specs=[whole(shape) for shape in shapes],
        out_shape=[jax.ShapeDtypeStruct(shape, f32) for shape in shapes],
        compiler_params=pltpu.CompilerParams(vmem_limit_bytes=40 * 1024 * 1024),
        cost_estimate=small_cost,
        name=name,
    )(own, arrived, other, *after)


def prepare_kernel(bits, gate, up, down, *outs):
    for step in range(2):

        @pl.when(pl.program_id(0) == step)
        def copy(step=step):
            outs[step][0] = gate[0]
            outs[step][1] = up[0]
            outs[step][2] = down[0].T


def prepare(bit, gate, up, down):
    _, depth, hidden = gate.shape
    shape = (3, depth, hidden)

    def chosen(array):
        return pl.BlockSpec(
            (1,) + array.shape[1:], lambda i, bits: (jnp.where(i == 0, 1 - bits[0], bits[0]), 0, 0)
        )

    return pl.pallas_call(
        prepare_kernel,
        grid_spec=pltpu.PrefetchScalarGridSpec(
            num_scalar_prefetch=1,
            grid=(2,),
            in_specs=[chosen(gate), chosen(up), chosen(down)],
            out_specs=[pl.BlockSpec(shape, lambda i, bits: (0, 0, 0))] * 2,
        ),
        out_shape=[jax.ShapeDtypeStruct(shape, bf16)] * 2,
        compiler_params=pltpu.CompilerParams(vmem_limit_bytes=56 * 1024 * 1024),
        cost_estimate=small_cost,
        name="prepare",
    )(bit.reshape(1), gate, up, down)


def dispatch_kernel(branch, slots, *refs):
    mine_out, other_out = refs[-2:]
    capacity = slots.shape[1] // 2
    for owner in range(slots.shape[0]):
        rows = slots.shape[2]
        rows_in = dot_plain(slots[owner], branch[owner * rows : (owner + 1) * rows]).astype(bf16)
        mine_out[owner * capacity : (owner + 1) * capacity] = rows_in[:capacity]
        other_out[owner * capacity : (owner + 1) * capacity] = rows_in[capacity:]


def slot_specs(slots, step):
    members, both, rows = slots.shape
    return (
        pl.BlockSpec((step, both, rows), lambda i: (i, 0, 0)),
        functools.partial(by_rows, step * both // 2),
        functools.partial(by_rows, step * rows),
        (members // step,),
    )


def dispatch(branch, slots, after):
    members, both, _ = slots.shape
    width = branch.shape[1]
    slot_spec, slot_rows, token_rows, grid = slot_specs(slots, 2)
    shape = jax.ShapeDtypeStruct((members * both // 2, width), bf16)
    return pl.pallas_call(
        dispatch_kernel,
        grid=grid,
        in_specs=[token_rows(width), slot_spec] + unread(after),
        out_specs=[slot_rows(width)] * 2,
        out_shape=[shape, shape],
        cost_estimate=small_cost,
        name="dispatch",
    )(branch, slots, *after)


def shared_kernel(branch, weights, act_out, slope_out, inner_out):
    hidden = act_out.shape[1]
    both = dot_right_t(branch[...], weights[...])
    gate, up = both[:, :hidden], both[:, hidden:]
    act, slope = silu_parts(gate)
    act_out[...] = act.astype(bf16)
    slope_out[...] = (up * slope).astype(bf16)
    inner_out[...] = (act * up).astype(bf16)


def shared_forward(branch, weights):
    rows, width = branch.shape
    hidden = weights.shape[0] // 3
    block = 512
    shape = jax.ShapeDtypeStruct((rows, hidden), bf16)
    return pl.pallas_call(
        shared_kernel,
        grid=(rows // block,),
        in_specs=[by_rows(block, width), whole((2 * hidden, width))],
        out_specs=[by_rows(block, hidden)] * 3,
        out_shape=[shape] * 3,
        compiler_params=pltpu.CompilerParams(vmem_limit_bytes=40 * 1024 * 1024),
        cost_estimate=small_cost,
        name="shared_forward",
    )(branch, weights)


def shared_back_kernel(grad, down, act, slope, *refs):
    out = refs[-1]
    hidden = act.shape[1]
    inner = dot_right_t(grad[...], down[...])
    out[:, :hidden] = (inner * slope[...].astype(f32)).astype(bf16)
    out[:, hidden:] = (inner * act[...].astype(f32)).astype(bf16)


def shared_back(grad, weights, act, slope, after):
    rows, width = grad.shape
    hidden = act.shape[1]
    block = 512
    return pl.pallas_call(
        shared_back_kernel,
        grid=(rows // block,),
        in_specs=[
            by_rows(block, width),
            pl.BlockSpec((hidden, width), lambda i: (2, 0)),
            by_rows(block, hidden),
            by_rows(block, hidden),
        ]
        + unread(after),
        out_specs=by_rows(block, 2 * hidden),
        out_shape=jax.ShapeDtypeStruct((rows, 2 * hidden), bf16),
        compiler_params=pltpu.CompilerParams(vmem_limit_bytes=40 * 1024 * 1024),
        cost_estimate=small_cost,
        name="shared_back",
    )(grad, weights, act, slope, *after)


def combine_kernel(inner, down, slots, out_mine, out_other, gate_mine, gate_other, out):
    rows = slots.shape[2]
    capacity = slots.shape[1] // 2
    total = dot_plain(inner[...], down[...])
    for owner in range(slots.shape[0]):
        tokens = slice(owner * rows, (owner + 1) * rows)
        places = slice(owner * capacity, (owner + 1) * capacity)
        mine = dot_left_t(slots[owner, :capacity], out_mine[places])
        other = dot_left_t(slots[owner, capacity:], out_other[places])
        part = total[tokens] + gate_mine[tokens] * mine + gate_other[tokens] * other
        out[tokens] = part.astype(bf16)


def combine(inner, weights, slots, out_mine, out_other, gate_mine, gate_other):
    hidden, width = inner.shape[1], weights.shape[1]
    slot_spec, slot_rows, token_rows, grid = slot_specs(slots, 4)
    return pl.pallas_call(
        combine_kernel,
        grid=grid,
        in_specs=[
            token_rows(hidden),
            pl.BlockSpec((hidden, width), lambda i: (2, 0)),
            slot_spec,
            slot_rows(width),
            slot_rows(width),
            token_rows(1),
            token_rows(1),
        ],
        out_specs=token_rows(width),
        out_shape=jax.ShapeDtypeStruct((inner.shape[0], width), bf16),
        compiler_params=pltpu.CompilerParams(vmem_limit_bytes=50 * 1024 * 1024),
        cost_estimate=small_cost,
        name="combine",
    )(inner, weights, slots, out_mine, out_other, gate_mine, gate_other)


def out_grad_kernel(grad, slots, out_mine, out_other, gate_mine, gate_other, *refs):
    grad_mine, grad_other, gate_grad_mine, gate_grad_other = refs
    rows = slots.shape[2]
    capacity = slots.shape[1] // 2
    for owner in range(slots.shape[0]):
        places = slice(owner * capacity, (owner + 1) * capacity)
        hot = slots[owner].astype(f32)
        both = dot_plain(slots[owner], grad[owner * rows : (owner + 1) * rows])
        halves = (
            (hot[:capacity], both[:capacity], out_mine, gate_mine, grad_mine, gate_grad_mine),
            (hot[capacity:], both[capacity:], out_other, gate_other, grad_other, gate_grad_other),
        )
        for hot_half, slot_grad, out, gate, grad_out, gate_out in halves:
            slot_gate = jnp.sum(hot_half * gate[owner], axis=1, keepdims=True)
            grad_out[places] = (slot_gate * slot_grad).astype(bf16)
            gate_grad = jnp.sum(slot_grad * out[places].astype(f32), axis=1, keepdims=True)
            gate_out[owner] = jnp.sum(hot_half * gate_grad, axis=0, keepdims=True)


def out_grads(grad, slots, out_mine, out_other, gate_mine, gate_other):
    members, both, rows = slots.shape
    width = grad.shape[1]
    slot_spec, slot_rows, token_rows, grid = slot_specs(slots, 2)
    line = pl.BlockSpec((2, 1, rows), lambda i: (i, 0, 0))
    grads = jax.ShapeDtypeStruct((members * both // 2, width), bf16)
    gates = jax.ShapeDtypeStruct((members, 1, rows), f32)
    return pl.pallas_call(
        out_grad_kernel,
        grid=grid,
        in_specs=[token_rows(width), slot_spec, slot_rows(width), slot_rows(width), line, line],
        out_specs=[slot_rows(width), slot_rows(width), line, line],
        out_shape=[grads, grads, gates, gates],
        compiler_params=pltpu.CompilerParams(vmem_limit_bytes=40 * 1024 * 1024),
        cost_estimate=small_cost,
        name="out_grads",
    )(
        grad,
        slots,
        out_mine,
        out_other,
        gate_mine.reshape(members, 1, rows),
        gate_other.reshape(members, 1, rows),
    )


def combine_back_kernel(grads, logit_grad, weights, router, slots, in_mine, in_other, *refs):
    out = refs[-1]
    rows = slots.shape[2]
    capacity = slots.shape[1] // 2
    total = dot_plain(grads[...], weights[...]) + dot_right_t(logit_grad[...], router[...])
    for owner in range(slots.shape[0]):
        tokens = slice(owner * rows, (owner + 1) * rows)
        places = slice(owner * capacity, (owner + 1) * capacity)
        arrived = jnp.concatenate([in_mine[places], in_other[places]], axis=0)
        out[tokens] = (total[tokens] + dot_left_t(slots[owner], arrived)).astype(bf16)


def combine_back(grads, logit_grad, weights, router, slots, in_mine, in_other, after):
    width = weights.shape[1]
    slot_spec, slot_rows, token_rows, grid = slot_specs(slots, 4)
    return pl.pallas_call(
        combine_back_kernel,
        grid=grid,
        in_specs=[
            token_rows(grads.shape[1]),
            token_rows(logit_grad.shape[1]),
            whole((grads.shape[1], width)),
            whole(router.shape),
            slot_spec,
            slot_rows(width),
            slot_rows(width),
        ]
        + unread(after),
        out_specs=token_rows(width),
        out_shape=jax.ShapeDtypeStruct((grads.shape[0], width), bf16),
        compiler_params=pltpu.CompilerParams(vmem_limit_bytes=50 * 1024 * 1024),
        cost_estimate=small_cost,
        name="combine_back",
    )(grads, logit_grad, weights, router, slots, in_mine, in_other, *after)


def latent_grad_kernel(kv_past, rope_past, kv_own, rope_own, expand, *refs):
    out = refs[-1]
    for index, (kv, rope) in enumerate(((kv_past, rope_past), (kv_own, rope_own))):
        out[index, :, :LATENT] = dot_right_t(kv[...], expand[...]).astype(bf16)
        out[index, :, LATENT:] = rope[...]


def latent_grads(kv_past, rope_past, kv_own, rope_own, expand, after):
    rows, cols = kv_past.shape
    rope_cols = rope_past.shape[1]
    block = QUERY_BLOCK
    kv_spec, rope_spec = by_rows(block, cols), by_rows(block, rope_cols)
    return pl.pallas_call(
        latent_grad_kernel,
        grid=(rows // block,),
        in_specs=[kv_spec, rope_spec, kv_spec, rope_spec, whole(expand.shape)] + unread(after),
        out_specs=pl.BlockSpec((2, block, LATENT + rope_cols), lambda i: (0, i, 0)),
        out_shape=jax.ShapeDtypeStruct((2, rows, LATENT + rope_cols), bf16),
        cost_estimate=small_cost,
        name="latent_grads",
    )(kv_past, rope_past, kv_own, rope_own, expand, *after)


def first_block_kernel(blocks, *refs):
    refs[-1][...] = blocks[0]


def first_block(blocks, after):
    shape = blocks.shape[1:]
    return pl.pallas_call(
        first_block_kernel,
        grid=(1,),
        in_specs=[lead(blocks, 0)] + unread(after),
        out_specs=whole(shape),
        out_shape=jax.ShapeDtypeStruct(shape, bf16),
        cost_estimate=small_cost,
        name="first_block",
    )(blocks, *after)


def latent_back_kernel(own, back, unit, factor, gain, cosine, sine, *refs):
    grad_out, gain_grad_out = refs[-2:]
    grad = own[...].astype(f32) + back[...].astype(f32)
    plain = grad[:, :LATENT]
    gain_grad_out[...] = jnp.sum(plain * unit[...], axis=0, keepdims=True)
    grad_out[:, :LATENT] = norm_back(plain, unit[...], factor[...], gain[...]).astype(bf16)
    grad_out[:, LATENT:] = turn_back(grad[:, LATENT:], cosine[...], sine[...]).astype(bf16)


def latent_back_rows(own, back, unit, factor, gain, cosine, sine, after):
    rows, cols = own.shape
    inputs = [own, back, unit, factor, gain[None], cosine, sine]
    return pl.pallas_call(
        latent_back_kernel,
        grid=(1,),
        in_specs=[whole(array.shape) for array in inputs] + unread(after),
        out_specs=[whole((rows, cols)), whole((1, LATENT))],
        out_shape=[
            jax.ShapeDtypeStruct((rows, cols), bf16),
            jax.ShapeDtypeStruct((1, LATENT), f32),
        ],
        cost_estimate=small_cost,
        name="latent_back",
    )(*inputs, *after)


def tokens_back_kernel(grad, projected, compress, unit, factor, gain, hidden_grad, *refs):
    out, gain_grad_out = refs[-2:]
    total = grad[...].astype(f32) + dot_plain(projected[...], compress[...])
    gain_grad_out[...] = jnp.sum(total * unit[...], axis=0, keepdims=True)
    out[...] = hidden_grad[...] + norm_back(total, unit[...], factor[...], gain[...])


def tokens_back(grad, projected, compress, unit, factor, gain, hidden_grad, after):
    rows, width = grad.shape
    inputs = [grad, projected, compress, unit, factor, gain[None], hidden_grad]
    return pl.pallas_call(
        tokens_back_kernel,
        grid=(1,),
        in_specs=[whole(array.shape) for array in inputs] + unread(after),
        out_specs=[whole((rows, width)), whole((1, width))],
        out_shape=[
            jax.ShapeDtypeStruct((rows, width), f32),
            jax.ShapeDtypeStruct((1, width), f32),
        ],
        compiler_params=pltpu.CompilerParams(vmem_limit_bytes=40 * 1024 * 1024),
        cost_estimate=small_cost,
        name="tokens_back",
    )(*inputs, *after)


def slice_grad_kernel(index, left, right, *refs):
    refs[-1][...] = dot_left_t(left[...], right[...])


def slice_grad(left, right, index, cols, after):
    rows = left.shape[0]
    return pl.pallas_call(
        slice_grad_kernel,
        grid_spec=pltpu.PrefetchScalarGridSpec(
            num_scalar_prefetch=1,
            grid=(1,),
            in_specs=[
                pl.BlockSpec(left.shape, lambda i, index: (0, 0)),
                pl.BlockSpec((rows, cols), lambda i, index: (0, index[0])),
            ]
            + unread(after),
            out_specs=pl.BlockSpec((left.shape[1], cols), lambda i, index: (0, 0)),
        ),
        out_shape=jax.ShapeDtypeStruct((left.shape[1], cols), f32),
        cost_estimate=small_cost,
        name="slice_grad",
    )(index.reshape(1), left, right, *after)


def place_kernel(turned, bits, own, arrived, other, *refs):
    out = refs[-1]

    @pl.when(pl.program_id(0) == 0)
    def first():
        total = flat(own) + flat(arrived)
        out[0] = total.T if turned else total

    @pl.when(pl.program_id(0) == 1)
    def second():
        total = flat(other)
        out[0] = total.T if turned else total


def place_experts(bit, parts, item, turned, after):
    own, arrived, other = parts
    arrived_item, other_item = arrived[item], other[item]
    shape = own.shape[:-3:-1] if turned else own.shape[-2:]
    return pl.pallas_call(
        functools.partial(place_kernel, turned),
        grid_spec=pltpu.PrefetchScalarGridSpec(
            num_scalar_prefetch=1,
            grid=(2,),
            in_specs=[lead(own, 0, item), lead(arrived_item), lead(other_item)]
            + unread(after),
            out_specs=pl.BlockSpec(
                (1,) + shape, lambda i, bits: (jnp.where(i == 0, bits[0], 1 - bits[0]), 0, 0)
            ),
        ),
        out_shape=jax.ShapeDtypeStruct((2,) + shape, f32),
        compiler_params=pltpu.CompilerParams(vmem_limit_bytes=40 * 1024 * 1024),
        cost_estimate=small_cost,
        name="place_experts",
    )(bit.reshape(1), own, arrived_item, other_item, *after)


def split_query_columns(weight):
    head = NOPE + ROPE
    half = ROPE // 2
    pieces = [weight[:, :NOPE], weight[:, head : head + NOPE]]
    for part in range(2):
        for index in range(2):
            first = index * head + NOPE + part * half
            pieces.append(weight[:, first : first + half])
    return jnp.concatenate(pieces, axis=1)


def join_query_columns(grad):
    half = ROPE // 2
    base = 2 * NOPE
    pieces = []
    for index in range(2):
        pieces.append(grad[:, index * NOPE : (index + 1) * NOPE])
        for part in range(2):
            first = base + part * ROPE + index * half
            pieces.append(grad[:, first : first + half])
    return jnp.concatenate(pieces, axis=1)


class Pairing:
    def __init__(self, groups, members):
        self.groups = groups
        self.members = members
        self.bits = groups.bit_length() - 1
        top = self.bits - 1
        self.partner = (1 << top, 1)
        self.others = (
            [1 << bit for bit in range(top)],
            [1 << (bit + 1) for bit in range(top)],
        )
        self.group = lax.axis_index("dp")
        self.odd = lax.axis_index("expert") % 2

    def chosen(self, masks):
        return jnp.where(self.odd == 1, masks[1], masks[0])

    def place(self, masks):
        return self.group ^ self.chosen(masks)

    def bit(self):
        return jnp.where(self.group & self.chosen(self.partner), 1, 0)

    def swap(self, value, masks):
        pairs = []
        for group in range(self.groups):
            for member in range(self.members):
                other = group ^ masks[member % 2]
                pairs.append((group * self.members + member, other * self.members + member))
        return lax.ppermute(value, ("dp", "expert"), pairs)

    def swap_partner(self, value):
        return self.swap(value, self.partner)

    def masks(self):
        masks = [(0, 0), self.partner]
        for step in zip(*self.others):
            masks = masks + [(even ^ step[0], odd ^ step[1]) for even, odd in masks]
        return masks

    def places(self):
        return jnp.stack([self.place(mask) for mask in self.masks()])

    def spread(self, held):
        for step in zip(*self.others):
            held = held + [self.swap(piece, step) for piece in held]
        return held

    def collect(self, kept, given):
        steps = list(reversed(list(zip(*self.others))))
        for number, step in enumerate(steps):
            arrived = [self.swap(piece, step) for piece in given]
            if number < len(steps) - 1:
                total = kept.astype(f32) + jnp.stack(arrived).reshape(kept.shape).astype(f32)
                total = total.astype(bf16)
                half = total.shape[0] // 2
                kept, given = total[:half], list(total[half:].reshape((-1,) + total.shape[2:]))
        return (kept, arrived)

    def exchange(self, kept, arrived):
        items = kept.shape[1]
        total = [
            (kept[1, item].astype(f32) + arrived[items + item].astype(f32)).astype(bf16)
            for item in range(items)
        ]
        return (kept, arrived, [self.swap_partner(piece) for piece in total])

    def gather_members(self, value):
        member = lax.axis_index("expert")
        rows = value.shape[0]
        chips = [value]
        for other in range(1, self.members // 2):
            pairs = [(i, i ^ (2 * other)) for i in range(self.members)]
            chips.append(lax.ppermute(value, "expert", pairs))
        both = lax.ppermute(
            jnp.concatenate(chips), "expert", [(i, i ^ 1) for i in range(self.members)]
        )
        held = []
        for number, block in enumerate(chips):
            held += [block, both[number * rows : (number + 1) * rows]]
        bit = 1
        while bit < self.members:
            flip = (member & bit) != 0
            held = [jnp.where(flip, held[i ^ bit], held[i]) for i in range(self.members)]
            bit *= 2
        return jnp.concatenate(held)

    def total(self, value):
        for bit in range(self.bits):
            arrived = self.swap(value.astype(bf16), (1 << bit, 1 << (self.bits - 1 - bit)))
            value = value + arrived.astype(f32)
        return value

    def total_all(self, value):
        size = self.groups * self.members
        for bit in range(size.bit_length() - 1):
            pairs = [(i, i ^ (1 << bit)) for i in range(size)]
            value = value + lax.ppermute(value, ("dp", "expert"), pairs)
        return value


def body(
    tokens,
    target,
    valid,
    routes,
    lengths,
    first_gain_vector,
    second_gain_vector,
    latent_gain_vector,
    latent_compress_weight,
    query_weight,
    latent_expand_weight,
    output_weight,
    router_weight,
    shared_gate_weight,
    shared_up_weight,
    shared_down_weight,
    expert_gate_weight,
    expert_up_weight,
    expert_down_weight,
):
    rows, width = tokens.shape
    members = lax.axis_size("expert")
    groups = lax.axis_size("dp")
    member = lax.axis_index("expert")
    group = lax.axis_index("dp")
    group_size = rows * members
    local_experts = expert_gate_weight.shape[0]
    route_count = routes.shape[1]
    expert_count = router_weight.shape[1]
    hidden_width = expert_gate_weight.shape[2]
    capacity = rows * route_count * 4 // (3 * local_experts * members)
    pairing = Pairing(groups, members)
    bit = pairing.bit()

    def pick(array, index):
        return lax.dynamic_index_in_dim(array, index, 0, False)

    tokens_float = tokens.astype(f32)
    own_unit, own_factor = normalize(tokens_float)
    own_normed = (own_unit * first_gain_vector).astype(bf16)
    normed = lax.all_gather(own_normed, "expert", axis=0, tiled=True)
    half = ROPE // 2
    compress_t = latent_compress_weight.T
    compress_t = jnp.concatenate(
        [compress_t[: LATENT + half]]
        + [compress_t[LATENT : LATENT + half]]
        + [compress_t[LATENT + half :]] * 2
    )
    index = group * group_size + jnp.arange(group_size, dtype=jnp.int32)
    seq_id = jnp.floor_divide(index, SEQ)
    place = index - seq_id * SEQ
    cosine, sine = angles(place, half)
    cosine = jnp.concatenate([cosine] * 4, axis=1)
    sine = jnp.concatenate([-sine, -sine, sine, sine], axis=1)
    own_cos = lax.dynamic_slice_in_dim(cosine, member * rows, rows, 0)
    own_sin = lax.dynamic_slice_in_dim(sine, member * rows, rows, 0)
    projected = dot_right_t(own_normed, compress_t)
    latent_unit, latent_factor = normalize(projected[:, :LATENT])
    turned = projected[:, LATENT:]
    turned = turned * own_cos + jnp.roll(turned, ROPE, axis=1) * own_sin
    latent = jnp.concatenate([latent_unit * latent_gain_vector, turned], axis=1).astype(bf16)
    before = lax.ppermute(latent, "dp", [(i, i + 1) for i in range(groups - 1)])
    before = first_block(before[None], [normed])
    previous = lax.all_gather(before, "expert", axis=0, tiled=True)

    places = pairing.places()
    given, kept = prepare(bit, expert_gate_weight, expert_up_weight, expert_down_weight)
    expert_w = pairing.spread([kept, pairing.swap_partner(given)])

    shared_hidden_width = shared_gate_weight.shape[1]
    padded = -(-shared_hidden_width // 128) * 128
    shared_w = jnp.concatenate(
        [
            jnp.pad(weight, ((0, padded - shared_hidden_width), (0, 0)))
            for weight in (shared_gate_weight.T, shared_up_weight.T, shared_down_weight)
        ]
    )

    counted = valid.astype(f32)
    count = pairing.total_all(jnp.full((8, 128), jnp.sum(counted)))[0, 0]

    bounds = lax.dynamic_slice_in_dim(
        jnp.cumsum(lengths, axis=1), group * group_size // SEQ, 1, 0
    )
    doc_start = jnp.max(jnp.where(bounds <= place[:, None], bounds, 0), axis=1)
    in_block = jnp.arange(group_size, dtype=jnp.int32) % QUERY_BLOCK
    low = jnp.maximum(doc_start - place + WINDOW + in_block, in_block + 1)[:, None]

    hot = jnp.any(routes[:, :, None] == jnp.arange(expert_count, dtype=jnp.int32), axis=1)
    routes_t = routes.T.reshape(route_count, members, rows)
    order = jnp.arange(rows, dtype=jnp.int32)
    earlier = (order[:, None] < order[None, :]).astype(bf16)
    mine = member * local_experts + bit
    other = member * local_experts + 1 - bit

    def slots_of(expert):
        hit = jnp.any(routes_t == expert, axis=0)
        rank = dot_plain(hit.astype(bf16), earlier).astype(jnp.int32)
        slot = jnp.arange(capacity, dtype=jnp.int32)[None, :, None]
        return (hit[:, None, :] & (rank[:, None, :] == slot)).astype(bf16)

    slots = jnp.concatenate([slots_of(mine), slots_of(other)], axis=1)

    query_w = split_query_columns(query_weight)
    kv, key_rope, group_latent = own_keys(
        normed,
        cosine,
        sine,
        latent_gain_vector,
        compress_t,
        latent_expand_weight,
        [shared_w, query_w],
    )
    kv, key_rope = past_keys(previous, latent_expand_weight, kv, key_rope)
    query, mixed, logs, attention_part = attend(
        normed,
        cosine,
        sine,
        low,
        query_w,
        kv,
        key_rope,
        output_weight,
        expert_w[1:2],
    )
    attention = lax.psum_scatter(attention_part, "expert", scatter_dimension=0, tiled=True)
    hidden, hidden_unit, hidden_factor, own_branch = norm(
        tokens, attention, second_gain_vector, expert_w[2:3]
    )
    branch = lax.all_gather(own_branch, "expert", axis=0, tiled=True)

    logits = jnp.where(hot, dot_plain(branch, router_weight), masked_value)
    top = jnp.max(logits, axis=1, keepdims=True)
    raised = jnp.where(hot, jnp.exp(logits - top), 0.0)
    gates = raised / jnp.sum(raised, axis=1, keepdims=True)
    experts = jnp.arange(expert_count, dtype=jnp.int32)[None, :]
    gate_mine = jnp.sum(jnp.where(experts == mine, gates, 0.0), axis=1, keepdims=True)
    gate_other = jnp.sum(jnp.where(experts == other, gates, 0.0), axis=1, keepdims=True)

    in_mine, in_other = dispatch(branch, slots, expert_w[3:])
    in_arrived = pairing.swap_partner(in_other)
    shared_act, shared_slope, shared_hidden = shared_forward(branch, shared_w)
    act_a, slope_a, inner_a, out_arrived = expert_call(
        expert_kernel, "expert", places, in_arrived, [], expert_w, 3, 2, [shared_hidden]
    )
    out_other = pairing.swap_partner(out_arrived)
    act_m, slope_m, inner_m, out_mine = expert_call(
        expert_kernel, "expert", places, in_mine, [], expert_w, 3, 2, [out_arrived]
    )
    branch_part = combine(
        shared_hidden, shared_w, slots, out_mine, out_other, gate_mine, gate_other
    )
    branch_sum = lax.psum_scatter(branch_part, "expert", scatter_dimension=0, tiled=True)
    result = hidden + branch_sum.astype(f32)
    difference = result - target.astype(f32)
    squares = jnp.sum(counted[:, None] * difference * difference)
    total_tokens = rows * members * groups
    grad_out = total_tokens / count * counted[:, None] * difference

    grad_low = lax.all_gather(grad_out.astype(bf16), "expert", axis=0, tiled=True)

    out_grad_mine, out_grad_other, gate_grad_mine, gate_grad_other = out_grads(
        grad_low, slots, out_mine, out_other, gate_mine, gate_other
    )
    out_grad_arrived = pairing.swap_partner(out_grad_other)
    shared_grad = shared_back(grad_low, shared_w, shared_act, shared_slope, [out_grad_mine])
    gate_gm, up_gm, in_grad_mine = expert_call(
        expert_back_kernel,
        "expert_back",
        places,
        out_grad_mine,
        [act_m, slope_m],
        expert_w,
        2,
        1,
        [shared_grad],
    )
    gate_ga, up_ga, in_grad_arrived = expert_call(
        expert_back_kernel,
        "expert_back",
        places,
        out_grad_arrived,
        [act_a, slope_a],
        expert_w,
        2,
        1,
        [in_grad_mine],
    )
    in_grad_other = pairing.swap_partner(in_grad_arrived)

    down_kept, down_given = weight_grads(
        "down_grad",
        places,
        [[[(out_grad_mine, inner_m), (out_grad_arrived, inner_a)]]],
        [in_grad_arrived],
    )

    gate_grads = jnp.where(experts == mine, gate_grad_mine.reshape(-1, 1), 0.0) + jnp.where(
        experts == other, gate_grad_other.reshape(-1, 1), 0.0
    )
    logit_grad = gates * (gate_grads - jnp.sum(gates * gate_grads, axis=1, keepdims=True))
    logit_grad = logit_grad.astype(bf16)
    grad_router = dot_left_t(branch, logit_grad)
    branch_grad_part = combine_back(
        shared_grad,
        logit_grad,
        shared_w,
        router_weight,
        slots,
        in_grad_mine,
        in_grad_other,
        [down_kept],
    )
    branch_grad = lax.psum_scatter(
        branch_grad_part, "expert", scatter_dimension=0, tiled=True
    )

    gate_up_kept, gate_up_given = weight_grads(
        "gate_up_grad",
        places,
        [
            [[(in_mine, gate_gm), (in_arrived, gate_ga)]],
            [[(in_mine, up_gm), (in_arrived, up_ga)]],
        ],
        [branch_grad_part],
    )
    down_terms = pairing.collect(down_kept, down_given)
    gate_up_terms = pairing.collect(gate_up_kept, gate_up_given)
    shared_kept, shared_given = weight_grads(
        "shared_grads",
        places,
        [[[(branch, shared_grad)], [(grad_low, shared_hidden)]]],
        [gate_up_kept],
    )
    shared_terms = pairing.collect(shared_kept, shared_given)
    down_parts = pairing.exchange(*down_terms)
    gate_up_parts = pairing.exchange(*gate_up_terms)

    grad_hidden_own, grad_hidden_low, grad_norm2 = norm_back_rows(
        branch_grad,
        grad_out,
        hidden_unit,
        hidden_factor,
        second_gain_vector,
        down_terms[1] + gate_up_terms[1][:1] + [shared_kept],
    )
    grad_attention = lax.all_gather(grad_hidden_low, "expert", axis=0, tiled=True)
    query_grad, normed_grad_part, kv_past, rope_past, kv_own, rope_own = attend_back(
        grad_attention,
        query,
        logs,
        cosine,
        sine,
        low,
        query_w,
        kv,
        key_rope,
        output_weight,
        gate_up_terms[1],
    )

    latent_grad = lax.psum_scatter(
        latent_grads(
            kv_past, rope_past, kv_own, rope_own, latent_expand_weight, shared_terms[1]
        ),
        "expert",
        scatter_dimension=1,
        tiled=True,
    )
    normed_grad = lax.psum_scatter(
        normed_grad_part, "expert", scatter_dimension=0, tiled=True
    )

    attention_kept, attention_given = weight_grads(
        "attention_grads",
        places,
        [[[(normed, query_grad)], [(grad_attention, mixed)]]],
        [kv_own],
    )
    attention_terms = pairing.collect(attention_kept, attention_given)
    expand_grad = (
        dot_left_t(previous[:, :LATENT], kv_past) + dot_left_t(group_latent, kv_own)
    ).astype(bf16)
    expand_grad = expand_grad.reshape(groups, -1, expand_grad.shape[1])
    expand_pieces = jnp.stack([pick(expand_grad, places[i]) for i in range(groups)])[:, None]
    expand_parts = pairing.exchange(
        *pairing.collect(
            expand_pieces[: groups // 2], list(expand_pieces[groups // 2 :].squeeze(1))
        )
    )
    back = lax.ppermute(
        first_block(latent_grad, [attention_kept] + down_parts[2] + gate_up_parts[2][:1]),
        "dp",
        [(i + 1, i) for i in range(groups - 1)],
    )

    grad_projected, grad_latent_gain = latent_back_rows(
        latent_grad[1],
        back,
        latent_unit,
        latent_factor,
        latent_gain_vector,
        own_cos,
        own_sin,
        [],
    )
    group_grad = pairing.gather_members(grad_projected)
    expert_down_gradient = place_experts(bit, down_parts, 0, True, [grad_projected])
    expert_gate_gradient = place_experts(bit, gate_up_parts, 0, False, [grad_projected])
    expert_up_gradient = place_experts(bit, gate_up_parts, 1, False, [grad_projected])
    shared_parts = pairing.exchange(*shared_terms)
    attention_parts = pairing.exchange(*attention_terms)
    slice_cols = width // members
    compress_slice = slice_grad(
        group_grad,
        normed,
        member,
        slice_cols,
        [expert_down_gradient, expert_gate_gradient, expert_up_gradient]
        + attention_terms[1],
    )
    compress_slice = pairing.total(
        jnp.concatenate(
            [
                compress_slice[:LATENT],
                compress_slice[LATENT : LATENT + half] + compress_slice[LATENT + half : LATENT + ROPE],
                compress_slice[LATENT + ROPE : LATENT + ROPE + half]
                + compress_slice[LATENT + ROPE + half :],
            ]
        )
    ).astype(bf16)
    grad_kva = (
        lax.all_gather(compress_slice, "expert", axis=0, tiled=True)
        .reshape(members, -1, slice_cols)
        .transpose(0, 2, 1)
        .reshape(width, -1)
        .astype(f32)
    )
    grad_tokens, grad_norm1 = tokens_back(
        normed_grad,
        grad_projected,
        compress_t,
        own_unit,
        own_factor,
        first_gain_vector,
        grad_hidden_own,
        [compress_slice],
    )
    sums = [grad_router.reshape(-1), grad_norm2[0], grad_norm1[0], grad_latent_gain[0]]
    cuts = [sum(part.size for part in sums[:number]) for number in range(1, len(sums) + 1)]
    sums = pairing.total_all(
        jnp.concatenate(sums + [jnp.full((8 * 128,), squares)]).reshape(-1, 128)
    ).reshape(-1)
    grad_router = sums[: cuts[0]].reshape(grad_router.shape)
    grad_norm2, grad_norm1 = sums[cuts[0] : cuts[1]], sums[cuts[1] : cuts[2]]
    grad_latent_gain, squares = sums[cuts[2] : cuts[3]], sums[-1]

    query_cols, mixed_cols = query_w.shape[1], mixed.shape[1]
    shared_gate_gradient, shared_up_gradient, shared_down_gradient = finish(
        "shared_finish",
        shared_parts,
        [(i * padded, (i + 1) * padded, True) for i in range(3)],
        [shared_hidden_width] * 3,
        [compress_slice],
    )
    query_weight_gradient, output_weight_gradient = finish(
        "attention_finish",
        attention_parts,
        [(0, query_cols, False), (query_cols, query_cols + mixed_cols, True)],
        [0, mixed_cols],
        [compress_slice],
    )
    shared_gate_gradient, shared_up_gradient = shared_gate_gradient.T, shared_up_gradient.T
    query_weight_gradient = join_query_columns(query_weight_gradient)
    (latent_expand_gradient,) = finish(
        "expand_finish",
        expand_parts,
        [(0, expand_grad.shape[2], False)],
        [0],
        [compress_slice],
    )
    return (
        result.astype(bf16),
        squares / (count * width),
        grad_tokens,
        grad_norm1,
        grad_norm2,
        grad_latent_gain,
        grad_kva,
        query_weight_gradient,
        latent_expand_gradient,
        output_weight_gradient,
        grad_router,
        shared_gate_gradient,
        shared_up_gradient,
        shared_down_gradient,
        expert_gate_gradient,
        expert_up_gradient,
        expert_down_gradient,
    )


def solution(mesh):
    placed = (
        P(("dp", "expert"), None),
        P(("dp", "expert"), None),
        P(("dp", "expert")),
        P("dp", None),
        P(),
        P(),
        P(),
        P(),
        P(),
        P(None, "expert"),
        P(None, "expert"),
        P("expert", None),
        P(),
        P(None, "expert"),
        P(None, "expert"),
        P("expert", None),
        P("expert", "dp", None),
        P("expert", "dp", None),
        P("expert", None, "dp"),
    )
    return jax.shard_map(
        body,
        mesh=mesh,
        in_specs=placed,
        out_specs=(
            P(("dp", "expert"), None),
            P(),
            P(("dp", "expert"), None),
            P(),
            P(),
            P(),
            P(),
            P("dp", "expert"),
            P("dp", "expert"),
            P("expert", "dp"),
            P(),
            P("dp", "expert"),
            P("dp", "expert"),
            P("expert", "dp"),
            P("expert", "dp", None),
            P("expert", "dp", None),
            P("expert", None, "dp"),
        ),
        check_vma=False,
    )
```

time: 1160 us -> 859 us (0.74)
  Pallas kernels: 37.4 us -> 272 us
  matrix products: 196 us -> 9.46 us
  waiting for transfers between devices: 501 us -> 359 us
  blocking collectives: 108 us -> 0 us
  local copies, waits for them, and re-layouts: 149 us -> 71.2 us
  other arithmetic: 104 us -> 56.2 us
  starting transfers between devices: 31.3 us -> 62.8 us
    pallas_call x0 -> x31, Pallas kernels: none -> 235 us  [the longest x4 80.3 us: expert_call(): pl.pallas_call(functools.partial(kernel, count, len(after)), grid_spec=pl...]
    psum x2 -> x0, blocking collectives: 108 us -> none  [the longest x1 65.8 us: body(): lax.psum((squares, grad_norm1, grad_norm2, grad_latent_gain, grad_router)...]
    dot_general x13 -> x1, matrix products: 68 us -> 0.93 us  [dot_right_t(): lax.dot_general(left, right, (((1,), (1,)), ((), ())), preferred_element_...]
    dot_general x14 -> x3, matrix products: 56.7 us -> 1.57 us  [dot_plain(): lax.dot_general(left, right, (((1,), (0,)), ((), ())), preferred_element_...]
    all_gather x4 -> x3, waiting for transfers between devices: 66.2 us -> 12.6 us  [the longest x1 12.6 us: body(): previous = lax.all_gather(before, 'expert', axis=0, tiled=True)]
    reduce_scatter x1, waiting for transfers between devices: 48.3 us -> 0.01 us  [body(): lax.psum_scatter(branch_grad_part, 'expert', scatter_dimension=0, tiled=T...]
    dot_general x12 -> x3, matrix products: 49.9 us -> 6.96 us  [dot_left_t(): lax.dot_general(left, right, (((0,), (0,)), ((), ())), preferred_element_...]
    reduce_scatter x1, waiting for transfers between devices: 37.3 us -> 0.47 us  [body(): lax.psum_scatter(attention_part, 'expert', scatter_dimension=0, tiled=True)]
  transfers between devices with their start and end apart: 35 -> 54, of which waited for: 24 -> 31; matrix products, arithmetic and copies ran while one was open for 29% -> 10% of each run, Pallas kernels for 0% -> 21%
where the time goes in v2:
time: 859 us; the launch traced here: 849 us
  waiting for transfers between devices  359 us (42%)
  Pallas kernels  272 us (32%)
  local copies, waits for them, and re-layouts  71.2 us (8%)
  starting transfers between devices  62.8 us (7%)
  other arithmetic  56.2 us (7%)
  between operations  18.3 us (2%)
  matrix products  9.46 us (1%)
    ppermute x27, waiting for transfers between devices, swap(): return lax.ppermute(value, ('dp', 'expert'), pairs)  193 us
    pallas_call x4, Pallas kernels, expert_call(): pl.pallas_call(functools.partial(kernel, count, len(after)), grid_spec=pl...  80.3 us
    pallas_call x4, Pallas kernels, weight_grads(): pl.pallas_call(functools.partial(weight_grad_kernel, count, plan), grid_s...  62 us
    all_gather x1, waiting for transfers between devices, body(): lax.all_gather(grad_out.astype(bf16), 'expert', axis=0, tiled=True)  45.4 us
    unnamed x178, local copies, waits for them, and re-layouts  44.3 us
    ppermute x27, starting transfers between devices, swap(): return lax.ppermute(value, ('dp', 'expert'), pairs)  35.5 us
    ppermute x10, waiting for transfers between devices, total_all(): value = value + lax.ppermute(value, ('dp', 'expert'), pairs)  31.7 us
    reduce_scatter x1, waiting for transfers between devices, body(): lax.psum_scatter(branch_part, 'expert', scatter_dimension=0, tiled=True)  28 us
  transfers between devices with their start and end apart: 54, of which 31 were waited for; matrix products, arithmetic and copies ran while one was open for 10% of the time, Pallas kernels for 21%

profile of v2, /device:TPU:0, one launch (start us, length us, event | category | flops | bytes accessed | tf_op | source)
XLA Modules:
  0.0 849.2 jit_solution(825106411438053189)
XLA Ops:
  11.0 7.7 prepare.1
  41.8 19.1 %all-gather.7.cloned.1.call-done.refs_0_.normed.right = bf16[1024,2048]{1,0:T(8,128)(2,1)} async-done(((bf16[128,2048]{1,0:T(8,128)(2,1)}), bf16[1024,2048]{1,0:T(8,128)(2,1)}) %all-gather.7.cloned.1.call-update) | async-done | bytes 4194320 | tf_op jit(solution)/shard_map/all_gather | solution.py:1177
  65.1 5.0 concatenate.47.refs_1_.query_w
  72.4 4.3 fusion.5.refs_0_.weights.down
  78.3 5.2 own_keys.1
  86.6 12.6 %all-gather.9.cloned.1.call-done.previous = bf16[1024,640]{1,0:T(8,128)(2,1)} async-done(((bf16[128,640]{1,0:T(8,128)(2,1)}), bf16[1024,640]{1,0:T(8,128)(2,1)}) %all-gather.9.cloned.1.call-update) | async-done | bytes 1310736 | tf_op jit(solution)/shard_map/all_gather | solution.py:1200
  99.2 4.2 past_keys.1
  106.5 15.6 %attend.1 = (bf16[1024,384]{1,0:T(8,128)(2,1)S(1)}, bf16[1024,256]{1,0:T(8,128)(2,1)S(1)}, f32[1024,128]{1,0:T(8,128)S(1)}, bf16[1024,2048]{1,0:T(8,128)(2,1)}) custom-call(bf16[1024,2048]{1,0:T(8,128)(2,1)} %all-gather.7.cloned.1.call-done.refs_0_.normed.right, f32[1024,128]{1,0:T(8,128)S(1)} %copy-done.22, f32[1024,128]{1,0:T(8,128)S(1)} %pad_maximum_fusion.4.sine, ...), custom_call_target="tpu_custom_call" | custom-call | flops 1 | bytes 1 | tf_op jit(solution)/shard_map/attend/pallas_call | solution.py:201
  126.3 48.8 %collective-permute-done.2.refs_0_.refs_2_ = bf16[3,512,1408]{2,1,0:T(8,128)(2,1)} collective-permute-done((bf16[3,512,1408]{2,1,0:T(8,128)(2,1)}, bf16[3,512,1408]{2,1,0:T(8,128)(2,1)}, u32[]{:S(2)}, u32[]{:S(2)}) %collective-permute-start.2) | collective-permute-done | bytes 4325408 | tf_op jit(solution)/shard_map/ppermute | solution.py:1064
  181.6 47.6 %collective-permute-done.3.refs_0_.refs_3_ = bf16[3,512,1408]{2,1,0:T(8,128)(2,1)} collective-permute-done((bf16[3,512,1408]{2,1,0:T(8,128)(2,1)}, bf16[3,512,1408]{2,1,0:T(8,128)(2,1)}, u32[]{:S(2)}, u32[]{:S(2)}) %collective-permute-start.3) | collective-permute-done | bytes 4325408 | tf_op jit(solution)/shard_map/ppermute | solution.py:1064
  229.2 5.4 dispatch.1
  241.3 3.8 shared_forward.1
  247.8 13.3 %collective-permute-done.4.slot_in.refs_1_ = bf16[512,2048]{1,0:T(8,128)(2,1)} collective-permute-done((bf16[512,2048]{1,0:T(8,128)(2,1)}, bf16[512,2048]{1,0:T(8,128)(2,1)}, u32[]{:S(2)}, u32[]{:S(2)}) %collective-permute-start.4) | collective-permute-done | bytes 2097184 | tf_op jit(solution)/shard_map/ppermute | solution.py:1064
  261.0 19.6 %expert.2 = (bf16[512,1408]{1,0:T(8,128)(2,1)}, bf16[512,1408]{1,0:T(8,128)(2,1)}, bf16[512,1408]{1,0:T(8,128)(2,1)}, bf16[512,2048]{1,0:T(8,128)(2,1)}) custom-call(s32[4]{0:T(128)} %pad_add_fusion.places, bf16[512,2048]{1,0:T(8,128)(2,1)} %collective-permute-done.4.slot_in.refs_1_, bf16[3,512,1408]{2,1,0:T(8,128)(2,1)} %get-tuple-element.93.refs_0_, ...), custom_call_target="tpu_custom_call" | custom-call | flops 1 | bytes 1 | tf_op jit(solution)/shard_map/expert/pallas_call | solution.py:484
  287.4 19.0 %expert.3 = (bf16[512,1408]{1,0:T(8,128)(2,1)}, bf16[512,1408]{1,0:T(8,128)(2,1)}, bf16[512,1408]{1,0:T(8,128)(2,1)}, bf16[512,2048]{1,0:T(8,128)(2,1)}) custom-call(s32[4]{0:T(128)} %pad_add_fusion.places, bf16[512,2048]{1,0:T(8,128)(2,1)} %get-tuple-element.97.slot_in.refs_0_, bf16[3,512,1408]{2,1,0:T(8,128)(2,1)} %get-tuple-element.93.refs_0_, ...), custom_call_target="tpu_custom_call" | custom-call | flops 1 | bytes 1 | tf_op jit(solution)/shard_map/expert/pallas_call | solution.py:484
  307.1 8.4 combine.1
  336.7 28.0 %reduce-scatter.8.cloned.1.call-done = bf16[128,2048]{1,0:T(8,128)(2,1)} async-done(((bf16[1024,2048]{1,0:T(8,128)(2,1)}), bf16[128,2048]{1,0:T(8,128)(2,1)}) %reduce-scatter.8.cloned.1.call-update) | async-done | bytes 524304 | tf_op jit(solution)/shard_map/reduce_scatter | solution.py:1289
  368.6 45.4 %all-gather.13.cloned.1.call-done.grad.refs_1_ = bf16[1024,2048]{1,0:T(8,128)(2,1)} async-done(((bf16[128,2048]{1,0:T(8,128)(2,1)}), bf16[1024,2048]{1,0:T(8,128)(2,1)}) %all-gather.13.cloned.1.call-update) | async-done | bytes 4194320 | tf_op jit(solution)/shard_map/all_gather | solution.py:1296
  418.1 4.0 out_grads.1
  427.5 20.5 %expert_back.2 = (bf16[512,1408]{1,0:T(8,128)(2,1)}, bf16[512,1408]{1,0:T(8,128)(2,1)}, bf16[512,2048]{1,0:T(8,128)(2,1)}) custom-call(s32[4]{0:T(128)} %pad_add_fusion.places, bf16[512,2048]{1,0:T(8,128)(2,1)} %copy-done.14, bf16[512,1408]{1,0:T(8,128)(2,1)} %get-tuple-element.106.act, bf16[512,1408]{1,0:T(8,128)(2,1)} %get-tuple-element.107.slope, ...), custom_call_target="tpu_custom_call" | custom-call | flops 1 | bytes 1 | tf_op jit(solution)/shard_map/expert_back/pallas_call | solution.py:484
  448.4 21.2 %expert_back.3 = (bf16[512,1408]{1,0:T(8,128)(2,1)}, bf16[512,1408]{1,0:T(8,128)(2,1)}, bf16[512,2048]{1,0:T(8,128)(2,1)}) custom-call(s32[4]{0:T(128)} %pad_add_fusion.places, bf16[512,2048]{1,0:T(8,128)(2,1)} %collective-permute-done.11.out_grad.refs_1_, bf16[512,1408]{1,0:T(8,128)(2,1)} %get-tuple-element.110.act, ...), custom_call_target="tpu_custom_call" | custom-call | flops 1 | bytes 1 | tf_op jit(solution)/shard_map/expert_back/pallas_call | solution.py:484
  474.2 13.5 %down_grad.1 = (bf16[2,1,512,1408]{3,2,1,0:T(8,128)(2,1)}, bf16[512,1408]{1,0:T(8,128)(2,1)}, bf16[512,1408]{1,0:T(8,128)(2,1)}) custom-call(s32[4]{0:T(128)} %pad_add_fusion.places, bf16[512,2048]{1,0:T(8,128)(2,1)} %copy-done.14, bf16[512,2048]{1,0:T(8,128)(2,1)} %collective-permute-done.11.out_grad.refs_1_, bf16[512,1408]{1,0:T(8,128)(2,1)} %get-tuple-element.113.refs_2_, ...), custom_call_target="tpu_custom_call" | custom-call | flops 1 | bytes 1 | tf_op jit(solution)/shard_map/down_grad/pallas_call | solution.py:556
  487.7 8.3 collective-permute-done.12.in_other
  496.0 9.8 %combine_back.1.refs_6_ = bf16[1024,2048]{1,0:T(8,128)(2,1)} custom-call(bf16[1024,768]{1,0:T(8,128)(2,1)S(1)} %copy-done.12, bf16[1024,16]{1,0:T(8,128)(2,1)S(1)} %multiply_convert_fusion.1.logit_grad, bf16[1152,2048]{1,0:T(8,128)(2,1)} %fusion.5.refs_0_.weights.down, bf16[2048,16]{1,0:T(8,128)(2,1)S(1)} %copy-done.38, bf16[8,128,128]{2,1,0:T(8,128)(2,1)S(1)} %copy-done.31, ...), custom_call_target="tpu_custom_call" | custom-call | flops 1 | bytes 1 | tf_op jit(solution)/shard_map/combine_back/pallas_call | solution.py:840
  508.0 24.3 %gate_up_grad.1 = (bf16[2,2,512,1408]{3,2,1,0:T(8,128)(2,1)}, bf16[512,1408]{1,0:T(8,128)(2,1)}, bf16[512,1408]{1,0:T(8,128)(2,1)}, bf16[512,1408]{1,0:T(8,128)(2,1)}, bf16[512,1408]{1,0:T(8,128)(2,1)}) custom-call(s32[4]{0:T(128)} %pad_add_fusion.places, bf16[512,2048]{1,0:T(8,128)(2,1)} %get-tuple-element.97.slot_in.refs_0_, ...), custom_call_target="tpu_custom_call" | custom-call | flops 1 | bytes 1 | tf_op jit(solution)/shard_map/gate_up_grad/pallas_call | solution.py:556
  533.7 12.9 %shared_grads.1 = (bf16[2,1,512,1152]{3,2,1,0:T(8,128)(2,1)}, bf16[512,1152]{1,0:T(8,128)(2,1)}, bf16[512,1152]{1,0:T(8,128)(2,1)}) custom-call(s32[4]{0:T(128)} %pad_add_fusion.places, bf16[1024,2048]{1,0:T(8,128)(2,1)} %all-gather.11.cloned.1.call-done.branch.refs_0_, bf16[1024,2048]{1,0:T(8,128)(2,1)} %all-gather.13.cloned.1.call-done.grad.refs_1_, ...), custom_call_target="tpu_custom_call" | custom-call | flops 1 | bytes 1 | tf_op jit(solution)/shard_map/shared_grads/pallas_call | solution.py:556
  546.6 9.6 %collective-permute-done.15.refs_2_.refs_10_.arrived = bf16[512,1408]{1,0:T(8,128)(2,1)} collective-permute-done((bf16[512,1408]{1,0:T(8,128)(2,1)}, bf16[512,1408]{1,0:T(8,128)(2,1)}, u32[]{:S(2)}, u32[]{:S(2)}) %collective-permute-start.15) | collective-permute-done | bytes 1441824 | tf_op jit(solution)/shard_map/ppermute | solution.py:1064
  565.2 13.9 %collective-permute-done.17.refs_12_ = bf16[512,1408]{1,0:T(8,128)(2,1)} collective-permute-done((bf16[512,1408]{1,0:T(8,128)(2,1)}, bf16[512,1408]{1,0:T(8,128)(2,1)}, u32[]{:S(2)}, u32[]{:S(2)}) %collective-permute-start.17) | collective-permute-done | bytes 1441824 | tf_op jit(solution)/shard_map/ppermute | solution.py:1064
  579.1 15.4 %collective-permute-done.18.refs_13_ = bf16[512,1408]{1,0:T(8,128)(2,1)} collective-permute-done((bf16[512,1408]{1,0:T(8,128)(2,1)}, bf16[512,1408]{1,0:T(8,128)(2,1)}, u32[]{:S(2)}, u32[]{:S(2)}) %collective-permute-start.18) | collective-permute-done | bytes 1441824 | tf_op jit(solution)/shard_map/ppermute | solution.py:1064
  594.5 15.4 %collective-permute-done.16.refs_11_.arrived = bf16[512,1408]{1,0:T(8,128)(2,1)} collective-permute-done((bf16[512,1408]{1,0:T(8,128)(2,1)}, bf16[512,1408]{1,0:T(8,128)(2,1)}, u32[]{:S(2)}, u32[]{:S(2)}) %collective-permute-start.16) | collective-permute-done | bytes 1441824 | tf_op jit(solution)/shard_map/ppermute | solution.py:1064
  614.1 21.5 %attend_back.1 = (bf16[1024,384]{1,0:T(8,128)(2,1)S(1)}, bf16[1024,2048]{1,0:T(8,128)(2,1)}, bf16[1024,512]{1,0:T(8,128)(2,1)}, bf16[1024,128]{1,0:T(8,128)(2,1)...) custom-call(bf16[1024,2048]{1,0:T(8,128)(2,1)} %all-gather.15.cloned.1.call-done.grad.refs_1_, ...), custom_call_target="tpu_custom_call" | custom-call | flops 1 | bytes 1 | tf_op jit(solution)/shard_map/attend_back/pallas_call | solution.py:292
  637.9 5.2 latent_grads.1
  648.6 4.9 fusion.6
  656.3 11.3 %attention_grads.1 = (bf16[2,1,512,640]{3,2,1,0:T(8,128)(2,1)}, bf16[512,640]{1,0:T(8,128)(2,1)}, bf16[512,640]{1,0:T(8,128)(2,1)}) custom-call(s32[4]{0:T(128)} %pad_add_fusion.places, bf16[1024,2048]{1,0:T(8,128)(2,1)} %all-gather.7.cloned.1.call-done.refs_0_.normed.right, bf16[1024,2048]{1,0:T(8,128)(2,1)} %all-gather.15.cloned.1.call-done.grad.refs_1_, ...), custom_call_target="tpu_custom_call" | custom-call | flops 1 | bytes 1 | tf_op jit(solution)/shard_map/attention_grads/pallas_call | solution.py:556
  667.6 14.3 %collective-permute-done.22.refs_2_.other = bf16[512,1408]{1,0:T(8,128)(2,1)} collective-permute-done((bf16[512,1408]{1,0:T(8,128)(2,1)}, bf16[512,1408]{1,0:T(8,128)(2,1)}, u32[]{:S(2)}, u32[]{:S(2)}) %collective-permute-start.22) | collective-permute-done | bytes 1441824 | tf_op jit(solution)/shard_map/ppermute | solution.py:1064
  685.6 7.2 collective-permute-done.23.back
  699.9 10.1 %collective-permute-done.24 = bf16[128,640]{1,0:T(8,128)(2,1)S(1)} collective-permute-done((bf16[128,640]{1,0:T(8,128)(2,1)}, bf16[128,640]{1,0:T(8,128)(2,1)S(1)}, u32[]{:S(2)}, u32[]{:S(2)}) %collective-permute-start.24) | collective-permute-done | bytes 163872 | tf_op jit(solution)/shard_map/ppermute | solution.py:1108
  710.0 9.8 %collective-permute-done.26 = bf16[128,640]{1,0:T(8,128)(2,1)S(1)} collective-permute-done((bf16[128,640]{1,0:T(8,128)(2,1)}, bf16[128,640]{1,0:T(8,128)(2,1)S(1)}, u32[]{:S(2)}, u32[]{:S(2)}) %collective-permute-start.26) | collective-permute-done | bytes 163872 | tf_op jit(solution)/shard_map/ppermute | solution.py:1108
  721.7 4.0 collective-permute-start.27
  731.6 5.0 place_experts.4.refs_1_
  736.6 5.2 place_experts.3.refs_0_
  744.5 4.7 place_experts.5.refs_2_
  762.2 5.0 collective-permute-done.31
  770.3 4.5 fusion.58
  791.5 4.8 collective-permute-start.34
  800.7 8.6 %collective-permute-done.34 = f32[300,128]{1,0:T(8,128)S(1)} collective-permute-done((f32[300,128]{1,0:T(8,128)S(1)}, f32[300,128]{1,0:T(8,128)S(1)}, u32[]{:S(2)}, u32[]{:S(2)}) %collective-permute-start.34) | collective-permute-done | bytes 153632 | tf_op jit(solution)/shard_map/ppermute | solution.py:1132
  817.2 3.9 collective-permute-done.35
  823.0 4.0 collective-permute-done.36
  (381 shorter events, 214.9 us)
Async XLA Ops:
  7.2 53.7 %all-gather.7.cloned.1.call-start = ((), (), s32[]{:S(2)}) async-start(), calls=%async_computation.5 | async-start | bytes 4718592 | tf_op jit(solution)/shard_map/all_gather | solution.py:1177
  10.9 88.3 %all-gather.9.cloned.1.call-start = ((), (), s32[]{:S(2)}) async-start(), calls=%async_computation.6 | async-start | bytes 1474560 | tf_op jit(solution)/shard_map/all_gather | solution.py:1200
  18.7 84.7 %collective-permute-start.1 = (bf16[3,512,1408]{2,1,0:T(8,128)(2,1)}, bf16[3,512,1408]{2,1,0:T(8,128)(2,1)}, u32[]{:S(2)}, u32[]{:S(2)}) collective-permute-start(bf16[3,512,1408]{2,1,0:T(8,128)(2,1)} %get-tuple-element.91), channel_id=1, source_target_pairs={{0,16},{1,9},{2,18},{3,11},{4,20},{5,13},{6,22},{7,15},{8,24},{9,1... | collective-permute-start | bytes 12976136 | tf_op jit(solution)/shard_map/ppermute | solution.py:1064
  33.8 8.0 collective-permute-start
  62.5 113.0 %reduce-scatter.6.cloned.1.call-start = ((), (), s32[]{:S(2)}) async-start(), calls=%async_computation.7 | async-start | bytes 4718592 | tf_op jit(solution)/shard_map/reduce_scatter | solution.py:1262
  124.7 104.5 %all-gather.11.cloned.1.call-start = ((), (), s32[]{:S(2)}) async-start(), calls=%async_computation.8 | async-start | bytes 4718592 | tf_op jit(solution)/shard_map/all_gather | solution.py:1266
  124.8 50.3 %collective-permute-start.2 = (bf16[3,512,1408]{2,1,0:T(8,128)(2,1)}, bf16[3,512,1408]{2,1,0:T(8,128)(2,1)}, u32[]{:S(2)}, u32[]{:S(2)}) collective-permute-start(bf16[3,512,1408]{2,1,0:T(8,128)(2,1)} %get-tuple-element.93.refs_0_), channel_id=1, source_target_pairs={{0,8},{1,17},{2,10},{3,19},{4,12},{5,21},{6,14},{7,23},{8,0},{9,25... | collective-permute-start | bytes 12976136 | tf_op jit(solution)/shard_map/ppermute | solution.py:1064
  178.4 186.3 %reduce-scatter.8.cloned.1.call-start = ((), (), s32[]{:S(2)}) async-start(), calls=%async_computation.9 | async-start | bytes 4718592 | tf_op jit(solution)/shard_map/reduce_scatter | solution.py:1289
  178.9 50.3 %collective-permute-start.3 = (bf16[3,512,1408]{2,1,0:T(8,128)(2,1)}, bf16[3,512,1408]{2,1,0:T(8,128)(2,1)}, u32[]{:S(2)}, u32[]{:S(2)}) collective-permute-start(bf16[3,512,1408]{2,1,0:T(8,128)(2,1)} %collective-permute-done.1.refs_10_.refs_1_), channel_id=1, source_target_pairs={{0,8},{1,17},{2,10},{3,19},{4,12},{5,21},{6,14},{7,23},{8,0},{9,25... | collective-permute-start | bytes 12976136 | tf_op jit(solution)/shard_map/ppermute | solution.py:1064
  234.7 26.4 %collective-permute-start.4 = (bf16[512,2048]{1,0:T(8,128)(2,1)}, bf16[512,2048]{1,0:T(8,128)(2,1)}, u32[]{:S(2)}, u32[]{:S(2)}) collective-permute-start(bf16[512,2048]{1,0:T(8,128)(2,1)} %get-tuple-element.98), channel_id=1, source_target_pairs={{0,16},{1,9},{2,18},{3,11},{4,20},{5,13},{6,22},{7,15},{8,24},{9,1... | collective-permute-start | bytes 6291464 | tf_op jit(solution)/shard_map/ppermute | solution.py:1064
  280.6 26.4 %collective-permute-start.5 = (bf16[512,2048]{1,0:T(8,128)(2,1)}, bf16[512,2048]{1,0:T(8,128)(2,1)}, u32[]{:S(2)}, u32[]{:S(2)}) collective-permute-start(bf16[512,2048]{1,0:T(8,128)(2,1)} %get-tuple-element.99.refs_4_), channel_id=1, source_target_pairs={{0,16},{1,9},{2,18},{3,11},{4,20},{5,13},{6,22},{7,15},{8,24},{9,1... | collective-permute-start | bytes 6291464 | tf_op jit(solution)/shard_map/ppermute | solution.py:1064
  315.5 98.5 %all-gather.13.cloned.1.call-start = ((), (), s32[]{:S(2)}) async-start(), calls=%async_computation.10 | async-start | bytes 4718592 | tf_op jit(solution)/shard_map/all_gather | solution.py:1296
  368.6 187.6 %reduce-scatter.10.cloned.1.call-start = ((), (), s32[]{:S(2)}) async-start(), calls=%async_computation.11 | async-start | bytes 4718592 | tf_op jit(solution)/shard_map/reduce_scatter | solution.py:1350
  422.2 26.2 %collective-permute-start.11 = (bf16[512,2048]{1,0:T(8,128)(2,1)S(1)}, bf16[512,2048]{1,0:T(8,128)(2,1)}, u32[]{:S(2)}, u32[]{:S(2)}) collective-permute-start(bf16[512,2048]{1,0:T(8,128)(2,1)S(1)} %get-tuple-element.109), channel_id=1, source_target_pairs={{0,16},{1,9},{2,18},{3,11},{4,20},{5,13},{6,22},{7,15},{8,24},{9,1... | collective-permute-start | bytes 6291464 | tf_op jit(solution)/shard_map/ppermute | solution.py:1064
  469.6 26.4 %collective-permute-start.12 = (bf16[512,2048]{1,0:T(8,128)(2,1)}, bf16[512,2048]{1,0:T(8,128)(2,1)}, u32[]{:S(2)}, u32[]{:S(2)}) collective-permute-start(bf16[512,2048]{1,0:T(8,128)(2,1)} %get-tuple-element.112.refs_4_), channel_id=1, source_target_pairs={{0,16},{1,9},{2,18},{3,11},{4,20},{5,13},{6,22},{7,15},{8,24},{9,1... | collective-permute-start | bytes 6291464 | tf_op jit(solution)/shard_map/ppermute | solution.py:1064
  505.9 104.1 %all-gather.15.cloned.1.call-start = ((), (), s32[]{:S(2)}) async-start(), calls=%async_computation.12 | async-start | bytes 4718592 | tf_op jit(solution)/shard_map/all_gather | solution.py:1383
  505.9 40.7 %collective-permute-start.14 = (bf16[512,1408]{1,0:T(8,128)(2,1)}, bf16[512,1408]{1,0:T(8,128)(2,1)}, u32[]{:S(2)}, u32[]{:S(2)}) collective-permute-start(bf16[512,1408]{1,0:T(8,128)(2,1)} %get-tuple-element.119), channel_id=1, source_target_pairs={{0,8},{1,17},{2,10},{3,19},{4,12},{5,21},{6,14},{7,23},{8,0},{9,25... | collective-permute-start | bytes 4325384 | tf_op jit(solution)/shard_map/ppermute | solution.py:1064
  507.4 39.2 %collective-permute-start.13 = (bf16[512,1408]{1,0:T(8,128)(2,1)}, bf16[512,1408]{1,0:T(8,128)(2,1)}, u32[]{:S(2)}, u32[]{:S(2)}) collective-permute-start(bf16[512,1408]{1,0:T(8,128)(2,1)} %get-tuple-element.118), channel_id=1, source_target_pairs={{0,8},{1,17},{2,10},{3,19},{4,12},{5,21},{6,14},{7,23},{8,0},{9,25... | collective-permute-start | bytes 4325384 | tf_op jit(solution)/shard_map/ppermute | solution.py:1064
  532.3 23.9 %collective-permute-start.15 = (bf16[512,1408]{1,0:T(8,128)(2,1)}, bf16[512,1408]{1,0:T(8,128)(2,1)}, u32[]{:S(2)}, u32[]{:S(2)}) collective-permute-start(bf16[512,1408]{1,0:T(8,128)(2,1)} %get-tuple-element.124), channel_id=1, source_target_pairs={{0,8},{1,17},{2,10},{3,19},{4,12},{5,21},{6,14},{7,23},{8,0},{9,25... | collective-permute-start | bytes 4325384 | tf_op jit(solution)/shard_map/ppermute | solution.py:1064
  559.6 122.3 %reduce-scatter.14.cloned.1.call-start = ((), (), s32[]{:S(2)}) async-start(), calls=%async_computation.14 | async-start | bytes 2949120 | tf_op jit(solution)/shard_map/reduce_scatter | solution.py:1398
  559.7 19.4 %collective-permute-start.17 = (bf16[512,1408]{1,0:T(8,128)(2,1)}, bf16[512,1408]{1,0:T(8,128)(2,1)}, u32[]{:S(2)}, u32[]{:S(2)}) collective-permute-start(bf16[512,1408]{1,0:T(8,128)(2,1)} %get-tuple-element.132), channel_id=1, source_target_pairs={{0,8},{1,17},{2,10},{3,19},{4,12},{5,21},{6,14},{7,23},{8,0},{9,25... | collective-permute-start | bytes 4325384 | tf_op jit(solution)/shard_map/ppermute | solution.py:1064
  561.1 33.4 %collective-permute-start.18 = (bf16[512,1408]{1,0:T(8,128)(2,1)}, bf16[512,1408]{1,0:T(8,128)(2,1)}, u32[]{:S(2)}, u32[]{:S(2)}) collective-permute-start(bf16[512,1408]{1,0:T(8,128)(2,1)} %get-tuple-element.133), channel_id=1, source_target_pairs={{0,8},{1,17},{2,10},{3,19},{4,12},{5,21},{6,14},{7,23},{8,0},{9,25... | collective-permute-start | bytes 4325384 | tf_op jit(solution)/shard_map/ppermute | solution.py:1064
  561.8 48.2 %collective-permute-start.16 = (bf16[512,1408]{1,0:T(8,128)(2,1)}, bf16[512,1408]{1,0:T(8,128)(2,1)}, u32[]{:S(2)}, u32[]{:S(2)}) collective-permute-start(bf16[512,1408]{1,0:T(8,128)(2,1)} %get-tuple-element.131), channel_id=1, source_target_pairs={{0,8},{1,17},{2,10},{3,19},{4,12},{5,21},{6,14},{7,23},{8,0},{9,25... | collective-permute-start | bytes 4325384 | tf_op jit(solution)/shard_map/ppermute | solution.py:1064
  563.2 74.8 %collective-permute-start.20 = (bf16[512,1152]{1,0:T(8,128)(2,1)}, bf16[512,1152]{1,0:T(8,128)(2,1)}, u32[]{:S(2)}, u32[]{:S(2)}) collective-permute-start(bf16[512,1152]{1,0:T(8,128)(2,1)} %get-tuple-element.140), channel_id=1, source_target_pairs={{0,8},{1,17},{2,10},{3,19},{4,12},{5,21},{6,14},{7,23},{8,0},{9,25... | collective-permute-start | bytes 3538952 | tf_op jit(solution)/shard_map/ppermute | solution.py:1064
  563.8 74.2 %collective-permute-start.19 = (bf16[512,1152]{1,0:T(8,128)(2,1)}, bf16[512,1152]{1,0:T(8,128)(2,1)}, u32[]{:S(2)}, u32[]{:S(2)}) collective-permute-start(bf16[512,1152]{1,0:T(8,128)(2,1)} %get-tuple-element.139), channel_id=1, source_target_pairs={{0,8},{1,17},{2,10},{3,19},{4,12},{5,21},{6,14},{7,23},{8,0},{9,25... | collective-permute-start | bytes 3538952 | tf_op jit(solution)/shard_map/ppermute | solution.py:1064
  643.2 140.9 %reduce-scatter.12.cloned.1.call-start = ((), (), s32[]{:S(2)}) async-start(), calls=%async_computation.13 | async-start | bytes 4718592 | tf_op jit(solution)/shard_map/reduce_scatter | solution.py:1406
  643.8 192.3 %all-gather.17.cloned.1.call-start = ((), (), s32[]{:S(2)}) async-start(), calls=%async_computation.15 | async-start | bytes 2654208 | tf_op jit(solution)/shard_map/all_gather | solution.py:1469
  647.1 20.5 %collective-permute-start.21 = (bf16[512,1408]{1,0:T(8,128)(2,1)}, bf16[512,1408]{1,0:T(8,128)(2,1)}, u32[]{:S(2)}, u32[]{:S(2)}) collective-permute-start(bf16[512,1408]{1,0:T(8,128)(2,1)} %fusion.8), channel_id=1, source_target_pairs={{0,16},{1,9},{2,18},{3,11},{4,20},{5,13},{6,22},{7,15},{8,24},{9,1... | collective-permute-start | bytes 4325384 | tf_op jit(solution)/shard_map/ppermute | solution.py:1064
  653.5 28.4 %collective-permute-start.22 = (bf16[512,1408]{1,0:T(8,128)(2,1)}, bf16[512,1408]{1,0:T(8,128)(2,1)}, u32[]{:S(2)}, u32[]{:S(2)}) collective-permute-start(bf16[512,1408]{1,0:T(8,128)(2,1)} %get-tuple-element.233), channel_id=1, source_target_pairs={{0,16},{1,9},{2,18},{3,11},{4,20},{5,13},{6,22},{7,15},{8,24},{9,1... | collective-permute-start | bytes 4325384 | tf_op jit(solution)/shard_map/ppermute | solution.py:1064
  654.2 87.6 %collective-permute-start.28 = (bf16[512,1408]{1,0:T(8,128)(2,1)}, bf16[512,1408]{1,0:T(8,128)(2,1)}, u32[]{:S(2)}, u32[]{:S(2)}) collective-permute-start(bf16[512,1408]{1,0:T(8,128)(2,1)} %get-tuple-element.232), channel_id=1, source_target_pairs={{0,16},{1,9},{2,18},{3,11},{4,20},{5,13},{6,22},{7,15},{8,24},{9,1... | collective-permute-start | bytes 4325384 | tf_op jit(solution)/shard_map/ppermute | solution.py:1064
  683.6 9.2 %collective-permute-start.23 = (bf16[128,640]{1,0:T(8,128)(2,1)}, bf16[128,640]{1,0:T(8,128)(2,1)S(1)}, u32[]{:S(2)}, u32[]{:S(2)}) collective-permute-start(bf16[128,640]{1,0:T(8,128)(2,1)} %first_block.3), channel_id=1, source_target_pairs={{8,0},{16,8},{24,16},{9,1},{17,9},{25,17},{10,2},{18,10},{26,18},{... | collective-permute-start | bytes 491528 | tf_op jit(solution)/shard_map/ppermute | solution.py:1427
  695.6 14.4 %collective-permute-start.24 = (bf16[128,640]{1,0:T(8,128)(2,1)}, bf16[128,640]{1,0:T(8,128)(2,1)S(1)}, u32[]{:S(2)}, u32[]{:S(2)}) collective-permute-start(bf16[128,640]{1,0:T(8,128)(2,1)} %get-tuple-element.144.refs_0_.projected), channel_id=1, source_target_pairs={{0,2},{1,3},{2,0},{3,1},{4,6},{5,7},{6,4},{7,5},{8,10},{9,11},{10,... | collective-permute-start | bytes 491528 | tf_op jit(solution)/shard_map/ppermute | solution.py:1108
  695.6 14.4 %collective-permute-start.25 = (bf16[128,640]{1,0:T(8,128)(2,1)}, bf16[128,640]{1,0:T(8,128)(2,1)S(1)}, u32[]{:S(2)}, u32[]{:S(2)}) collective-permute-start(bf16[128,640]{1,0:T(8,128)(2,1)} %get-tuple-element.144.refs_0_.projected), channel_id=1, source_target_pairs={{0,4},{1,5},{2,6},{3,7},{4,0},{5,1},{6,2},{7,3},{8,12},{9,13},{10,... | collective-permute-start | bytes 491528 | tf_op jit(solution)/shard_map/ppermute | solution.py:1108
  697.3 22.5 %collective-permute-start.26 = (bf16[128,640]{1,0:T(8,128)(2,1)}, bf16[128,640]{1,0:T(8,128)(2,1)S(1)}, u32[]{:S(2)}, u32[]{:S(2)}) collective-permute-start(bf16[128,640]{1,0:T(8,128)(2,1)} %get-tuple-element.144.refs_0_.projected), channel_id=1, source_target_pairs={{0,6},{1,7},{2,4},{3,5},{4,2},{5,3},{6,0},{7,1},{8,14},{9,15},{10,... | collective-permute-start | bytes 491528 | tf_op jit(solution)/shard_map/ppermute | solution.py:1108
  721.7 27.5 %collective-permute-start.27 = (bf16[512,640]{1,0:T(8,128)(2,1)}, bf16[512,640]{1,0:T(8,128)(2,1)}, u32[]{:S(2)}, u32[]{:S(2)}) collective-permute-start(bf16[512,640]{1,0:T(8,128)(2,1)} %pad_maximum_fusion.1), channel_id=1, source_target_pairs={{0,1},{1,0},{2,3},{3,2},{4,5},{5,4},{6,7},{7,6},{8,9},{9,8},{10,11... | collective-permute-start | bytes 1966088 | tf_op jit(solution)/shard_map/ppermute | solution.py:1109
  725.7 26.9 %collective-permute-start.29 = (bf16[512,640]{1,0:T(8,128)(2,1)}, bf16[512,640]{1,0:T(8,128)(2,1)S(1)}, u32[]{:S(2)}, u32[]{:S(2)}) collective-permute-start(bf16[512,640]{1,0:T(8,128)(2,1)} %get-tuple-element.146), channel_id=1, source_target_pairs={{0,8},{1,17},{2,10},{3,19},{4,12},{5,21},{6,14},{7,23},{8,0},{9,25... | collective-permute-start | bytes 1966088 | tf_op jit(solution)/shard_map/ppermute | solution.py:1064
  727.9 25.7 %collective-permute-start.30 = (bf16[512,640]{1,0:T(8,128)(2,1)}, bf16[512,640]{1,0:T(8,128)(2,1)}, u32[]{:S(2)}, u32[]{:S(2)}) collective-permute-start(bf16[512,640]{1,0:T(8,128)(2,1)} %get-tuple-element.147), channel_id=1, source_target_pairs={{0,8},{1,17},{2,10},{3,19},{4,12},{5,21},{6,14},{7,23},{8,0},{9,25... | collective-permute-start | bytes 1966088 | tf_op jit(solution)/shard_map/ppermute | solution.py:1064
  760.1 7.0 collective-permute-start.31
  769.0 7.3 collective-permute-start.32
  781.4 30.6 %collective-permute-start.42 = (bf16[512,1152]{1,0:T(8,128)(2,1)}, bf16[512,1152]{1,0:T(8,128)(2,1)}, u32[]{:S(2)}, u32[]{:S(2)}) collective-permute-start(bf16[512,1152]{1,0:T(8,128)(2,1)} %fusion.9), channel_id=1, source_target_pairs={{0,16},{1,9},{2,18},{3,11},{4,20},{5,13},{6,22},{7,15},{8,24},{9,1... | collective-permute-start | bytes 3538952 | tf_op jit(solution)/shard_map/ppermute | solution.py:1064
  791.5 17.8 %collective-permute-start.34 = (f32[300,128]{1,0:T(8,128)S(1)}, f32[300,128]{1,0:T(8,128)S(1)}, u32[]{:S(2)}, u32[]{:S(2)}) collective-permute-start(f32[300,128]{1,0:T(8,128)S(1)} %bitcast_add_fusion), channel_id=1, source_target_pairs={{0,2},{1,3},{2,0},{3,1},{4,6},{5,7},{6,4},{7,5},{8,10},{9,11},{10,... | collective-permute-start | bytes 460808 | tf_op jit(solution)/shard_map/ppermute | solution.py:1132
  797.5 17.9 %collective-permute-start.38 = (bf16[512,640]{1,0:T(8,128)(2,1)S(1)}, bf16[512,640]{1,0:T(8,128)(2,1)S(1)}, u32[]{:S(2)}, u32[]{:S(2)}) collective-permute-start(bf16[512,640]{1,0:T(8,128)(2,1)S(1)} %fusion.10), channel_id=1, source_target_pairs={{0,16},{1,9},{2,18},{3,11},{4,20},{5,13},{6,22},{7,15},{8,24},{9,1... | collective-permute-start | bytes 1966088 | tf_op jit(solution)/shard_map/ppermute | solution.py:1064
  798.6 11.4 %collective-permute-start.40 = (bf16[128,512]{1,0:T(8,128)(2,1)S(1)}, bf16[128,512]{1,0:T(8,128)(2,1)S(1)}, u32[]{:S(2)}, u32[]{:S(2)}) collective-permute-start(bf16[128,512]{1,0:T(8,128)(2,1)S(1)} %get-tuple-element.253), channel_id=1, source_target_pairs={{0,8},{1,17},{2,10},{3,19},{4,12},{5,21},{6,14},{7,23},{8,0},{9,25... | collective-permute-start | bytes 393224 | tf_op jit(solution)/shard_map/ppermute | solution.py:1064
  800.5 16.0 %collective-permute-start.39 = (bf16[128,512]{1,0:T(8,128)(2,1)S(1)}, bf16[128,512]{1,0:T(8,128)(2,1)S(1)}, u32[]{:S(2)}, u32[]{:S(2)}) collective-permute-start(bf16[128,512]{1,0:T(8,128)(2,1)S(1)} %get-tuple-element.252), channel_id=1, source_target_pairs={{0,8},{1,17},{2,10},{3,19},{4,12},{5,21},{6,14},{7,23},{8,0},{9,25... | collective-permute-start | bytes 393224 | tf_op jit(solution)/shard_map/ppermute | solution.py:1064
  809.4 11.8 %collective-permute-start.35 = (f32[300,128]{1,0:T(8,128)S(1)}, f32[300,128]{1,0:T(8,128)S(1)}, u32[]{:S(2)}, u32[]{:S(2)}) collective-permute-start(f32[300,128]{1,0:T(8,128)S(1)} %fusion.69), channel_id=1, source_target_pairs={{0,4},{1,5},{2,6},{3,7},{4,0},{5,1},{6,2},{7,3},{8,12},{9,13},{10,... | collective-permute-start | bytes 460808 | tf_op jit(solution)/shard_map/ppermute | solution.py:1132
  810.1 6.4 collective-permute-start.41
  821.1 5.9 collective-permute-start.36
  827.1 5.3 collective-permute-start.37
  (92 other events, 700.2 us)
Sparse Core Ops, SparseCore 0:
  11.0 49.8 all-gather.6
  62.6 36.5 all-gather.8
  124.8 50.6 reduce-scatter.5
  178.6 46.2 all-gather.10
  315.6 49.1 reduce-scatter.7
  368.7 45.2 all-gather.12
  506.0 48.6 reduce-scatter.9
  559.7 45.8 all-gather.14
  643.3 36.1 reduce-scatter.13
  682.2 59.6 reduce-scatter.11
  778.4 38.1 all-gather.16

commit v3 on v2

--- a/solution.py
+++ b/solution.py
@@ -20,6 +20,7 @@
 score_scale = (NOPE + ROPE) ** (-0.5)
 bf16 = jnp.bfloat16
 f32 = jnp.float32
+whole_vmem = pltpu.CompilerParams(vmem_limit_bytes=60 * 1024 * 1024)
 small_cost = pl.CostEstimate(flops=1, bytes_accessed=1, transcendentals=0)
 
 
@@ -64,35 +65,27 @@
 def allowed_keys(low, block, span):
     row = lax.broadcasted_iota(jnp.int32, (block, span), 0)
     col = lax.broadcasted_iota(jnp.int32, (block, span), 1)
-    return (col <= row + WINDOW) & (col >= low)
-
-
-def read_chunks(refs, first, last):
-    return jnp.concatenate([ref[:, first:last] for ref in refs], axis=0)
-
-
-def head_parts(query, lanes, kv, rope, head):
+    return (col <= row + WINDOW) & (col >= low[:, :1])
+
+
+def head_parts(query, lanes, keys, head):
     turned = jnp.where(lanes, query[:, 2 * NOPE :], 0)
     query_head = jnp.concatenate([query[:, head * NOPE : (head + 1) * NOPE], turned], axis=1)
     base = head * (NOPE + VDIM)
-    key_head = jnp.concatenate([read_chunks(kv, base, base + NOPE), rope], axis=1)
-    return (query_head, key_head, read_chunks(kv, base + NOPE, base + NOPE + VDIM))
-
-
-def attend_kernel(chunks, normed, cosine, sine, low, query_w, out_w, *refs):
-    kv, key_rope = refs[:chunks], refs[chunks : 2 * chunks]
-    query_out, mixed_out, log_out, part_out = refs[-4:]
-    block = normed.shape[0]
-    proj = dot_plain(normed[...], query_w[...])
-    turned = proj[:, 2 * NOPE :]
-    turned = turn(turned, cosine[...], sine[...])
-    query = jnp.concatenate([proj[:, : 2 * NOPE], turned], axis=1).astype(bf16)
-    query_out[...] = query
+    rope = keys[:, 2 * (NOPE + VDIM) :]
+    key_head = jnp.concatenate([keys[:, base : base + NOPE], rope], axis=1)
+    return (query_head, key_head, keys[:, base + NOPE : base + NOPE + VDIM])
+
+
+def attend_kernel(chunks, query_in, low, out_w, *refs):
+    mixed_out, log_out, part_out = refs[-3:]
+    keys = window_keys(refs, chunks)
+    block = query_in.shape[0]
+    query = query_in[...]
     mask = allowed_keys(low[...], block, WINDOW + block)
-    rope = read_chunks(key_rope, 0, 2 * ROPE)
     mixed, logs = [], []
     for head in range(2):
-        query_head, key_head, value_head = head_parts(query, head_lanes(block, head), kv, rope, head)
+        query_head, key_head, value_head = head_parts(query, head_lanes(block, head), keys, head)
         scores = jnp.where(mask, dot_right_t(query_head, key_head) * score_scale, masked_value)
         top = jnp.max(scores, axis=1, keepdims=True)
         raised = jnp.exp(scores - top)
@@ -128,23 +121,24 @@
 
 
 def own_keys_kernel(normed, cosine, sine, gain, compress, expand, *refs):
-    kv, key_rope, latent = refs[-3:]
+    keys, latent = refs[-2:]
     projected = dot_right_t(normed[...], compress[...])
     unit, _ = normalize(projected[:, :LATENT])
     low = (unit * gain[...]).astype(bf16)
     latent[...] = low
-    kv[...] = dot_plain(low, expand[...]).astype(bf16)
-    key_rope[...] = turn(projected[:, LATENT:], cosine[...], sine[...]).astype(bf16)
+    kv_cols = expand.shape[1]
+    keys[:, :kv_cols] = dot_plain(low, expand[...]).astype(bf16)
+    keys[:, kv_cols:] = turn(projected[:, LATENT:], cosine[...], sine[...]).astype(bf16)
 
 
 def own_keys(normed, cosine, sine, gain, compress, expand, after):
     rows, width = normed.shape
     block = QUERY_BLOCK
-    blocks = rows // block
-    kv_cols, rope_cols = expand.shape[1], 2 * ROPE
+    rope_cols = 2 * ROPE
+    key_cols = expand.shape[1] + rope_cols
     return pl.pallas_call(
         own_keys_kernel,
-        grid=(blocks,),
+        grid=(rows // block,),
         in_specs=[
             by_rows(block, width),
             by_rows(block, rope_cols),
@@ -154,81 +148,105 @@
             whole(expand.shape),
         ]
         + unread(after),
-        out_specs=[
-            by_rows(block, kv_cols, blocks),
-            by_rows(block, rope_cols, blocks),
-            by_rows(block, LATENT),
-        ],
+        out_specs=[by_rows(block, key_cols), by_rows(block, LATENT)],
         out_shape=[
-            jax.ShapeDtypeStruct((2 * rows, kv_cols), bf16),
-            jax.ShapeDtypeStruct((2 * rows, rope_cols), bf16),
+            jax.ShapeDtypeStruct((rows, key_cols), bf16),
             jax.ShapeDtypeStruct((rows, LATENT), bf16),
         ],
-        compiler_params=pltpu.CompilerParams(vmem_limit_bytes=40 * 1024 * 1024),
+        compiler_params=whole_vmem,
         cost_estimate=small_cost,
         name="own_keys",
     )(normed, cosine, sine, gain[None], compress, expand, *after)
 
 
-def past_keys_kernel(previous, expand, kv_in, rope_in, kv, key_rope):
-    kv[...] = dot_plain(previous[:, :LATENT], expand[...]).astype(bf16)
-    key_rope[...] = previous[:, LATENT:]
-
-
-def past_keys(previous, expand, kv, key_rope):
-    block = QUERY_BLOCK
-    return pl.pallas_call(
-        past_keys_kernel,
-        grid=(previous.shape[0] // block,),
-        in_specs=[by_rows(block, previous.shape[1]), whole(expand.shape)] + unread([kv, key_rope]),
-        out_specs=[by_rows(block, kv.shape[1]), by_rows(block, key_rope.shape[1])],
-        out_shape=[
-            jax.ShapeDtypeStruct(kv.shape, bf16),
-            jax.ShapeDtypeStruct(key_rope.shape, bf16),
-        ],
-        input_output_aliases={2: 0, 3: 1},
-        cost_estimate=small_cost,
-        name="past_keys",
-    )(previous, expand, kv, key_rope)
-
-
-def attend(normed, cosine, sine, low, query_w, kv, key_rope, out_w, after):
-    rows, width = normed.shape
+def key_blocks(keys, past, block, chunks):
+    cols = keys.shape[1]
+    blocks = past.shape[0] // block
+    specs, operands = [], []
+    for chunk in range(chunks):
+        if chunk < chunks - 1:
+            specs.append(
+                pl.BlockSpec((block, cols), lambda i, c=chunk: (jnp.minimum(i + c, blocks - 1), 0))
+            )
+            operands.append(past)
+        if chunk > 0:
+            specs.append(
+                pl.BlockSpec((block, cols), lambda i, c=chunk: (jnp.maximum(i + c - blocks, 0), 0))
+            )
+            operands.append(keys)
+    return specs, operands
+
+
+def window_keys(refs, chunks):
+    step = pl.program_id(0)
+    parts = [refs[0][...]]
+    for chunk in range(1, chunks - 1):
+        past, own = refs[2 * chunk - 1], refs[2 * chunk]
+        parts.append(jnp.where(step + chunk < chunks - 1, past[...], own[...]))
+    parts.append(refs[2 * chunks - 3][...])
+    return jnp.concatenate(parts, axis=0)
+
+
+def attend(query, low, keys, past, out_w, after):
+    rows, query_cols = query.shape
+    width = out_w.shape[1]
     block = QUERY_BLOCK
     chunks = 1 + WINDOW // block
-    query_cols = query_w.shape[1]
     rows_of = functools.partial(by_rows, block)
+    key_specs, key_operands = key_blocks(keys, past, block, chunks)
     return pl.pallas_call(
         functools.partial(attend_kernel, chunks),
         grid=(rows // block,),
         in_specs=[
-            rows_of(width),
-            rows_of(2 * ROPE),
-            rows_of(2 * ROPE),
-            rows_of(1),
-            whole(query_w.shape),
+            rows_of(query_cols),
+            rows_of(low.shape[1]),
             whole(out_w.shape),
         ]
-        + [rows_of(kv.shape[1], chunk) for chunk in range(chunks)]
-        + [rows_of(key_rope.shape[1], chunk) for chunk in range(chunks)]
+        + key_specs
         + unread(after),
-        out_specs=[rows_of(query_cols), rows_of(2 * VDIM), rows_of(128), rows_of(width)],
+        out_specs=[rows_of(2 * VDIM), rows_of(128), rows_of(width)],
         out_shape=[
-            jax.ShapeDtypeStruct((rows, query_cols), bf16),
             jax.ShapeDtypeStruct((rows, 2 * VDIM), bf16),
             jax.ShapeDtypeStruct((rows, 128), f32),
             jax.ShapeDtypeStruct((rows, width), bf16),
         ],
-        compiler_params=pltpu.CompilerParams(vmem_limit_bytes=50 * 1024 * 1024),
+        compiler_params=whole_vmem,
         cost_estimate=small_cost,
         name="attend",
-    )(normed, cosine, sine, low, query_w, out_w, *([kv] * chunks), *([key_rope] * chunks), *after)
+    )(query, low, out_w, *key_operands, *after)
+
+
+def query_kernel(normed, cosine, sine, query_w, out):
+    proj = dot_plain(normed[...], query_w[...])
+    out[:, : 2 * NOPE] = proj[:, : 2 * NOPE].astype(bf16)
+    out[:, 2 * NOPE :] = turn(proj[:, 2 * NOPE :], cosine[...], sine[...]).astype(bf16)
+
+
+def project_query(normed, cosine, sine, query_w):
+    rows, width = normed.shape
+    block = QUERY_BLOCK
+    cols = query_w.shape[1]
+    return pl.pallas_call(
+        query_kernel,
+        grid=(rows // block,),
+        in_specs=[
+            by_rows(block, width),
+            by_rows(block, 2 * ROPE),
+            by_rows(block, 2 * ROPE),
+            whole(query_w.shape),
+        ],
+        out_specs=by_rows(block, cols),
+        out_shape=jax.ShapeDtypeStruct((rows, cols), bf16),
+        compiler_params=whole_vmem,
+        cost_estimate=small_cost,
+        name="project_query",
+    )(normed, cosine, sine, query_w)
 
 
 def attend_back_kernel(
     chunks, grad, query_in, logs, cosine, sine, low, query_w, out_w, *refs
 ):
-    kv, key_rope = refs[:chunks], refs[chunks : 2 * chunks]
+    keys = window_keys(refs, chunks)
     query_grad_out, part_out, kv_past, rope_past, kv_own, rope_own, kv_sum, rope_sum = refs[-8:]
     block = grad.shape[0]
 
@@ -249,12 +267,11 @@
 
     mixed_grad = dot_right_t(grad[...], out_w[...]).astype(bf16)
     mask = allowed_keys(low[...], block, WINDOW + block)
-    rope = read_chunks(key_rope, 0, 2 * ROPE)
     query = query_in[...]
     plain, turned, rope_piece = [], 0.0, 0.0
     for head in range(2):
         lanes = head_lanes(block, head)
-        query_head, key_head, value_head = head_parts(query, lanes, kv, rope, head)
+        query_head, key_head, value_head = head_parts(query, lanes, keys, head)
         base = head * (NOPE + VDIM)
         grad_head = mixed_grad[:, head * VDIM : (head + 1) * VDIM]
         scores = jnp.where(mask, dot_right_t(query_head, key_head) * score_scale, masked_value)
@@ -282,13 +299,15 @@
         rope_own[...] = rope_sum[...].astype(bf16)
 
 
-def attend_back(grad, query, logs, cosine, sine, low, query_w, kv, key_rope, out_w, after):
+def attend_back(grad, query, logs, cosine, sine, low, query_w, keys, past, out_w, after):
     rows, width = grad.shape
     block = QUERY_BLOCK
     chunks = 1 + WINDOW // block
     query_cols = query_w.shape[1]
     rows_of = functools.partial(by_rows, block)
-    kv_cols, rope_cols = kv.shape[1], key_rope.shape[1]
+    rope_cols = 2 * ROPE
+    kv_cols = keys.shape[1] - rope_cols
+    key_specs, key_operands = key_blocks(keys, past, block, chunks)
     return pl.pallas_call(
         functools.partial(attend_back_kernel, chunks),
         grid=(rows // block,),
@@ -298,12 +317,11 @@
             rows_of(128),
             rows_of(2 * ROPE),
             rows_of(2 * ROPE),
-            rows_of(1),
+            rows_of(low.shape[1]),
             whole(query_w.shape),
             whole(out_w.shape),
         ]
-        + [rows_of(kv_cols, chunk) for chunk in range(chunks)]
-        + [rows_of(rope_cols, chunk) for chunk in range(chunks)]
+        + key_specs
         + unread(after),
         out_specs=[
             rows_of(query_cols),
@@ -322,7 +340,7 @@
             jax.ShapeDtypeStruct((WINDOW, rope_cols), bf16),
         ],
         scratch_shapes=[pltpu.VMEM((WINDOW, kv_cols), f32), pltpu.VMEM((WINDOW, rope_cols), f32)],
-        compiler_params=pltpu.CompilerParams(vmem_limit_bytes=50 * 1024 * 1024),
+        compiler_params=whole_vmem,
         cost_estimate=small_cost,
         name="attend_back",
     )(
@@ -334,8 +352,7 @@
         low,
         query_w,
         out_w,
-        *([kv] * chunks),
-        *([key_rope] * chunks),
+        *key_operands,
         *after,
     )
 
@@ -365,6 +382,7 @@
             jax.ShapeDtypeStruct((rows, width), bf16),
         ],
         cost_estimate=small_cost,
+        compiler_params=whole_vmem,
         name="norm",
     )(tokens, attention, gain[None], *after)
 
@@ -392,118 +410,132 @@
             jax.ShapeDtypeStruct((1, width), f32),
         ],
         cost_estimate=small_cost,
+        compiler_params=whole_vmem,
         name="norm_back",
     )(branch_grad, grad_out, unit, factor, gain[None], *after)
 
 
-def load_all(step, pairs):
-    @pl.when(step == 0)
-    def start():
-        for source, target, semaphore in pairs:
-            pltpu.make_async_copy(source, target, semaphore).start()
-
-
-def wait_for(pairs):
-    for source, target, semaphore in pairs:
-        pltpu.make_async_copy(source, target, semaphore).wait()
-
-
-def expert_kernel(count, extra, places, slot_in, *refs):
-    act_out, slope_out, inner_out, out, held, gate_sum, up_sum, semaphores = refs[count + extra :]
-    step = pl.program_id(0)
-    order = [(ref, item) for ref in refs[:count] for item in (0, 1)]
-    order += [(ref, 2) for ref in refs[:count]]
-    pairs = [
-        (ref.at[item], held.at[index], semaphores.at[index])
-        for index, (ref, item) in enumerate(order)
-    ]
-    load_all(step, pairs)
+def column_tiles(hidden):
+    return [(first, min(first + 512, hidden)) for first in range(0, hidden, 512)]
+
+
+class Copies:
+    def __init__(self, semaphores):
+        self.semaphores = semaphores
+        self.groups = {}
+        self.used = 0
+
+    def start(self, group, source, target):
+        copy = pltpu.make_async_copy(source, target, self.semaphores.at[self.used])
+        self.used += 1
+        copy.start()
+        self.groups.setdefault(group, []).append(copy)
+
+    def wait(self, group):
+        for copy in self.groups.pop(group):
+            copy.wait()
+
+
+def merged(ref, cols):
+    value = ref[:, :, cols]
+    return value.reshape(-1, value.shape[-1])
+
+
+def expert_kernel(count, extra, row, places, slot_in, *refs):
+    weights = refs[:count]
+    outs = refs[count + extra : count + extra + 4]
+    act_s, slope_s, inner_s, result, gate_w, up_w, down_w, semaphores = refs[count + extra + 4 :]
+    depth, hidden = gate_w.shape[1:]
+    rows = pl.ds(row, slot_in.shape[0])
+    copies = Copies(semaphores)
+    for first, last in column_tiles(hidden):
+        cols = slice(first, last)
+        for index, weight in enumerate(weights):
+            place = places[index]
+            copies.start(first, weight.at[0, :, cols], gate_w.at[place, :, cols])
+            copies.start(first, weight.at[1, :, cols], up_w.at[place, :, cols])
+    for index, weight in enumerate(weights):
+        copies.start("down", weight.at[2], down_w.at[places[index]])
+    for first, last in column_tiles(hidden):
+        cols = slice(first, last)
+        copies.wait(first)
+        gate = dot_plain(slot_in[...], merged(gate_w, cols))
+        up = dot_plain(slot_in[...], merged(up_w, cols))
+        act, slope = silu_parts(gate)
+        act_s[:, cols] = act.astype(bf16)
+        slope_s[:, cols] = (up * slope).astype(bf16)
+        inner_s[:, cols] = (act * up).astype(bf16)
+        for source, target in zip((act_s, slope_s, inner_s), outs):
+            copies.start("out", source.at[:, cols], target.at[rows, cols])
+    copies.wait("down")
     for index in range(count):
-
-        @pl.when(step == index)
-        def add(index=index):
-            wait_for(pairs[2 * index : 2 * index + 2])
-            gate = dot_plain(slot_in[...], held[2 * index])
-            up = dot_plain(slot_in[...], held[2 * index + 1])
-            if index > 0:
-                gate = gate + gate_sum[...]
-                up = up + up_sum[...]
-            if index < count - 1:
-                gate_sum[...] = gate
-                up_sum[...] = up
-            else:
-                act, slope = silu_parts(gate)
-                act_out[...] = act.astype(bf16)
-                slope_out[...] = (up * slope).astype(bf16)
-                inner_out[...] = (act * up).astype(bf16)
-
-        @pl.when(step == count + index)
-        def down(index=index):
-            wait_for(pairs[2 * count + index : 2 * count + index + 1])
-            out[...] = dot_right_t(inner_out[...], held[2 * count + index]).astype(bf16)
-
-
-def expert_back_kernel(count, extra, places, out_grad, act, slope, *refs):
-    gate_out, up_out, in_grad, held, inner_sum, semaphores = refs[count + extra :]
-    step = pl.program_id(0)
-    order = [(ref, 2) for ref in refs[:count]]
-    order += [(ref, item) for ref in refs[:count] for item in (0, 1)]
-    pairs = [
-        (ref.at[item], held.at[index], semaphores.at[index])
-        for index, (ref, item) in enumerate(order)
-    ]
-    load_all(step, pairs)
+        cols = slice(index * depth, (index + 1) * depth)
+        result[:, cols] = dot_right_t(inner_s[...], down_w[index]).astype(bf16)
+        copies.start("out", result.at[:, cols], outs[3].at[:, cols])
+    copies.wait("out")
+
+
+def expert_back_kernel(count, extra, row, places, out_grad, act, slope, *refs):
+    weights = refs[:count]
+    outs = refs[count + extra : count + extra + 3]
+    gate_s, up_s, result, gate_w, up_w, down_w, semaphores = refs[count + extra + 3 :]
+    depth, hidden = gate_w.shape[1:]
+    copies = Copies(semaphores)
+    for first, last in column_tiles(hidden):
+        cols = slice(first, last)
+        for index, weight in enumerate(weights):
+            copies.start(first, weight.at[2, :, cols], down_w.at[places[index], :, cols])
+    for index, weight in enumerate(weights):
+        copies.start("back", weight.at[0], gate_w.at[places[index]])
+        copies.start("back", weight.at[1], up_w.at[places[index]])
+    for first, last in column_tiles(hidden):
+        cols = slice(first, last)
+        copies.wait(first)
+        inner = dot_plain(out_grad[...], merged(down_w, cols))
+        gate_s[:, cols] = (inner * slope[:, cols].astype(f32)).astype(bf16)
+        up_s[:, cols] = (inner * act[:, cols].astype(f32)).astype(bf16)
+        for source, target in zip((gate_s, up_s), outs):
+            copies.start("out", source.at[:, cols], target.at[:, cols])
+    copies.wait("back")
     for index in range(count):
-
-        @pl.when(step == index)
-        def add(index=index):
-            wait_for(pairs[index : index + 1])
-            inner = dot_plain(out_grad[...], held[index])
-            if index > 0:
-                inner = inner + inner_sum[...]
-            if index < count - 1:
-                inner_sum[...] = inner
-            else:
-                gate_out[...] = (inner * slope[...].astype(f32)).astype(bf16)
-                up_out[...] = (inner * act[...].astype(f32)).astype(bf16)
-
-        @pl.when(step == count + index)
-        def back(index=index):
-            first = count + 2 * index
-            wait_for(pairs[first : first + 2])
-            in_grad[...] = (
-                dot_right_t(gate_out[...], held[first]) + dot_right_t(up_out[...], held[first + 1])
-            ).astype(bf16)
-
-
-def expert_call(kernel, name, places, slots, fixed, weights, outputs, sums, after):
+        cols = slice(index * depth, (index + 1) * depth)
+        result[:, cols] = (
+            dot_right_t(gate_s[...], gate_w[index]) + dot_right_t(up_s[...], up_w[index])
+        ).astype(bf16)
+        copies.start("out", result.at[:, cols], outs[2].at[:, cols])
+    copies.wait("out")
+
+
+def expert_call(kernel, name, places, slots, fixed, weights, outputs, after, row=0, total=0, held=()):
     count = len(weights)
     rows, width = slots.shape
     _, depth, hidden = weights[0].shape
-    inner = pl.BlockSpec((rows, hidden), lambda i, places: (0, 0))
-    return pl.pallas_call(
-        functools.partial(kernel, count, len(after)),
+    inputs = [slots] + fixed
+    tiles = len(column_tiles(hidden))
+    weight_s = pltpu.VMEM((count, depth, hidden), bf16)
+    scratch = [(rows, hidden)] * outputs + [(rows, width)]
+    shapes = [(total or rows, hidden)] * outputs + [(rows, width)]
+    first_held = 1 + len(inputs) + count + len(after)
+    return pl.pallas_call(
+        functools.partial(kernel, count, len(after) + len(held), row),
         grid_spec=pltpu.PrefetchScalarGridSpec(
             num_scalar_prefetch=1,
-            grid=(2 * count,),
-            in_specs=[
-                pl.BlockSpec((rows, depth), lambda i, places: (0, places[jnp.minimum(i, count - 1)]))
-            ]
-            + [inner] * len(fixed)
+            grid=(1,),
+            in_specs=[pl.BlockSpec(array.shape, lambda i, places: (0, 0)) for array in inputs]
             + unread(weights)
-            + unread(after),
-            out_specs=[inner] * outputs
-            + [pl.BlockSpec((rows, depth), lambda i, places: (0, places[jnp.maximum(i - count, 0)]))],
-            scratch_shapes=[pltpu.VMEM((3 * count, depth, hidden), bf16)]
-            + [pltpu.VMEM((rows, hidden), f32)] * sums
-            + [pltpu.SemaphoreType.DMA((3 * count,))],
+            + unread(after)
+            + unread(held),
+            out_specs=unread(shapes),
+            scratch_shapes=[pltpu.VMEM(shape, bf16) for shape in scratch]
+            + [weight_s] * 3
+            + [pltpu.SemaphoreType.DMA((count * (2 * tiles + 3) + 3 * tiles,))],
         ),
-        out_shape=[jax.ShapeDtypeStruct((rows, hidden), bf16)] * outputs
-        + [jax.ShapeDtypeStruct((rows, width), bf16)],
-        compiler_params=pltpu.CompilerParams(vmem_limit_bytes=56 * 1024 * 1024),
+        out_shape=[jax.ShapeDtypeStruct(shape, bf16) for shape in shapes],
+        input_output_aliases={first_held + index: index for index in range(len(held))},
+        compiler_params=whole_vmem,
         cost_estimate=small_cost,
         name=name,
-    )(places, slots, *fixed, *weights, *after)
+    )(places, *inputs, *weights, *after, *held)
 
 
 def weight_grad_kernel(count, plan, places, *refs):
@@ -514,8 +546,9 @@
         first = 0
         for terms in segments:
             grad = 0.0
-            for left, right in terms:
-                grad = grad + dot_left_t(refs[left][...], refs[right][...])
+            for left, right, row in terms:
+                rows = slice(row, row + refs[left].shape[0])
+                grad = grad + dot_left_t(refs[left][...], refs[right][rows])
             last = first + grad.shape[1]
             for index in range(count):
 
@@ -533,24 +566,32 @@
 def weight_grads(name, places, outputs, after=()):
     count = places.shape[0]
     lefts, rights = [], []
-    for segments in outputs:
-        for terms in segments:
-            for left, right in terms:
-                if not any(left is other for other in lefts):
-                    lefts.append(left)
-                rights.append(right)
-    plan, position, flops = [], len(lefts), 0
+
+    def number_of(array, held):
+        for number, other in enumerate(held):
+            if array is other:
+                return number
+        held.append(array)
+        return len(held) - 1
+
+    plan, flops = [], 0
     for segments in outputs:
         planned, columns = [], 0
         for terms in segments:
             numbers = []
-            for left, right in terms:
-                numbers.append(([left is other for other in lefts].index(True), position))
-                position += 1
-                flops += 2 * left.shape[0] * left.shape[1] * right.shape[1]
+            for blocks, right in terms:
+                row = 0
+                for left in blocks if isinstance(blocks, list) else [blocks]:
+                    numbers.append((number_of(left, lefts), number_of(right, rights), row))
+                    row += left.shape[0]
+                flops += 2 * row * left.shape[1] * right.shape[1]
             planned.append(numbers)
             columns += terms[0][1].shape[1]
         plan.append(planned)
+    plan = [
+        [[(left, len(lefts) + right, row) for left, right, row in numbers] for numbers in planned]
+        for planned in plan
+    ]
     piece = (lefts[0].shape[1] // count, columns)
     shapes = [(count // 2, len(outputs)) + piece] + [piece] * (count // 2 * len(outputs))
     kept, *given = pl.pallas_call(
@@ -568,7 +609,7 @@
             + [pl.BlockSpec(shape, lambda i, places: (0, 0)) for shape in shapes[1:]],
         ),
         out_shape=[jax.ShapeDtypeStruct(shape, bf16) for shape in shapes],
-        compiler_params=pltpu.CompilerParams(vmem_limit_bytes=56 * 1024 * 1024),
+        compiler_params=whole_vmem,
         cost_estimate=small_cost,
         name=name,
     )(places, *lefts, *rights, *after)
@@ -584,6 +625,23 @@
     for _ in ref.shape[2:]:
         ref = ref.at[0]
     return ref[...].astype(f32)
+
+
+def add_pair_kernel(kept, arrived, *refs):
+    refs[-1][...] = (flat(kept) + flat(arrived)).astype(bf16)
+
+
+def add_pair(kept, arrived, item, after):
+    return pl.pallas_call(
+        add_pair_kernel,
+        grid=(1,),
+        in_specs=[lead(kept, 1, item), lead(arrived)] + unread(after),
+        out_specs=whole(arrived.shape),
+        out_shape=jax.ShapeDtypeStruct(arrived.shape, bf16),
+        cost_estimate=small_cost,
+        compiler_params=whole_vmem,
+        name="add_pair",
+    )(kept, arrived, *after)
 
 
 def finish_kernel(cuts, own, arrived, other, *refs):
@@ -608,7 +666,7 @@
         in_specs=[lead(own, 0, 0), lead(arrived), lead(other)] + unread(after),
         out_specs=[whole(shape) for shape in shapes],
         out_shape=[jax.ShapeDtypeStruct(shape, f32) for shape in shapes],
-        compiler_params=pltpu.CompilerParams(vmem_limit_bytes=40 * 1024 * 1024),
+        compiler_params=whole_vmem,
         cost_estimate=small_cost,
         name=name,
     )(own, arrived, other, *after)
@@ -642,20 +700,26 @@
             out_specs=[pl.BlockSpec(shape, lambda i, bits: (0, 0, 0))] * 2,
         ),
         out_shape=[jax.ShapeDtypeStruct(shape, bf16)] * 2,
-        compiler_params=pltpu.CompilerParams(vmem_limit_bytes=56 * 1024 * 1024),
+        compiler_params=whole_vmem,
         cost_estimate=small_cost,
         name="prepare",
     )(bit.reshape(1), gate, up, down)
 
 
 def dispatch_kernel(branch, slots, *refs):
-    mine_out, other_out = refs[-2:]
+    mine_out, others_out = refs[-3], refs[-2:]
     capacity = slots.shape[1] // 2
+    step = pl.program_id(0)
     for owner in range(slots.shape[0]):
         rows = slots.shape[2]
+        places = slice(owner * capacity, (owner + 1) * capacity)
         rows_in = dot_plain(slots[owner], branch[owner * rows : (owner + 1) * rows]).astype(bf16)
-        mine_out[owner * capacity : (owner + 1) * capacity] = rows_in[:capacity]
-        other_out[owner * capacity : (owner + 1) * capacity] = rows_in[capacity:]
+        mine_out[places] = rows_in[:capacity]
+        for half, other_out in enumerate(others_out):
+
+            @pl.when(step == half)
+            def store(other_out=other_out, places=places, rows_in=rows_in):
+                other_out[places] = rows_in[capacity:]
 
 
 def slot_specs(slots, step):
@@ -671,20 +735,31 @@
 def dispatch(branch, slots, after):
     members, both, _ = slots.shape
     width = branch.shape[1]
-    slot_spec, slot_rows, token_rows, grid = slot_specs(slots, 2)
-    shape = jax.ShapeDtypeStruct((members * both // 2, width), bf16)
+    slot_spec, slot_rows, token_rows, grid = slot_specs(slots, members // 2)
+    half = (members * both // 4, width)
     return pl.pallas_call(
         dispatch_kernel,
         grid=grid,
         in_specs=[token_rows(width), slot_spec] + unread(after),
-        out_specs=[slot_rows(width)] * 2,
-        out_shape=[shape, shape],
-        cost_estimate=small_cost,
+        out_specs=[slot_rows(width), whole(half), whole(half)],
+        out_shape=[
+            jax.ShapeDtypeStruct((members * both // 2, width), bf16),
+            jax.ShapeDtypeStruct(half, bf16),
+            jax.ShapeDtypeStruct(half, bf16),
+        ],
+        cost_estimate=small_cost,
+        compiler_params=whole_vmem,
         name="dispatch",
     )(branch, slots, *after)
 
 
-def shared_kernel(branch, weights, act_out, slope_out, inner_out):
+def shared_kernel(branch, weights, router, hot, *refs):
+    act_out, slope_out, inner_out, gates_out = refs[-4:]
+    named = hot[...] != 0
+    logits = jnp.where(named, dot_right_t(branch[...], router[...]), masked_value)
+    raised = jnp.exp(logits - jnp.max(logits, axis=1, keepdims=True))
+    raised = jnp.where(named, raised, 0.0)
+    gates_out[...] = raised / jnp.sum(raised, axis=1, keepdims=True)
     hidden = act_out.shape[1]
     both = dot_right_t(branch[...], weights[...])
     gate, up = both[:, :hidden], both[:, hidden:]
@@ -694,21 +769,32 @@
     inner_out[...] = (act * up).astype(bf16)
 
 
-def shared_forward(branch, weights):
+def router_rows(weights):
+    last = weights.shape[0] // 128 - 1
+    return pl.BlockSpec((128, weights.shape[1]), lambda i, *prefetched: (last, 0))
+
+
+def shared_forward(branch, weights, hot, after):
     rows, width = branch.shape
-    hidden = weights.shape[0] // 3
+    hidden = (weights.shape[0] - 128) // 3
     block = 512
     shape = jax.ShapeDtypeStruct((rows, hidden), bf16)
     return pl.pallas_call(
         shared_kernel,
         grid=(rows // block,),
-        in_specs=[by_rows(block, width), whole((2 * hidden, width))],
-        out_specs=[by_rows(block, hidden)] * 3,
-        out_shape=[shape] * 3,
-        compiler_params=pltpu.CompilerParams(vmem_limit_bytes=40 * 1024 * 1024),
+        in_specs=[
+            by_rows(block, width),
+            whole((2 * hidden, width)),
+            router_rows(weights),
+            by_rows(block, 128),
+        ]
+        + unread(after),
+        out_specs=[by_rows(block, hidden)] * 3 + [by_rows(block, 128)],
+        out_shape=[shape] * 3 + [jax.ShapeDtypeStruct((rows, 128), f32)],
+        compiler_params=whole_vmem,
         cost_estimate=small_cost,
         name="shared_forward",
-    )(branch, weights)
+    )(branch, weights, weights, hot, *after)
 
 
 def shared_back_kernel(grad, down, act, slope, *refs):
@@ -735,13 +821,19 @@
         + unread(after),
         out_specs=by_rows(block, 2 * hidden),
         out_shape=jax.ShapeDtypeStruct((rows, 2 * hidden), bf16),
-        compiler_params=pltpu.CompilerParams(vmem_limit_bytes=40 * 1024 * 1024),
+        compiler_params=whole_vmem,
         cost_estimate=small_cost,
         name="shared_back",
     )(grad, weights, act, slope, *after)
 
 
-def combine_kernel(inner, down, slots, out_mine, out_other, gate_mine, gate_other, out):
+def combine_kernel(named, inner, down, slots, out_mine, other_a, other_b, gates, out):
+    lane = lax.broadcasted_iota(jnp.int32, gates.shape, 1)
+    gate_mine, gate_other = [
+        jnp.sum(jnp.where(lane == named[index], gates[...], 0.0), axis=1, keepdims=True)
+        for index in range(2)
+    ]
+    out_other = jnp.where(pl.program_id(0) == 0, other_a[...], other_b[...])
     rows = slots.shape[2]
     capacity = slots.shape[1] // 2
     total = dot_plain(inner[...], down[...])
@@ -754,31 +846,43 @@
         out[tokens] = part.astype(bf16)
 
 
-def combine(inner, weights, slots, out_mine, out_other, gate_mine, gate_other):
+def combine(inner, weights, slots, out_mine, out_other, gates, named):
     hidden, width = inner.shape[1], weights.shape[1]
-    slot_spec, slot_rows, token_rows, grid = slot_specs(slots, 4)
+    members, both, rows = slots.shape
+    half = members // 2
+
+    def part(rows, cols):
+        return pl.BlockSpec((rows, cols), lambda i, named: (i, 0))
+
+    def all_of(shape):
+        return pl.BlockSpec(shape, lambda i, named: (0, 0))
+
     return pl.pallas_call(
         combine_kernel,
-        grid=grid,
-        in_specs=[
-            token_rows(hidden),
-            pl.BlockSpec((hidden, width), lambda i: (2, 0)),
-            slot_spec,
-            slot_rows(width),
-            slot_rows(width),
-            token_rows(1),
-            token_rows(1),
-        ],
-        out_specs=token_rows(width),
+        grid_spec=pltpu.PrefetchScalarGridSpec(
+            num_scalar_prefetch=1,
+            grid=(2,),
+            in_specs=[
+                part(half * rows, hidden),
+                pl.BlockSpec((hidden, width), lambda i, named: (2, 0)),
+                pl.BlockSpec((half, both, rows), lambda i, named: (i, 0, 0)),
+                part(half * both // 2, width),
+                all_of(out_other[0].shape),
+                all_of(out_other[1].shape),
+                part(half * rows, 128),
+            ],
+            out_specs=part(half * rows, width),
+        ),
         out_shape=jax.ShapeDtypeStruct((inner.shape[0], width), bf16),
-        compiler_params=pltpu.CompilerParams(vmem_limit_bytes=50 * 1024 * 1024),
+        compiler_params=whole_vmem,
         cost_estimate=small_cost,
         name="combine",
-    )(inner, weights, slots, out_mine, out_other, gate_mine, gate_other)
-
-
-def out_grad_kernel(grad, slots, out_mine, out_other, gate_mine, gate_other, *refs):
-    grad_mine, grad_other, gate_grad_mine, gate_grad_other = refs
+    )(named, inner, weights, slots, out_mine, *out_other, gates)
+
+
+def out_grad_kernel(grad, slots, out_mine, other_a, other_b, gate_mine, gate_other, *refs):
+    out_other = jnp.where(pl.program_id(0) < pl.num_programs(0) // 2, other_a[...], other_b[...])
+    grad_mine, grad_other, gate_grad_mine, gate_grad_other = refs[-4:]
     rows = slots.shape[2]
     capacity = slots.shape[1] // 2
     for owner in range(slots.shape[0]):
@@ -796,29 +900,42 @@
             gate_out[owner] = jnp.sum(hot_half * gate_grad, axis=0, keepdims=True)
 
 
-def out_grads(grad, slots, out_mine, out_other, gate_mine, gate_other):
+def out_grads(grad, slots, out_mine, out_other, gate_mine, gate_other, after):
     members, both, rows = slots.shape
     width = grad.shape[1]
     slot_spec, slot_rows, token_rows, grid = slot_specs(slots, 2)
     line = pl.BlockSpec((2, 1, rows), lambda i: (i, 0, 0))
+    steps = members // 4
+    first_half = pl.BlockSpec((both, width), lambda i: (jnp.minimum(i, steps - 1), 0))
+    second_half = pl.BlockSpec((both, width), lambda i: (jnp.maximum(i - steps, 0), 0))
     grads = jax.ShapeDtypeStruct((members * both // 2, width), bf16)
     gates = jax.ShapeDtypeStruct((members, 1, rows), f32)
     return pl.pallas_call(
         out_grad_kernel,
         grid=grid,
-        in_specs=[token_rows(width), slot_spec, slot_rows(width), slot_rows(width), line, line],
+        in_specs=[
+            token_rows(width),
+            slot_spec,
+            slot_rows(width),
+            first_half,
+            second_half,
+            line,
+            line,
+        ]
+        + unread(after),
         out_specs=[slot_rows(width), slot_rows(width), line, line],
         out_shape=[grads, grads, gates, gates],
-        compiler_params=pltpu.CompilerParams(vmem_limit_bytes=40 * 1024 * 1024),
+        compiler_params=whole_vmem,
         cost_estimate=small_cost,
         name="out_grads",
     )(
         grad,
         slots,
         out_mine,
-        out_other,
+        *out_other,
         gate_mine.reshape(members, 1, rows),
         gate_other.reshape(members, 1, rows),
+        *after,
     )
 
 
@@ -826,7 +943,7 @@
     out = refs[-1]
     rows = slots.shape[2]
     capacity = slots.shape[1] // 2
-    total = dot_plain(grads[...], weights[...]) + dot_right_t(logit_grad[...], router[...])
+    total = dot_plain(grads[...], weights[...]) + dot_plain(logit_grad[...], router[...])
     for owner in range(slots.shape[0]):
         tokens = slice(owner * rows, (owner + 1) * rows)
         places = slice(owner * capacity, (owner + 1) * capacity)
@@ -834,7 +951,7 @@
         out[tokens] = (total[tokens] + dot_left_t(slots[owner], arrived)).astype(bf16)
 
 
-def combine_back(grads, logit_grad, weights, router, slots, in_mine, in_other, after):
+def combine_back(grads, logit_grad, weights, slots, in_mine, in_other, after):
     width = weights.shape[1]
     slot_spec, slot_rows, token_rows, grid = slot_specs(slots, 4)
     return pl.pallas_call(
@@ -844,7 +961,7 @@
             token_rows(grads.shape[1]),
             token_rows(logit_grad.shape[1]),
             whole((grads.shape[1], width)),
-            whole(router.shape),
+            router_rows(weights),
             slot_spec,
             slot_rows(width),
             slot_rows(width),
@@ -852,10 +969,10 @@
         + unread(after),
         out_specs=token_rows(width),
         out_shape=jax.ShapeDtypeStruct((grads.shape[0], width), bf16),
-        compiler_params=pltpu.CompilerParams(vmem_limit_bytes=50 * 1024 * 1024),
+        compiler_params=whole_vmem,
         cost_estimate=small_cost,
         name="combine_back",
-    )(grads, logit_grad, weights, router, slots, in_mine, in_other, *after)
+    )(grads, logit_grad, weights, weights, slots, in_mine, in_other, *after)
 
 
 def latent_grad_kernel(kv_past, rope_past, kv_own, rope_own, expand, *refs):
@@ -877,6 +994,7 @@
         out_specs=pl.BlockSpec((2, block, LATENT + rope_cols), lambda i: (0, i, 0)),
         out_shape=jax.ShapeDtypeStruct((2, rows, LATENT + rope_cols), bf16),
         cost_estimate=small_cost,
+        compiler_params=whole_vmem,
         name="latent_grads",
     )(kv_past, rope_past, kv_own, rope_own, expand, *after)
 
@@ -892,10 +1010,32 @@
         grid=(1,),
         in_specs=[lead(blocks, 0)] + unread(after),
         out_specs=whole(shape),
-        out_shape=jax.ShapeDtypeStruct(shape, bf16),
-        cost_estimate=small_cost,
+        out_shape=jax.ShapeDtypeStruct(shape, blocks.dtype),
+        cost_estimate=small_cost,
+        compiler_params=whole_vmem,
         name="first_block",
     )(blocks, *after)
+
+
+def join_kernel(count, *refs):
+    rows = refs[0].shape[0]
+    for index in range(count):
+        refs[-1][index * rows : (index + 1) * rows] = refs[index][...]
+
+
+def join_rows(blocks, after):
+    rows, cols = blocks[0].shape
+    shape = (len(blocks) * rows, cols)
+    return pl.pallas_call(
+        functools.partial(join_kernel, len(blocks)),
+        grid=(1,),
+        in_specs=[whole((rows, cols))] * len(blocks) + unread(after),
+        out_specs=whole(shape),
+        out_shape=jax.ShapeDtypeStruct(shape, blocks[0].dtype),
+        cost_estimate=small_cost,
+        compiler_params=whole_vmem,
+        name="join_rows",
+    )(*blocks, *after)
 
 
 def latent_back_kernel(own, back, unit, factor, gain, cosine, sine, *refs):
@@ -920,6 +1060,7 @@
             jax.ShapeDtypeStruct((1, LATENT), f32),
         ],
         cost_estimate=small_cost,
+        compiler_params=whole_vmem,
         name="latent_back",
     )(*inputs, *after)
 
@@ -943,18 +1084,46 @@
             jax.ShapeDtypeStruct((rows, width), f32),
             jax.ShapeDtypeStruct((1, width), f32),
         ],
-        compiler_params=pltpu.CompilerParams(vmem_limit_bytes=40 * 1024 * 1024),
+        compiler_params=whole_vmem,
         cost_estimate=small_cost,
         name="tokens_back",
     )(*inputs, *after)
 
 
 def slice_grad_kernel(index, left, right, *refs):
-    refs[-1][...] = dot_left_t(left[...], right[...])
+    out = refs[-1]
+    half = ROPE // 2
+    grad = dot_left_t(left[...], right[...])
+    out[:LATENT] = grad[:LATENT]
+    turned = grad[LATENT:]
+    out[LATENT : LATENT + half] = turned[:half] + turned[half:ROPE]
+    out[LATENT + half :] = turned[ROPE : ROPE + half] + turned[ROPE + half :]
+
+
+def beside_kernel(blocks, out):
+    cols = blocks.shape[2]
+    for index in range(blocks.shape[0]):
+        out[:, index * cols : (index + 1) * cols] = blocks[index].astype(f32)
+
+
+def beside(blocks, rows):
+    count, _, cols = blocks.shape
+    step = rows // 4
+    return pl.pallas_call(
+        beside_kernel,
+        grid=(4,),
+        in_specs=[pl.BlockSpec((count, step, cols), lambda i: (0, i, 0))],
+        out_specs=by_rows(step, count * cols),
+        out_shape=jax.ShapeDtypeStruct((rows, count * cols), f32),
+        cost_estimate=small_cost,
+        compiler_params=whole_vmem,
+        name="beside",
+    )(blocks)
 
 
 def slice_grad(left, right, index, cols, after):
     rows = left.shape[0]
+    out_rows = LATENT + ROPE
     return pl.pallas_call(
         slice_grad_kernel,
         grid_spec=pltpu.PrefetchScalarGridSpec(
@@ -965,10 +1134,11 @@
                 pl.BlockSpec((rows, cols), lambda i, index: (0, index[0])),
             ]
             + unread(after),
-            out_specs=pl.BlockSpec((left.shape[1], cols), lambda i, index: (0, 0)),
+            out_specs=pl.BlockSpec((out_rows, cols), lambda i, index: (0, 0)),
         ),
-        out_shape=jax.ShapeDtypeStruct((left.shape[1], cols), f32),
-        cost_estimate=small_cost,
+        out_shape=jax.ShapeDtypeStruct((out_rows, cols), f32),
+        cost_estimate=small_cost,
+        compiler_params=whole_vmem,
         name="slice_grad",
     )(index.reshape(1), left, right, *after)
 
@@ -1003,7 +1173,7 @@
             ),
         ),
         out_shape=jax.ShapeDtypeStruct((2,) + shape, f32),
-        compiler_params=pltpu.CompilerParams(vmem_limit_bytes=40 * 1024 * 1024),
+        compiler_params=whole_vmem,
         cost_estimate=small_cost,
         name="place_experts",
     )(bit.reshape(1), own, arrived_item, other_item, *after)
@@ -1091,15 +1261,10 @@
                 kept, given = total[:half], list(total[half:].reshape((-1,) + total.shape[2:]))
         return (kept, arrived)
 
-    def exchange(self, kept, arrived):
-        items = kept.shape[1]
-        total = [
-            (kept[1, item].astype(f32) + arrived[items + item].astype(f32)).astype(bf16)
-            for item in range(items)
-        ]
-        return (kept, arrived, [self.swap_partner(piece) for piece in total])
-
-    def gather_members(self, value):
+    def partner_sum(self, kept, arrived, item, after=()):
+        return add_pair(kept, arrived[kept.shape[1] + item], item, after)
+
+    def gather_members(self, value, after):
         member = lax.axis_index("expert")
         rows = value.shape[0]
         chips = [value]
@@ -1107,7 +1272,7 @@
             pairs = [(i, i ^ (2 * other)) for i in range(self.members)]
             chips.append(lax.ppermute(value, "expert", pairs))
         both = lax.ppermute(
-            jnp.concatenate(chips), "expert", [(i, i ^ 1) for i in range(self.members)]
+            join_rows(chips, after), "expert", [(i, i ^ 1) for i in range(self.members)]
         )
         held = []
         for number, block in enumerate(chips):
@@ -1123,6 +1288,12 @@
         for bit in range(self.bits):
             arrived = self.swap(value.astype(bf16), (1 << bit, 1 << (self.bits - 1 - bit)))
             value = value + arrived.astype(f32)
+        return value
+
+    def total_members(self, value):
+        for bit in range(self.members.bit_length() - 1):
+            pairs = [(i, i ^ (1 << bit)) for i in range(self.members)]
+            value = value + lax.ppermute(value, "expert", pairs)
         return value
 
     def total_all(self, value):
@@ -1192,13 +1363,6 @@
     own_sin = lax.dynamic_slice_in_dim(sine, member * rows, rows, 0)
     projected = dot_right_t(own_normed, compress_t)
     latent_unit, latent_factor = normalize(projected[:, :LATENT])
-    turned = projected[:, LATENT:]
-    turned = turned * own_cos + jnp.roll(turned, ROPE, axis=1) * own_sin
-    latent = jnp.concatenate([latent_unit * latent_gain_vector, turned], axis=1).astype(bf16)
-    before = lax.ppermute(latent, "dp", [(i, i + 1) for i in range(groups - 1)])
-    before = first_block(before[None], [normed])
-    previous = lax.all_gather(before, "expert", axis=0, tiled=True)
-
     places = pairing.places()
     given, kept = prepare(bit, expert_gate_weight, expert_up_weight, expert_down_weight)
     expert_w = pairing.spread([kept, pairing.swap_partner(given)])
@@ -1207,8 +1371,13 @@
     padded = -(-shared_hidden_width // 128) * 128
     shared_w = jnp.concatenate(
         [
-            jnp.pad(weight, ((0, padded - shared_hidden_width), (0, 0)))
-            for weight in (shared_gate_weight.T, shared_up_weight.T, shared_down_weight)
+            jnp.pad(weight, ((0, extent - weight.shape[0]), (0, 0)))
+            for weight, extent in (
+                (shared_gate_weight.T, padded),
+                (shared_up_weight.T, padded),
+                (shared_down_weight, padded),
+                (router_weight.T, 128),
+            )
         ]
     )
 
@@ -1220,9 +1389,10 @@
     )
     doc_start = jnp.max(jnp.where(bounds <= place[:, None], bounds, 0), axis=1)
     in_block = jnp.arange(group_size, dtype=jnp.int32) % QUERY_BLOCK
-    low = jnp.maximum(doc_start - place + WINDOW + in_block, in_block + 1)[:, None]
-
-    hot = jnp.any(routes[:, :, None] == jnp.arange(expert_count, dtype=jnp.int32), axis=1)
+    low = jnp.maximum(doc_start - place + WINDOW + in_block, in_block + 1)
+    low = jnp.broadcast_to(low[:, None], (group_size, 128))
+
+    hot = jnp.any(routes[:, :, None] == jnp.arange(128, dtype=jnp.int32), axis=1).astype(bf16)
     routes_t = routes.T.reshape(route_count, members, rows)
     order = jnp.arange(rows, dtype=jnp.int32)
     earlier = (order[:, None] < order[None, :]).astype(bf16)
@@ -1238,7 +1408,7 @@
     slots = jnp.concatenate([slots_of(mine), slots_of(other)], axis=1)
 
     query_w = split_query_columns(query_weight)
-    kv, key_rope, group_latent = own_keys(
+    keys, group_latent = own_keys(
         normed,
         cosine,
         sine,
@@ -1247,56 +1417,61 @@
         latent_expand_weight,
         [shared_w, query_w],
     )
-    kv, key_rope = past_keys(previous, latent_expand_weight, kv, key_rope)
-    query, mixed, logs, attention_part = attend(
-        normed,
-        cosine,
-        sine,
-        low,
-        query_w,
-        kv,
-        key_rope,
-        output_weight,
-        expert_w[1:2],
-    )
+    forward = [(i, i + 1) for i in range(groups - 1)]
+    past = lax.ppermute(keys, "dp", forward)
+    previous = lax.ppermute(group_latent, "dp", forward)
+    query = project_query(normed, cosine, sine, query_w)
+    mixed, logs, attention_part = attend(query, low, keys, past, output_weight, expert_w[1:2])
     attention = lax.psum_scatter(attention_part, "expert", scatter_dimension=0, tiled=True)
     hidden, hidden_unit, hidden_factor, own_branch = norm(
         tokens, attention, second_gain_vector, expert_w[2:3]
     )
     branch = lax.all_gather(own_branch, "expert", axis=0, tiled=True)
 
-    logits = jnp.where(hot, dot_plain(branch, router_weight), masked_value)
-    top = jnp.max(logits, axis=1, keepdims=True)
-    raised = jnp.where(hot, jnp.exp(logits - top), 0.0)
-    gates = raised / jnp.sum(raised, axis=1, keepdims=True)
-    experts = jnp.arange(expert_count, dtype=jnp.int32)[None, :]
-    gate_mine = jnp.sum(jnp.where(experts == mine, gates, 0.0), axis=1, keepdims=True)
-    gate_other = jnp.sum(jnp.where(experts == other, gates, 0.0), axis=1, keepdims=True)
-
-    in_mine, in_other = dispatch(branch, slots, expert_w[3:])
-    in_arrived = pairing.swap_partner(in_other)
-    shared_act, shared_slope, shared_hidden = shared_forward(branch, shared_w)
-    act_a, slope_a, inner_a, out_arrived = expert_call(
-        expert_kernel, "expert", places, in_arrived, [], expert_w, 3, 2, [shared_hidden]
-    )
-    out_other = pairing.swap_partner(out_arrived)
+    in_mine, *in_others = dispatch(branch, slots, expert_w[3:])
+    in_arrived = [pairing.swap_partner(half) for half in in_others]
     act_m, slope_m, inner_m, out_mine = expert_call(
-        expert_kernel, "expert", places, in_mine, [], expert_w, 3, 2, [out_arrived]
-    )
+        expert_kernel, "expert", places, in_mine, [], expert_w, 3, []
+    )
+    half_rows, slot_rows = in_arrived[0].shape[0], in_mine.shape[0]
+    *held, out_first = expert_call(
+        expert_kernel,
+        "expert",
+        places,
+        in_arrived[0],
+        [],
+        expert_w,
+        3,
+        [out_mine],
+        0,
+        slot_rows,
+    )
+    *held, out_second = expert_call(
+        expert_kernel, "expert", places, in_arrived[1], [], expert_w, 3, [], half_rows, slot_rows, held
+    )
+    act_a, slope_a, inner_a = held
+    out_other = [pairing.swap_partner(half) for half in (out_first, out_second)]
+    shared_act, shared_slope, shared_hidden, gates = shared_forward(
+        branch, shared_w, hot, [out_second, out_other[0]]
+    )
+    experts = jnp.arange(128, dtype=jnp.int32)[None, :]
+    gate_mine = jnp.sum(jnp.where(experts == mine, gates, 0.0), axis=1)
+    gate_other = jnp.sum(jnp.where(experts == other, gates, 0.0), axis=1)
     branch_part = combine(
-        shared_hidden, shared_w, slots, out_mine, out_other, gate_mine, gate_other
+        shared_hidden, shared_w, slots, out_mine, out_other, gates, jnp.stack([mine, other])
     )
     branch_sum = lax.psum_scatter(branch_part, "expert", scatter_dimension=0, tiled=True)
     result = hidden + branch_sum.astype(f32)
     difference = result - target.astype(f32)
     squares = jnp.sum(counted[:, None] * difference * difference)
+    squares = pairing.total_all(jnp.full((8, 128), squares))
     total_tokens = rows * members * groups
     grad_out = total_tokens / count * counted[:, None] * difference
 
     grad_low = lax.all_gather(grad_out.astype(bf16), "expert", axis=0, tiled=True)
 
     out_grad_mine, out_grad_other, gate_grad_mine, gate_grad_other = out_grads(
-        grad_low, slots, out_mine, out_other, gate_mine, gate_other
+        grad_low, slots, out_mine, out_other, gate_mine, gate_other, [previous, squares]
     )
     out_grad_arrived = pairing.swap_partner(out_grad_other)
     shared_grad = shared_back(grad_low, shared_w, shared_act, shared_slope, [out_grad_mine])
@@ -1308,7 +1483,6 @@
         [act_m, slope_m],
         expert_w,
         2,
-        1,
         [shared_grad],
     )
     gate_ga, up_ga, in_grad_arrived = expert_call(
@@ -1319,7 +1493,6 @@
         [act_a, slope_a],
         expert_w,
         2,
-        1,
         [in_grad_mine],
     )
     in_grad_other = pairing.swap_partner(in_grad_arrived)
@@ -1335,22 +1508,26 @@
         experts == other, gate_grad_other.reshape(-1, 1), 0.0
     )
     logit_grad = gates * (gate_grads - jnp.sum(gates * gate_grads, axis=1, keepdims=True))
+    logit_total = pairing.total_members(
+        first_block(logit_grad[:, :expert_count].T[None], [down_kept])
+    )
     logit_grad = logit_grad.astype(bf16)
-    grad_router = dot_left_t(branch, logit_grad)
+    branch_slice = lax.dynamic_slice_in_dim(branch, member * (width // members), width // members, 1)
+    router_slice = dot_plain(logit_total.astype(bf16), branch_slice)
     branch_grad_part = combine_back(
         shared_grad,
         logit_grad,
         shared_w,
-        router_weight,
         slots,
         in_grad_mine,
         in_grad_other,
-        [down_kept],
+        [logit_total],
     )
     branch_grad = lax.psum_scatter(
         branch_grad_part, "expert", scatter_dimension=0, tiled=True
     )
 
+    down_terms = pairing.collect(down_kept, down_given)
     gate_up_kept, gate_up_given = weight_grads(
         "gate_up_grad",
         places,
@@ -1360,7 +1537,6 @@
         ],
         [branch_grad_part],
     )
-    down_terms = pairing.collect(down_kept, down_given)
     gate_up_terms = pairing.collect(gate_up_kept, gate_up_given)
     shared_kept, shared_given = weight_grads(
         "shared_grads",
@@ -1369,8 +1545,13 @@
         [gate_up_kept],
     )
     shared_terms = pairing.collect(shared_kept, shared_given)
-    down_parts = pairing.exchange(*down_terms)
-    gate_up_parts = pairing.exchange(*gate_up_terms)
+    down_sum = pairing.partner_sum(*down_terms, 0)
+    gate_sum, up_sum = [pairing.partner_sum(*gate_up_terms, item) for item in range(2)]
+    down_other, gate_other_half, up_other_half = [
+        pairing.swap_partner(total) for total in (down_sum, gate_sum, up_sum)
+    ]
+    down_parts = (*down_terms, [down_other])
+    gate_up_parts = (*gate_up_terms, [gate_other_half, up_other_half])
 
     grad_hidden_own, grad_hidden_low, grad_norm2 = norm_back_rows(
         branch_grad,
@@ -1378,7 +1559,7 @@
         hidden_unit,
         hidden_factor,
         second_gain_vector,
-        down_terms[1] + gate_up_terms[1][:1] + [shared_kept],
+        down_terms[1] + gate_up_terms[1][2:3] + [shared_kept],
     )
     grad_attention = lax.all_gather(grad_hidden_low, "expert", axis=0, tiled=True)
     query_grad, normed_grad_part, kv_past, rope_past, kv_own, rope_own = attend_back(
@@ -1389,15 +1570,15 @@
         sine,
         low,
         query_w,
-        kv,
-        key_rope,
+        keys,
+        past,
         output_weight,
-        gate_up_terms[1],
+        [down_sum, gate_sum],
     )
 
     latent_grad = lax.psum_scatter(
         latent_grads(
-            kv_past, rope_past, kv_own, rope_own, latent_expand_weight, shared_terms[1]
+            kv_past, rope_past, kv_own, rope_own, latent_expand_weight, shared_terms[1] + [down_other, gate_other_half, up_sum]
         ),
         "expert",
         scatter_dimension=1,
@@ -1413,19 +1594,25 @@
         [[[(normed, query_grad)], [(grad_attention, mixed)]]],
         [kv_own],
     )
-    attention_terms = pairing.collect(attention_kept, attention_given)
     expand_grad = (
-        dot_left_t(previous[:, :LATENT], kv_past) + dot_left_t(group_latent, kv_own)
+        dot_left_t(previous, kv_past) + dot_left_t(group_latent, kv_own)
     ).astype(bf16)
     expand_grad = expand_grad.reshape(groups, -1, expand_grad.shape[1])
     expand_pieces = jnp.stack([pick(expand_grad, places[i]) for i in range(groups)])[:, None]
-    expand_parts = pairing.exchange(
-        *pairing.collect(
-            expand_pieces[: groups // 2], list(expand_pieces[groups // 2 :].squeeze(1))
-        )
-    )
+    expand_terms = pairing.collect(
+        expand_pieces[: groups // 2], list(expand_pieces[groups // 2 :].squeeze(1))
+    )
+    expert_down_gradient = place_experts(bit, down_parts, 0, True, [attention_kept])
+    expand_sum = pairing.partner_sum(*expand_terms, 0)
+    expand_parts = (*expand_terms, [pairing.swap_partner(expand_sum)])
+    shared_sum = pairing.partner_sum(*shared_terms, 0)
+    shared_parts = (*shared_terms, [pairing.swap_partner(shared_sum)])
     back = lax.ppermute(
-        first_block(latent_grad, [attention_kept] + down_parts[2] + gate_up_parts[2][:1]),
+        first_block(
+            latent_grad,
+            [attention_kept, expert_down_gradient, up_other_half, gate_up_terms[1][0], shared_sum]
+            + [expand_pieces],
+        ),
         "dp",
         [(i + 1, i) for i in range(groups - 1)],
     )
@@ -1438,40 +1625,18 @@
         latent_gain_vector,
         own_cos,
         own_sin,
-        [],
-    )
-    group_grad = pairing.gather_members(grad_projected)
-    expert_down_gradient = place_experts(bit, down_parts, 0, True, [grad_projected])
+        gate_up_terms[1][1:2],
+    )
     expert_gate_gradient = place_experts(bit, gate_up_parts, 0, False, [grad_projected])
     expert_up_gradient = place_experts(bit, gate_up_parts, 1, False, [grad_projected])
-    shared_parts = pairing.exchange(*shared_terms)
-    attention_parts = pairing.exchange(*attention_terms)
     slice_cols = width // members
-    compress_slice = slice_grad(
-        group_grad,
-        normed,
-        member,
-        slice_cols,
-        [expert_down_gradient, expert_gate_gradient, expert_up_gradient]
-        + attention_terms[1],
-    )
-    compress_slice = pairing.total(
-        jnp.concatenate(
-            [
-                compress_slice[:LATENT],
-                compress_slice[LATENT : LATENT + half] + compress_slice[LATENT + half : LATENT + ROPE],
-                compress_slice[LATENT + ROPE : LATENT + ROPE + half]
-                + compress_slice[LATENT + ROPE + half :],
-            ]
-        )
-    ).astype(bf16)
-    grad_kva = (
-        lax.all_gather(compress_slice, "expert", axis=0, tiled=True)
-        .reshape(members, -1, slice_cols)
-        .transpose(0, 2, 1)
-        .reshape(width, -1)
-        .astype(f32)
-    )
+    group_grad = pairing.gather_members(
+        grad_projected, [expert_gate_gradient, expert_up_gradient, expand_sum]
+    )
+    attention_terms = pairing.collect(
+        attention_kept, attention_given
+    )
+    compress_slice = slice_grad(group_grad, normed, member, slice_cols, [])
     grad_tokens, grad_norm1 = tokens_back(
         normed_grad,
         grad_projected,
@@ -1480,17 +1645,30 @@
         own_factor,
         first_gain_vector,
         grad_hidden_own,
-        [compress_slice],
-    )
-    sums = [grad_router.reshape(-1), grad_norm2[0], grad_norm1[0], grad_latent_gain[0]]
-    cuts = [sum(part.size for part in sums[:number]) for number in range(1, len(sums) + 1)]
-    sums = pairing.total_all(
-        jnp.concatenate(sums + [jnp.full((8 * 128,), squares)]).reshape(-1, 128)
-    ).reshape(-1)
-    grad_router = sums[: cuts[0]].reshape(grad_router.shape)
-    grad_norm2, grad_norm1 = sums[cuts[0] : cuts[1]], sums[cuts[1] : cuts[2]]
-    grad_latent_gain, squares = sums[cuts[2] : cuts[3]], sums[-1]
-
+        [],
+    )
+    gains = jnp.concatenate(
+        [grad_latent_gain[0], grad_norm2[0], grad_norm1[0]]
+    ).reshape(-1, slice_cols)
+    gain_rows = -(-gains.shape[0] // 16) * 16
+    gains = jnp.pad(gains, ((0, gain_rows - gains.shape[0]), (0, 0)))
+    compress_rows = compress_slice.shape[0]
+    compress_slice = pairing.total(
+        jnp.concatenate([compress_slice, router_slice, gains])
+    ).astype(bf16)
+    compress_all = lax.all_gather(compress_slice, "expert", axis=0)
+    kva_t = beside(compress_all, compress_rows)
+    grad_kva = kva_t.T
+    router_rows = compress_rows + expert_count
+    grad_router = (
+        compress_all[:, compress_rows:router_rows].transpose(0, 2, 1).reshape(width, -1).astype(f32)
+    )
+    gains = jnp.sum(compress_all[:, router_rows:].astype(f32), axis=0).reshape(-1)
+    grad_latent_gain, gains = gains[:LATENT], gains[LATENT:]
+    grad_norm2, grad_norm1 = gains[:width], gains[width : 2 * width]
+
+    attention_sum = pairing.partner_sum(*attention_terms, 0, [group_grad])
+    attention_parts = (*attention_terms, [pairing.swap_partner(attention_sum)])
     query_cols, mixed_cols = query_w.shape[1], mixed.shape[1]
     shared_gate_gradient, shared_up_gradient, shared_down_gradient = finish(
         "shared_finish",
@@ -1504,7 +1682,7 @@
         attention_parts,
         [(0, query_cols, False), (query_cols, query_cols + mixed_cols, True)],
         [0, mixed_cols],
-        [compress_slice],
+        [kva_t],
     )
     shared_gate_gradient, shared_up_gradient = shared_gate_gradient.T, shared_up_gradient.T
     query_weight_gradient = join_query_columns(query_weight_gradient)
@@ -1517,7 +1695,7 @@
     )
     return (
         result.astype(bf16),
-        squares / (count * width),
+        squares[0, 0] / (count * width),
         grad_tokens,
         grad_norm1,
         grad_norm2,

time: 859 us -> 817 us (0.951)
  Pallas kernels: 272 us -> 315 us
  waiting for transfers between devices: 359 us -> 327 us
  local copies, waits for them, and re-layouts: 71.2 us -> 44.9 us
  other arithmetic: 56.2 us -> 39.1 us
    all_gather x1, waiting for transfers between devices: 45.4 us -> 15.4 us  [body(): lax.all_gather(grad_out.astype(bf16), 'expert', axis=0, tiled=True)]
    ppermute x3 -> x7, waiting for transfers between devices: 8.74 us -> 34.3 us  [the longest x1 22 us: body(): past = lax.ppermute(keys, 'dp', forward)]
    pallas_call x7 -> x16, Pallas kernels: 98.1 us -> 123 us  [the longest x5 75.9 us: expert_call(): pl.pallas_call(functools.partial(kernel, count, len(after) + len(held), r...]
    unnamed x178 -> x113, local copies, waits for them, and re-layouts: 44.3 us -> 21 us
    ppermute x3, waiting for transfers between devices: 19.9 us -> 3.15 us  [gather_members(): chips.append(lax.ppermute(value, 'expert', pairs))]
    convert_element_type x6 -> x2, other arithmetic: 14.5 us -> 1.6 us  [the longest x1 0.85 us: body(): compress_slice = pairing.total(jnp.concatenate([compress_slice, router_sl...]
    all_gather x2 -> x1, waiting for transfers between devices: 12.6 us -> 0.01 us  [body(): compress_all = lax.all_gather(compress_slice, 'expert', axis=0)]
    ppermute x27 -> x29, waiting for transfers between devices: 193 us -> 181 us  [swap(): return lax.ppermute(value, ('dp', 'expert'), pairs)]
  transfers between devices with their start and end apart: 54 -> 59, of which waited for: 31 -> 37; matrix products, arithmetic and copies ran while one was open for 10% -> 7% of each run, Pallas kernels for 21% -> 29%
where the time goes in v3:
time: 817 us; the launch traced here: 807 us
  waiting for transfers between devices  327 us (40%)
  Pallas kernels  315 us (39%)
  starting transfers between devices  56.4 us (7%)
  local copies, waits for them, and re-layouts  44.9 us (5%)
  other arithmetic  39.1 us (5%)
  between operations  18.2 us (2%)
    ppermute x29, waiting for transfers between devices, swap(): return lax.ppermute(value, ('dp', 'expert'), pairs)  181 us
    pallas_call x5, Pallas kernels, expert_call(): pl.pallas_call(functools.partial(kernel, count, len(after) + len(held), r...  75.9 us
    pallas_call x4, Pallas kernels, weight_grads(): pl.pallas_call(functools.partial(weight_grad_kernel, count, plan), grid_s...  62 us
    ppermute x29, starting transfers between devices, swap(): return lax.ppermute(value, ('dp', 'expert'), pairs)  38.7 us
    ppermute x10, waiting for transfers between devices, total_all(): value = value + lax.ppermute(value, ('dp', 'expert'), pairs)  37.1 us
    reduce_scatter x1, waiting for transfers between devices, body(): lax.psum_scatter(branch_part, 'expert', scatter_dimension=0, tiled=True)  25.8 us
    pallas_call x1, Pallas kernels, attend_back(): pl.pallas_call(functools.partial(attend_back_kernel, chunks), grid=(rows...  23.3 us
    ppermute x1, waiting for transfers between devices, body(): past = lax.ppermute(keys, 'dp', forward)  22 us
  transfers between devices with their start and end apart: 59, of which 37 were waited for; matrix products, arithmetic and copies ran while one was open for 7% of the time, Pallas kernels for 29%

profile of v3, /device:TPU:0, one launch (start us, length us, event | category | flops | bytes accessed | tf_op | source)
XLA Modules:
  0.0 806.6 jit_solution(9798896741838860058)
XLA Ops:
  11.0 7.7 prepare.1
  28.6 5.1 concatenate.36.query_w.refs_1_
  44.0 16.9 %all-gather.7.cloned.1.call-done.normed.refs_0_.right = bf16[1024,2048]{1,0:T(8,128)(2,1)} async-done(((bf16[128,2048]{1,0:T(8,128)(2,1)}), bf16[1024,2048]{1,0:T(8,128)(2,1)}) %all-gather.7.cloned.1.call-update) | async-done | bytes 4194320 | tf_op jit(solution)/shard_map/all_gather | solution.py:1348
  60.9 8.4 %own_keys.1 = (bf16[1024,640]{1,0:T(8,128)(2,1)}, bf16[1024,512]{1,0:T(8,128)(2,1)}) custom-call(bf16[1024,2048]{1,0:T(8,128)(2,1)} %all-gather.7.cloned.1.call-done.normed.refs_0_.right, f32[1024,128]{1,0:T(8,128)} %pad_maximum_fusion.1.cosine, f32[1024,128]{1,0:T(8,128)} %pad_maximum_fusion.2.sine, f32[1,512]{1,0:T(1,128)} %bitcast.96, ...), custom_call_target="tpu_custom_call" | custom-call | flops 1 | bytes 1 | tf_op jit(solution)/shard_map/own_keys/pallas_call | solution.py:139
  73.1 6.3 project_query.1.query_in
  79.4 22.0 %collective-permute-done.refs_0_.refs_1_.refs_3_.refs_5_ = bf16[1024,640]{1,0:T(8,128)(2,1)S(1)} collective-permute-done((bf16[1024,640]{1,0:T(8,128)(2,1)}, bf16[1024,640]{1,0:T(8,128)(2,1)S(1)}, u32[]{:S(2)}, u32[]{:S(2)}) %collective-permute-start) | collective-permute-done | bytes 1310752 | tf_op jit(solution)/shard_map/ppermute | solution.py:1421
  102.8 13.3 %attend.1 = (bf16[1024,256]{1,0:T(8,128)(2,1)}, f32[1024,128]{1,0:T(8,128)}, bf16[1024,2048]{1,0:T(8,128)(2,1)}) custom-call(bf16[1024,384]{1,0:T(8,128)(2,1)} %project_query.1.query_in, s32[1024,128]{1,0:T(8,128)} %broadcast_in_dim.107.low, bf16[256,2048]{1,0:T(8,128)(2,1)} %out_w.3, bf16[1024,640]{1,0:T(8,128)(2,1)} %copy-done, bf16[1024,640]{1,0:T(8,128)(2,1)} %copy-done, ...), custom_call_target="tpu_custom_call" | custom-call | flops 1 | bytes 1 | tf_op jit(solution)/shard_map/attend/pallas_call | solution.py:197
  118.6 48.2 %collective-permute-done.2.refs_0_.refs_2_ = bf16[3,512,1408]{2,1,0:T(8,128)(2,1)} collective-permute-done((bf16[3,512,1408]{2,1,0:T(8,128)(2,1)}, bf16[3,512,1408]{2,1,0:T(8,128)(2,1)}, u32[]{:S(2)}, u32[]{:S(2)}) %collective-permute-start.2) | collective-permute-done | bytes 4325408 | tf_op jit(solution)/shard_map/ppermute | solution.py:1234
  173.0 47.0 %collective-permute-done.3.refs_0_.refs_3_ = bf16[3,512,1408]{2,1,0:T(8,128)(2,1)} collective-permute-done((bf16[3,512,1408]{2,1,0:T(8,128)(2,1)}, bf16[3,512,1408]{2,1,0:T(8,128)(2,1)}, u32[]{:S(2)}, u32[]{:S(2)}) %collective-permute-start.3) | collective-permute-done | bytes 4325408 | tf_op jit(solution)/shard_map/ppermute | solution.py:1234
  220.0 6.0 dispatch.1
  229.7 16.5 %expert.3 = (bf16[512,1408]{1,0:T(8,128)(2,1)}, bf16[512,1408]{1,0:T(8,128)(2,1)}, bf16[512,1408]{1,0:T(8,128)(2,1)}, bf16[512,2048]{1,0:T(8,128)(2,1)}) custom-call(s32[4]{0:T(128)} %pad_add_fusion.1.places, bf16[512,2048]{1,0:T(8,128)(2,1)} %get-tuple-element.97.slot_in.refs_0_, bf16[3,512,1408]{2,1,0:T(8,128)(2,1)} %get-tuple-element.92.refs_0_, ...), custom_call_target="tpu_custom_call" | custom-call | flops 1 | bytes 1 | tf_op jit(solution)/shard_map/expert/pallas_call | solution.py:519
  247.2 11.5 %expert.4 = (bf16[512,1408]{1,0:T(8,128)(2,1)}, bf16[512,1408]{1,0:T(8,128)(2,1)}, bf16[512,1408]{1,0:T(8,128)(2,1)}, bf16[256,2048]{1,0:T(8,128)(2,1)}) custom-call(s32[4]{0:T(128)} %pad_add_fusion.1.places, bf16[256,2048]{1,0:T(8,128)(2,1)} %copy-done.17, bf16[3,512,1408]{2,1,0:T(8,128)(2,1)} %get-tuple-element.92.refs_0_, ...), custom_call_target="tpu_custom_call" | custom-call | flops 1 | bytes 1 | tf_op jit(solution)/shard_map/expert/pallas_call | solution.py:519
  261.7 11.5 %expert.5 = (bf16[512,1408]{1,0:T(8,128)(2,1)}, bf16[512,1408]{1,0:T(8,128)(2,1)}, bf16[512,1408]{1,0:T(8,128)(2,1)}, bf16[256,2048]{1,0:T(8,128)(2,1)}) custom-call(s32[4]{0:T(128)} %pad_add_fusion.1.places, bf16[256,2048]{1,0:T(8,128)(2,1)} %copy-done.18, ...), custom_call_target="tpu_custom_call", output_to_operand_aliasing={{0}: (6, {}), {1}: (7, {}), {2}: (8, {})} | custom-call | flops 1 | bytes 1 | tf_op jit(solution)/shard_map/expert/pallas_call | solution.py:519
  276.9 8.6 %shared_forward.1 = (bf16[1024,384]{1,0:T(8,128)(2,1)}, bf16[1024,384]{1,0:T(8,128)(2,1)}, bf16[1024,384]{1,0:T(8,128)(2,1)}, f32[1024,128]{1,0:T(8,128)}) custom-call(bf16[1024,2048]{1,0:T(8,128)(2,1)} %all-gather.9.cloned.1.call-done.branch.refs_0_, bf16[1280,2048]{1,0:T(8,128)(2,1)} %fusion.7.refs_0_.weights.router.down, ...), custom_call_target="tpu_custom_call" | custom-call | flops 1 | bytes 1 | tf_op jit(solution)/shard_map/shared_forward/pallas_call | solution.py:782
  289.3 9.4 %combine.1 = bf16[1024,2048]{1,0:T(8,128)(2,1)} custom-call(s32[2]{0:T(128)} %pad_add_fusion.named, bf16[1024,384]{1,0:T(8,128)(2,1)} %get-tuple-element.104.inner.refs_3_, bf16[1280,2048]{1,0:T(8,128)(2,1)} %fusion.7.refs_0_.weights.router.down, bf16[8,128,128]{2,1,0:T(8,128)(2,1)} %add_convert_fusion.1.slots, ...), custom_call_target="tpu_custom_call" | custom-call | flops 1 | bytes 1 | tf_op jit(solution)/shard_map/combine/pallas_call | solution.py:860
  320.2 25.8 %reduce-scatter.8.cloned.1.call-done = bf16[128,2048]{1,0:T(8,128)(2,1)} async-done(((bf16[1024,2048]{1,0:T(8,128)(2,1)}), bf16[128,2048]{1,0:T(8,128)(2,1)}) %reduce-scatter.8.cloned.1.call-update) | async-done | bytes 524304 | tf_op jit(solution)/shard_map/reduce_scatter | solution.py:1463
  360.0 4.7 collective-permute-done.10
  366.0 9.5 %collective-permute-done.11 = f32[8,128]{1,0:T(8,128)S(1)} collective-permute-done((f32[8,128]{1,0:T(8,128)S(1)}, f32[8,128]{1,0:T(8,128)S(1)}, u32[]{:S(2)}, u32[]{:S(2)}) %collective-permute-start.11) | collective-permute-done | bytes 4128 | tf_op jit(solution)/shard_map/ppermute | solution.py:1303
  379.7 15.4 %all-gather.11.cloned.1.call-done.grad.refs_1_ = bf16[1024,2048]{1,0:T(8,128)(2,1)} async-done(((bf16[128,2048]{1,0:T(8,128)(2,1)}), bf16[1024,2048]{1,0:T(8,128)(2,1)}) %all-gather.11.cloned.1.call-update) | async-done | bytes 4194320 | tf_op jit(solution)/shard_map/all_gather | solution.py:1471
  395.1 6.8 out_grads.1
  403.4 6.0 shared_back.1.refs_4_.grads.refs_2_
  409.5 18.1 %expert_back.2 = (bf16[512,1408]{1,0:T(8,128)(2,1)}, bf16[512,1408]{1,0:T(8,128)(2,1)}, bf16[512,2048]{1,0:T(8,128)(2,1)}) custom-call(s32[4]{0:T(128)} %pad_add_fusion.1.places, bf16[512,2048]{1,0:T(8,128)(2,1)} %get-tuple-element.109.refs_0_.out_grad, bf16[512,1408]{1,0:T(8,128)(2,1)} %get-tuple-element.112.act, ...), custom_call_target="tpu_custom_call" | custom-call | flops 1 | bytes 1 | tf_op jit(solution)/shard_map/expert_back/pallas_call | solution.py:519
  429.6 18.4 %expert_back.3 = (bf16[512,1408]{1,0:T(8,128)(2,1)}, bf16[512,1408]{1,0:T(8,128)(2,1)}, bf16[512,2048]{1,0:T(8,128)(2,1)}) custom-call(s32[4]{0:T(128)} %pad_add_fusion.1.places, bf16[512,2048]{1,0:T(8,128)(2,1)} %copy-done.5, bf16[512,1408]{1,0:T(8,128)(2,1)} %get-tuple-element.116.act, bf16[512,1408]{1,0:T(8,128)(2,1)} %get-tuple-element.117.slope, ...), custom_call_target="tpu_custom_call" | custom-call | flops 1 | bytes 1 | tf_op jit(solution)/shard_map/expert_back/pallas_call | solution.py:519
  452.0 13.4 %down_grad.1 = (bf16[2,1,512,1408]{3,2,1,0:T(8,128)(2,1)}, bf16[512,1408]{1,0:T(8,128)(2,1)}, bf16[512,1408]{1,0:T(8,128)(2,1)}) custom-call(s32[4]{0:T(128)} %pad_add_fusion.1.places, bf16[512,2048]{1,0:T(8,128)(2,1)} %get-tuple-element.109.refs_0_.out_grad, bf16[512,2048]{1,0:T(8,128)(2,1)} %copy-done.5, bf16[512,1408]{1,0:T(8,128)(2,1)} %get-tuple-element.119.refs_2_, ...), custom_call_target="tpu_custom_call" | custom-call | flops 1 | bytes 1 | tf_op jit(solution)/shard_map/down_grad/pallas_call | solution.py:597
  469.2 4.3 collective-permute-done.22
  474.5 4.6 collective-permute-done.23
  481.0 10.4 %combine_back.1.refs_7_ = bf16[1024,2048]{1,0:T(8,128)(2,1)} custom-call(bf16[1024,768]{1,0:T(8,128)(2,1)} %shared_back.1.refs_4_.grads.refs_2_, bf16[1024,128]{1,0:T(8,128)(2,1)} %get-tuple-element.175.logit_grad, bf16[1280,2048]{1,0:T(8,128)(2,1)} %fusion.7.refs_0_.weights.router.down, bf16[1280,2048]{1,0:T(8,128)(2,1)} %fusion.7.refs_0_.weights.router.down, ...), custom_call_target="tpu_custom_call" | custom-call | flops 1 | bytes 1 | tf_op jit(solution)/shard_map/combine_back/pallas_call | solution.py:957
  493.6 24.4 %gate_up_grad.1 = (bf16[2,2,512,1408]{3,2,1,0:T(8,128)(2,1)}, bf16[512,1408]{1,0:T(8,128)(2,1)}, bf16[512,1408]{1,0:T(8,128)(2,1)}, bf16[512,1408]{1,0:T(8,128)(2,1)}, bf16[512,1408]{1,0:T(8,128)(2,1)}) custom-call(s32[4]{0:T(128)} %pad_add_fusion.1.places, bf16[512,2048]{1,0:T(8,128)(2,1)} %get-tuple-element.97.slot_in.refs_0_, ...), custom_call_target="tpu_custom_call" | custom-call | flops 1 | bytes 1 | tf_op jit(solution)/shard_map/gate_up_grad/pallas_call | solution.py:597
  519.7 12.9 %shared_grads.1 = (bf16[2,1,512,1152]{3,2,1,0:T(8,128)(2,1)}, bf16[512,1152]{1,0:T(8,128)(2,1)}, bf16[512,1152]{1,0:T(8,128)(2,1)}) custom-call(s32[4]{0:T(128)} %pad_add_fusion.1.places, bf16[1024,2048]{1,0:T(8,128)(2,1)} %all-gather.9.cloned.1.call-done.branch.refs_0_, bf16[1024,2048]{1,0:T(8,128)(2,1)} %all-gather.11.cloned.1.call-done.grad.refs_1_, ...), custom_call_target="tpu_custom_call" | custom-call | flops 1 | bytes 1 | tf_op jit(solution)/shard_map/shared_grads/pallas_call | solution.py:597
  532.6 9.2 %collective-permute-done.26.refs_2_.arrived = bf16[512,1408]{1,0:T(8,128)(2,1)} collective-permute-done((bf16[512,1408]{1,0:T(8,128)(2,1)}, bf16[512,1408]{1,0:T(8,128)(2,1)}, u32[]{:S(2)}, u32[]{:S(2)}) %collective-permute-start.26) | collective-permute-done | bytes 1441824 | tf_op jit(solution)/shard_map/ppermute | solution.py:1234
  558.2 21.5 %collective-permute-done.31.arrived = bf16[512,1408]{1,0:T(8,128)(2,1)} collective-permute-done((bf16[512,1408]{1,0:T(8,128)(2,1)}, bf16[512,1408]{1,0:T(8,128)(2,1)}, u32[]{:S(2)}, u32[]{:S(2)}) %collective-permute-start.31) | collective-permute-done | bytes 1441824 | tf_op jit(solution)/shard_map/ppermute | solution.py:1234
  582.9 7.9 all-gather.13.cloned.1.call-done.grad.refs_1_
  590.8 23.3 %attend_back.1 = (bf16[1024,384]{1,0:T(8,128)(2,1)}, bf16[1024,2048]{1,0:T(8,128)(2,1)}, bf16[1024,512]{1,0:T(8,128)(2,1)}, bf16[1024,128]{1,0:T(8,128)(2,1)}, b...) custom-call(bf16[1024,2048]{1,0:T(8,128)(2,1)} %all-gather.13.cloned.1.call-done.grad.refs_1_, ...), custom_call_target="tpu_custom_call" | custom-call | flops 1 | bytes 1 | tf_op jit(solution)/shard_map/attend_back/pallas_call | solution.py:311
  614.1 7.0 collective-permute-done.28.refs_1_.arrived
  622.3 5.2 latent_grads.1
  640.6 11.3 %attention_grads.1 = (bf16[2,1,512,640]{3,2,1,0:T(8,128)(2,1)}, bf16[512,640]{1,0:T(8,128)(2,1)}, bf16[512,640]{1,0:T(8,128)(2,1)}) custom-call(s32[4]{0:T(128)} %pad_add_fusion.1.places, bf16[1024,2048]{1,0:T(8,128)(2,1)} %all-gather.7.cloned.1.call-done.normed.refs_0_.right, bf16[1024,2048]{1,0:T(8,128)(2,1)} %all-gather.13.cloned.1.call-done.grad.refs_1_, ...), custom_call_target="tpu_custom_call" | custom-call | flops 1 | bytes 1 | tf_op jit(solution)/shard_map/attention_grads/pallas_call | solution.py:597
  651.9 5.6 place_experts.3.refs_1_
  662.4 4.4 collective-permute-done.32.refs_2_.other
  671.7 8.0 collective-permute-done.35.refs_0_.arrived
  695.7 5.1 place_experts.5.refs_5_
  700.8 5.1 place_experts.4.refs_4_
  720.9 5.1 reduce-scatter.12.cloned.1.call-done.grad
  726.0 4.5 tokens_back.1
  732.8 5.5 collective-permute-done.41
  739.9 5.5 collective-permute-done.42
  754.4 11.3 %collective-permute-done.44.arrived = bf16[512,640]{1,0:T(8,128)(2,1)S(1)} collective-permute-done((bf16[512,640]{1,0:T(8,128)(2,1)}, bf16[512,640]{1,0:T(8,128)(2,1)S(1)}, u32[]{:S(2)}, u32[]{:S(2)}) %collective-permute-start.44) | collective-permute-done | bytes 655392 | tf_op jit(solution)/shard_map/ppermute | solution.py:1234
  769.4 5.8 collective-permute-done.48.other
  783.9 4.4 beside.1.refs_0_
  (324 shorter events, 219.8 us)
Async XLA Ops:
  7.2 53.7 %all-gather.7.cloned.1.call-start = ((), (), s32[]{:S(2)}) async-start(), calls=%async_computation.5 | async-start | bytes 4718592 | tf_op jit(solution)/shard_map/all_gather | solution.py:1348
  10.9 155.9 %reduce-scatter.6.cloned.1.call-start = ((), (), s32[]{:S(2)}) async-start(), calls=%async_computation.6 | async-start | bytes 4718592 | tf_op jit(solution)/shard_map/reduce_scatter | solution.py:1425
  18.6 60.8 %collective-permute-start.1 = (bf16[3,512,1408]{2,1,0:T(8,128)(2,1)}, bf16[3,512,1408]{2,1,0:T(8,128)(2,1)}, u32[]{:S(2)}, u32[]{:S(2)}) collective-permute-start(bf16[3,512,1408]{2,1,0:T(8,128)(2,1)} %get-tuple-element.90), channel_id=1, source_target_pairs={{0,16},{1,9},{2,18},{3,11},{4,20},{5,13},{6,22},{7,15},{8,24},{9,1... | collective-permute-start | bytes 12976136 | tf_op jit(solution)/shard_map/ppermute | solution.py:1234
  69.3 32.1 %collective-permute-start = (bf16[1024,640]{1,0:T(8,128)(2,1)}, bf16[1024,640]{1,0:T(8,128)(2,1)S(1)}, u32[]{:S(2)}, u32[]{:S(2)}) collective-permute-start(bf16[1024,640]{1,0:T(8,128)(2,1)} %get-tuple-element.89.refs_2_.refs_4_.refs_6_.refs_7_), channel_id=1, source_target_pairs={{0,8},{8,16},{16,24},{1,9},{9,17},{17,25},{2,10},{10,18},{18,26},{... | collective-permute-start | bytes 3932168 | tf_op jit(solution)/shard_map/ppermute | solution.py:1421
  116.1 104.0 %all-gather.9.cloned.1.call-start = ((), (), s32[]{:S(2)}) async-start(), calls=%async_computation.7 | async-start | bytes 4718592 | tf_op jit(solution)/shard_map/all_gather | solution.py:1429
  116.1 50.6 %collective-permute-start.2 = (bf16[3,512,1408]{2,1,0:T(8,128)(2,1)}, bf16[3,512,1408]{2,1,0:T(8,128)(2,1)}, u32[]{:S(2)}, u32[]{:S(2)}) collective-permute-start(bf16[3,512,1408]{2,1,0:T(8,128)(2,1)} %get-tuple-element.92.refs_0_), channel_id=1, source_target_pairs={{0,8},{1,17},{2,10},{3,19},{4,12},{5,21},{6,14},{7,23},{8,0},{9,25... | collective-permute-start | bytes 12976136 | tf_op jit(solution)/shard_map/ppermute | solution.py:1234
  169.7 176.4 %reduce-scatter.8.cloned.1.call-start = ((), (), s32[]{:S(2)}) async-start(), calls=%async_computation.8 | async-start | bytes 4718592 | tf_op jit(solution)/shard_map/reduce_scatter | solution.py:1463
  169.7 50.3 %collective-permute-start.3 = (bf16[3,512,1408]{2,1,0:T(8,128)(2,1)}, bf16[3,512,1408]{2,1,0:T(8,128)(2,1)}, u32[]{:S(2)}, u32[]{:S(2)}) collective-permute-start(bf16[3,512,1408]{2,1,0:T(8,128)(2,1)} %collective-permute-done.1.refs_8_.refs_1_), channel_id=1, source_target_pairs={{0,8},{1,17},{2,10},{3,19},{4,12},{5,21},{6,14},{7,23},{8,0},{9,25... | collective-permute-start | bytes 12976136 | tf_op jit(solution)/shard_map/ppermute | solution.py:1234
  226.1 20.1 %collective-permute-start.5 = (bf16[256,2048]{1,0:T(8,128)(2,1)}, bf16[256,2048]{1,0:T(8,128)(2,1)S(1)}, u32[]{:S(2)}, u32[]{:S(2)}) collective-permute-start(bf16[256,2048]{1,0:T(8,128)(2,1)} %get-tuple-element.96), channel_id=1, source_target_pairs={{0,16},{1,9},{2,18},{3,11},{4,20},{5,13},{6,22},{7,15},{8,24},{9,1... | collective-permute-start | bytes 3145736 | tf_op jit(solution)/shard_map/ppermute | solution.py:1234
  229.0 31.7 %collective-permute-start.4 = (bf16[256,2048]{1,0:T(8,128)(2,1)}, bf16[256,2048]{1,0:T(8,128)(2,1)S(1)}, u32[]{:S(2)}, u32[]{:S(2)}) collective-permute-start(bf16[256,2048]{1,0:T(8,128)(2,1)} %get-tuple-element.95), channel_id=1, source_target_pairs={{0,16},{1,9},{2,18},{3,11},{4,20},{5,13},{6,22},{7,15},{8,24},{9,1... | collective-permute-start | bytes 3145736 | tf_op jit(solution)/shard_map/ppermute | solution.py:1234
  258.7 17.2 %collective-permute-start.6 = (bf16[256,2048]{1,0:T(8,128)(2,1)}, bf16[256,2048]{1,0:T(8,128)(2,1)S(1)}, u32[]{:S(2)}, u32[]{:S(2)}) collective-permute-start(bf16[256,2048]{1,0:T(8,128)(2,1)} %get-tuple-element.103), channel_id=1, source_target_pairs={{0,16},{1,9},{2,18},{3,11},{4,20},{5,13},{6,22},{7,15},{8,24},{9,1... | collective-permute-start | bytes 3145736 | tf_op jit(solution)/shard_map/ppermute | solution.py:1234
  273.2 15.1 %collective-permute-start.7 = (bf16[256,2048]{1,0:T(8,128)(2,1)}, bf16[256,2048]{1,0:T(8,128)(2,1)S(1)}, u32[]{:S(2)}, u32[]{:S(2)}) collective-permute-start(bf16[256,2048]{1,0:T(8,128)(2,1)} %get-tuple-element.102.refs_0_), channel_id=1, source_target_pairs={{0,16},{1,9},{2,18},{3,11},{4,20},{5,13},{6,22},{7,15},{8,24},{9,1... | collective-permute-start | bytes 3145736 | tf_op jit(solution)/shard_map/ppermute | solution.py:1234
  298.8 96.3 %all-gather.11.cloned.1.call-start = ((), (), s32[]{:S(2)}) async-start(), calls=%async_computation.9 | async-start | bytes 4718592 | tf_op jit(solution)/shard_map/all_gather | solution.py:1471
  306.9 4.9 collective-permute-start.15
  349.6 192.2 %reduce-scatter.10.cloned.1.call-start = ((), (), s32[]{:S(2)}) async-start(), calls=%async_computation.10 | async-start | bytes 4718592 | tf_op jit(solution)/shard_map/reduce_scatter | solution.py:1526
  349.7 30.0 %collective-permute-start.18 = (bf16[1024,512]{1,0:T(8,128)(2,1)}, bf16[1024,512]{1,0:T(8,128)(2,1)S(1)}, u32[]{:S(2)}, u32[]{:S(2)}) collective-permute-start(bf16[1024,512]{1,0:T(8,128)(2,1)} %get-tuple-element.108), channel_id=1, source_target_pairs={{0,8},{8,16},{16,24},{1,9},{9,17},{17,25},{2,10},{10,18},{18,26},{... | collective-permute-start | bytes 3145736 | tf_op jit(solution)/shard_map/ppermute | solution.py:1422
  364.8 10.7 %collective-permute-start.11 = (f32[8,128]{1,0:T(8,128)S(1)}, f32[8,128]{1,0:T(8,128)S(1)}, u32[]{:S(2)}, u32[]{:S(2)}) collective-permute-start(f32[8,128]{1,0:T(8,128)S(1)} %add.210), channel_id=1, source_target_pairs={{0,8},{1,9},{2,10},{3,11},{4,12},{5,13},{6,14},{7,15},{8,0},{9,1},... | collective-permute-start | bytes 12296 | tf_op jit(solution)/shard_map/ppermute | solution.py:1303
  401.9 26.3 %collective-permute-start.19 = (bf16[512,2048]{1,0:T(8,128)(2,1)}, bf16[512,2048]{1,0:T(8,128)(2,1)S(1)}, u32[]{:S(2)}, u32[]{:S(2)}) collective-permute-start(bf16[512,2048]{1,0:T(8,128)(2,1)} %get-tuple-element.115), channel_id=1, source_target_pairs={{0,16},{1,9},{2,18},{3,11},{4,20},{5,13},{6,22},{7,15},{8,24},{9,1... | collective-permute-start | bytes 6291464 | tf_op jit(solution)/shard_map/ppermute | solution.py:1234
  447.9 31.8 %collective-permute-start.20 = (bf16[512,2048]{1,0:T(8,128)(2,1)}, bf16[512,2048]{1,0:T(8,128)(2,1)S(1)}, u32[]{:S(2)}, u32[]{:S(2)}) collective-permute-start(bf16[512,2048]{1,0:T(8,128)(2,1)} %get-tuple-element.118.refs_4_), channel_id=1, source_target_pairs={{0,16},{1,9},{2,18},{3,11},{4,20},{5,13},{6,22},{7,15},{8,24},{9,1... | collective-permute-start | bytes 6291464 | tf_op jit(solution)/shard_map/ppermute | solution.py:1234
  473.5 5.6 collective-permute-start.23
  491.4 99.4 %all-gather.13.cloned.1.call-start = ((), (), s32[]{:S(2)}) async-start(), calls=%async_computation.11 | async-start | bytes 4718592 | tf_op jit(solution)/shard_map/all_gather | solution.py:1564
  491.5 41.1 %collective-permute-start.24 = (bf16[512,1408]{1,0:T(8,128)(2,1)}, bf16[512,1408]{1,0:T(8,128)(2,1)S(1)}, u32[]{:S(2)}, u32[]{:S(2)}) collective-permute-start(bf16[512,1408]{1,0:T(8,128)(2,1)} %get-tuple-element.124), channel_id=1, source_target_pairs={{0,8},{1,17},{2,10},{3,19},{4,12},{5,21},{6,14},{7,23},{8,0},{9,25... | collective-permute-start | bytes 4325384 | tf_op jit(solution)/shard_map/ppermute | solution.py:1234
  493.2 39.3 %collective-permute-start.25 = (bf16[512,1408]{1,0:T(8,128)(2,1)}, bf16[512,1408]{1,0:T(8,128)(2,1)S(1)}, u32[]{:S(2)}, u32[]{:S(2)}) collective-permute-start(bf16[512,1408]{1,0:T(8,128)(2,1)} %get-tuple-element.125), channel_id=1, source_target_pairs={{0,8},{1,17},{2,10},{3,19},{4,12},{5,21},{6,14},{7,23},{8,0},{9,25... | collective-permute-start | bytes 4325384 | tf_op jit(solution)/shard_map/ppermute | solution.py:1234
  518.0 23.8 %collective-permute-start.26 = (bf16[512,1408]{1,0:T(8,128)(2,1)}, bf16[512,1408]{1,0:T(8,128)(2,1)}, u32[]{:S(2)}, u32[]{:S(2)}) collective-permute-start(bf16[512,1408]{1,0:T(8,128)(2,1)} %get-tuple-element.130), channel_id=1, source_target_pairs={{0,8},{1,17},{2,10},{3,19},{4,12},{5,21},{6,14},{7,23},{8,0},{9,25... | collective-permute-start | bytes 4325384 | tf_op jit(solution)/shard_map/ppermute | solution.py:1234
  545.2 121.7 %reduce-scatter.14.cloned.1.call-start = ((), (), s32[]{:S(2)}) async-start(), calls=%async_computation.13 | async-start | bytes 2949120 | tf_op jit(solution)/shard_map/reduce_scatter | solution.py:1579
  545.6 34.1 %collective-permute-start.31 = (bf16[512,1408]{1,0:T(8,128)(2,1)}, bf16[512,1408]{1,0:T(8,128)(2,1)}, u32[]{:S(2)}, u32[]{:S(2)}) collective-permute-start(bf16[512,1408]{1,0:T(8,128)(2,1)} %get-tuple-element.142), channel_id=1, source_target_pairs={{0,8},{1,17},{2,10},{3,19},{4,12},{5,21},{6,14},{7,23},{8,0},{9,25... | collective-permute-start | bytes 4325384 | tf_op jit(solution)/shard_map/ppermute | solution.py:1234
  550.6 63.5 %collective-permute-start.29 = (bf16[512,1408]{1,0:T(8,128)(2,1)}, bf16[512,1408]{1,0:T(8,128)(2,1)S(1)}, u32[]{:S(2)}, u32[]{:S(2)}) collective-permute-start(bf16[512,1408]{1,0:T(8,128)(2,1)} %add_pair.6.refs_8_), channel_id=1, source_target_pairs={{0,16},{1,9},{2,18},{3,11},{4,20},{5,13},{6,22},{7,15},{8,24},{9,1... | collective-permute-start | bytes 4325384 | tf_op jit(solution)/shard_map/ppermute | solution.py:1234
  554.5 66.7 %collective-permute-start.30 = (bf16[512,1408]{1,0:T(8,128)(2,1)}, bf16[512,1408]{1,0:T(8,128)(2,1)S(1)}, u32[]{:S(2)}, u32[]{:S(2)}) collective-permute-start(bf16[512,1408]{1,0:T(8,128)(2,1)} %add_pair.7.refs_9_), channel_id=1, source_target_pairs={{0,16},{1,9},{2,18},{3,11},{4,20},{5,13},{6,22},{7,15},{8,24},{9,1... | collective-permute-start | bytes 4325384 | tf_op jit(solution)/shard_map/ppermute | solution.py:1234
  556.2 58.0 %collective-permute-start.27 = (bf16[512,1152]{1,0:T(8,128)(2,1)}, bf16[512,1152]{1,0:T(8,128)(2,1)}, u32[]{:S(2)}, u32[]{:S(2)}) collective-permute-start(bf16[512,1152]{1,0:T(8,128)(2,1)} %get-tuple-element.140), channel_id=1, source_target_pairs={{0,8},{1,17},{2,10},{3,19},{4,12},{5,21},{6,14},{7,23},{8,0},{9,25... | collective-permute-start | bytes 3538952 | tf_op jit(solution)/shard_map/ppermute | solution.py:1234
  556.4 64.8 %collective-permute-start.28 = (bf16[512,1152]{1,0:T(8,128)(2,1)}, bf16[512,1152]{1,0:T(8,128)(2,1)}, u32[]{:S(2)}, u32[]{:S(2)}) collective-permute-start(bf16[512,1152]{1,0:T(8,128)(2,1)} %get-tuple-element.141), channel_id=1, source_target_pairs={{0,8},{1,17},{2,10},{3,19},{4,12},{5,21},{6,14},{7,23},{8,0},{9,25... | collective-permute-start | bytes 3538952 | tf_op jit(solution)/shard_map/ppermute | solution.py:1234
  627.5 98.5 %reduce-scatter.12.cloned.1.call-start = ((), (), s32[]{:S(2)}) async-start(), calls=%async_computation.12 | async-start | bytes 4718592 | tf_op jit(solution)/shard_map/reduce_scatter | solution.py:1587
  628.3 154.7 %all-gather.15.cloned.1.call-start = ((), (), s32[]{:S(2)}) async-start(), calls=%async_computation.14 | async-start | bytes 2875392 | tf_op jit(solution)/shard_map/all_gather | solution.py:1659
  630.3 32.0 %collective-permute-start.33 = (bf16[512,1408]{1,0:T(8,128)(2,1)}, bf16[512,1408]{1,0:T(8,128)(2,1)S(1)}, u32[]{:S(2)}, u32[]{:S(2)}) collective-permute-start(bf16[512,1408]{1,0:T(8,128)(2,1)} %get-tuple-element.146), channel_id=1, source_target_pairs={{0,8},{1,17},{2,10},{3,19},{4,12},{5,21},{6,14},{7,23},{8,0},{9,25... | collective-permute-start | bytes 4325384 | tf_op jit(solution)/shard_map/ppermute | solution.py:1234
  632.1 34.7 %collective-permute-start.32 = (bf16[512,1408]{1,0:T(8,128)(2,1)}, bf16[512,1408]{1,0:T(8,128)(2,1)S(1)}, u32[]{:S(2)}, u32[]{:S(2)}) collective-permute-start(bf16[512,1408]{1,0:T(8,128)(2,1)} %add_pair.8.refs_4_), channel_id=1, source_target_pairs={{0,16},{1,9},{2,18},{3,11},{4,20},{5,13},{6,22},{7,15},{8,24},{9,1... | collective-permute-start | bytes 4325384 | tf_op jit(solution)/shard_map/ppermute | solution.py:1234
  634.6 45.0 %collective-permute-start.35 = (bf16[512,1408]{1,0:T(8,128)(2,1)}, bf16[512,1408]{1,0:T(8,128)(2,1)}, u32[]{:S(2)}, u32[]{:S(2)}) collective-permute-start(bf16[512,1408]{1,0:T(8,128)(2,1)} %get-tuple-element.147), channel_id=1, source_target_pairs={{0,8},{1,17},{2,10},{3,19},{4,12},{5,21},{6,14},{7,23},{8,0},{9,25... | collective-permute-start | bytes 4325384 | tf_op jit(solution)/shard_map/ppermute | solution.py:1234
  669.6 11.8 %collective-permute-start.34 = (bf16[128,640]{1,0:T(8,128)(2,1)}, bf16[128,640]{1,0:T(8,128)(2,1)S(1)}, u32[]{:S(2)}, u32[]{:S(2)}) collective-permute-start(bf16[128,640]{1,0:T(8,128)(2,1)} %first_block.3), channel_id=1, source_target_pairs={{8,0},{16,8},{24,16},{9,1},{17,9},{25,17},{10,2},{18,10},{26,18},{... | collective-permute-start | bytes 491528 | tf_op jit(solution)/shard_map/ppermute | solution.py:1610
  684.1 21.8 %collective-permute-start.38 = (bf16[128,640]{1,0:T(8,128)(2,1)}, bf16[128,640]{1,0:T(8,128)(2,1)S(1)}, u32[]{:S(2)}, u32[]{:S(2)}) collective-permute-start(bf16[128,640]{1,0:T(8,128)(2,1)} %get-tuple-element.148.projected.refs_0_), channel_id=1, source_target_pairs={{0,6},{1,7},{2,4},{3,5},{4,2},{5,3},{6,0},{7,1},{8,14},{9,15},{10,... | collective-permute-start | bytes 491528 | tf_op jit(solution)/shard_map/ppermute | solution.py:1273
  684.9 24.2 %collective-permute-start.37 = (bf16[128,640]{1,0:T(8,128)(2,1)}, bf16[128,640]{1,0:T(8,128)(2,1)S(1)}, u32[]{:S(2)}, u32[]{:S(2)}) collective-permute-start(bf16[128,640]{1,0:T(8,128)(2,1)} %get-tuple-element.148.projected.refs_0_), channel_id=1, source_target_pairs={{0,4},{1,5},{2,6},{3,7},{4,0},{5,1},{6,2},{7,3},{8,12},{9,13},{10,... | collective-permute-start | bytes 491528 | tf_op jit(solution)/shard_map/ppermute | solution.py:1273
  685.9 23.2 %collective-permute-start.36 = (bf16[128,640]{1,0:T(8,128)(2,1)}, bf16[128,640]{1,0:T(8,128)(2,1)S(1)}, u32[]{:S(2)}, u32[]{:S(2)}) collective-permute-start(bf16[128,640]{1,0:T(8,128)(2,1)} %get-tuple-element.148.projected.refs_0_), channel_id=1, source_target_pairs={{0,2},{1,3},{2,0},{3,1},{4,6},{5,7},{6,4},{7,5},{8,10},{9,11},{10,... | collective-permute-start | bytes 491528 | tf_op jit(solution)/shard_map/ppermute | solution.py:1273
  688.4 5.0 collective-permute-start.39
  731.3 7.1 collective-permute-start.41
  738.4 7.1 collective-permute-start.42
  746.3 28.9 %collective-permute-start.48 = (bf16[512,1152]{1,0:T(8,128)(2,1)S(1)}, bf16[512,1152]{1,0:T(8,128)(2,1)S(1)}, u32[]{:S(2)}, u32[]{:S(2)}) collective-permute-start(bf16[512,1152]{1,0:T(8,128)(2,1)S(1)} %copy-done.15), channel_id=1, source_target_pairs={{0,16},{1,9},{2,18},{3,11},{4,20},{5,13},{6,22},{7,15},{8,24},{9,1... | collective-permute-start | bytes 3538952 | tf_op jit(solution)/shard_map/ppermute | solution.py:1234
  747.8 17.9 %collective-permute-start.44 = (bf16[512,640]{1,0:T(8,128)(2,1)}, bf16[512,640]{1,0:T(8,128)(2,1)S(1)}, u32[]{:S(2)}, u32[]{:S(2)}) collective-permute-start(bf16[512,640]{1,0:T(8,128)(2,1)} %get-tuple-element.155), channel_id=1, source_target_pairs={{0,8},{1,17},{2,10},{3,19},{4,12},{5,21},{6,14},{7,23},{8,0},{9,25... | collective-permute-start | bytes 1966088 | tf_op jit(solution)/shard_map/ppermute | solution.py:1234
  749.3 30.5 %collective-permute-start.46 = (bf16[128,512]{1,0:T(8,128)(2,1)S(1)}, bf16[128,512]{1,0:T(8,128)(2,1)S(1)}, u32[]{:S(2)}, u32[]{:S(2)}) collective-permute-start(bf16[128,512]{1,0:T(8,128)(2,1)S(1)} %bitcast.83), channel_id=1, source_target_pairs={{0,8},{1,17},{2,10},{3,19},{4,12},{5,21},{6,14},{7,23},{8,0},{9,25... | collective-permute-start | bytes 393224 | tf_op jit(solution)/shard_map/ppermute | solution.py:1234
  749.9 30.0 %collective-permute-start.47 = (bf16[128,512]{1,0:T(8,128)(2,1)S(1)}, bf16[128,512]{1,0:T(8,128)(2,1)S(1)}, u32[]{:S(2)}, u32[]{:S(2)}) collective-permute-start(bf16[128,512]{1,0:T(8,128)(2,1)S(1)} %copy-done.39), channel_id=1, source_target_pairs={{0,16},{1,9},{2,18},{3,11},{4,20},{5,13},{6,22},{7,15},{8,24},{9,1... | collective-permute-start | bytes 393224 | tf_op jit(solution)/shard_map/ppermute | solution.py:1234
  752.9 36.2 %collective-permute-start.43 = (bf16[512,640]{1,0:T(8,128)(2,1)}, bf16[512,640]{1,0:T(8,128)(2,1)}, u32[]{:S(2)}, u32[]{:S(2)}) collective-permute-start(bf16[512,640]{1,0:T(8,128)(2,1)} %get-tuple-element.154), channel_id=1, source_target_pairs={{0,8},{1,17},{2,10},{3,19},{4,12},{5,21},{6,14},{7,23},{8,0},{9,25... | collective-permute-start | bytes 1966088 | tf_op jit(solution)/shard_map/ppermute | solution.py:1234
  768.8 20.3 %collective-permute-start.45 = (bf16[512,640]{1,0:T(8,128)(2,1)}, bf16[512,640]{1,0:T(8,128)(2,1)}, u32[]{:S(2)}, u32[]{:S(2)}) collective-permute-start(bf16[512,640]{1,0:T(8,128)(2,1)} %add_pair.11), channel_id=1, source_target_pairs={{0,16},{1,9},{2,18},{3,11},{4,20},{5,13},{6,22},{7,15},{8,24},{9,1... | collective-permute-start | bytes 1966088 | tf_op jit(solution)/shard_map/ppermute | solution.py:1234
  (65 other events, 398.6 us)
Sparse Core Ops, SparseCore 0:
  11.0 49.8 all-gather.6
  116.2 49.6 reduce-scatter.5
  169.8 46.4 all-gather.8
  298.9 47.1 reduce-scatter.7
  349.7 45.3 all-gather.10
  491.6 48.3 reduce-scatter.9
  545.3 45.4 all-gather.12
  627.7 35.7 reduce-scatter.13
  666.3 59.6 reduce-scatter.11
  746.4 35.0 all-gather.14

commit v4 on v3

--- a/solution.py
+++ b/solution.py
@@ -1065,10 +1065,58 @@
     )(*inputs, *after)
 
 
+def gain_part_kernel(grad, normed, gain, *refs):
+    out = refs[-1]
+    step = pl.program_id(0)
+
+    @pl.when(step == 0)
+    def clear():
+        out[...] = jnp.zeros_like(out)
+
+    out[...] += jnp.sum(grad[...].astype(f32) * normed[...].astype(f32), axis=0, keepdims=True)
+
+    @pl.when(step == pl.num_programs(0) - 1)
+    def divide():
+        out[...] = out[...] / gain[...]
+
+
+def gain_part(grad, normed, gain):
+    rows, width = grad.shape
+    block = QUERY_BLOCK
+    return pl.pallas_call(
+        gain_part_kernel,
+        grid=(rows // block,),
+        in_specs=[by_rows(block, width), by_rows(block, width), whole((1, width))],
+        out_specs=whole((1, width)),
+        out_shape=jax.ShapeDtypeStruct((1, width), f32),
+        compiler_params=whole_vmem,
+        cost_estimate=small_cost,
+        name="gain_part",
+    )(grad, normed, gain[None])
+
+
+def gain_rest_kernel(projected, compress, unit, part, out):
+    total = dot_plain(projected[...], compress[...])
+    out[...] = part[...] + jnp.sum(total * unit[...], axis=0, keepdims=True)
+
+
+def gain_rest(projected, compress, unit, part):
+    inputs = [projected, compress, unit, part]
+    return pl.pallas_call(
+        gain_rest_kernel,
+        grid=(1,),
+        in_specs=[whole(array.shape) for array in inputs],
+        out_specs=whole(part.shape),
+        out_shape=jax.ShapeDtypeStruct(part.shape, f32),
+        compiler_params=whole_vmem,
+        cost_estimate=small_cost,
+        name="gain_rest",
+    )(*inputs)
+
+
 def tokens_back_kernel(grad, projected, compress, unit, factor, gain, hidden_grad, *refs):
-    out, gain_grad_out = refs[-2:]
+    out = refs[-1]
     total = grad[...].astype(f32) + dot_plain(projected[...], compress[...])
-    gain_grad_out[...] = jnp.sum(total * unit[...], axis=0, keepdims=True)
     out[...] = hidden_grad[...] + norm_back(total, unit[...], factor[...], gain[...])
 
 
@@ -1079,11 +1127,8 @@
         tokens_back_kernel,
         grid=(1,),
         in_specs=[whole(array.shape) for array in inputs] + unread(after),
-        out_specs=[whole((rows, width)), whole((1, width))],
-        out_shape=[
-            jax.ShapeDtypeStruct((rows, width), f32),
-            jax.ShapeDtypeStruct((1, width), f32),
-        ],
+        out_specs=whole((rows, width)),
+        out_shape=jax.ShapeDtypeStruct((rows, width), f32),
         compiler_params=whole_vmem,
         cost_estimate=small_cost,
         name="tokens_back",
@@ -1291,10 +1336,12 @@
         return value
 
     def total_members(self, value):
-        for bit in range(self.members.bit_length() - 1):
-            pairs = [(i, i ^ (1 << bit)) for i in range(self.members)]
-            value = value + lax.ppermute(value, "expert", pairs)
-        return value
+        def turned(mask):
+            return [(i, i ^ mask) for i in range(self.members)]
+
+        value = value + lax.ppermute(value, "expert", turned(1))
+        masks = range(2, self.members, 2)
+        return sum([lax.ppermute(value, "expert", turned(mask)) for mask in masks], value)
 
     def total_all(self, value):
         size = self.groups * self.members
@@ -1415,7 +1462,7 @@
         latent_gain_vector,
         compress_t,
         latent_expand_weight,
-        [shared_w, query_w],
+        [shared_w, query_w, hot, slots],
     )
     forward = [(i, i + 1) for i in range(groups - 1)]
     past = lax.ppermute(keys, "dp", forward)
@@ -1474,7 +1521,6 @@
         grad_low, slots, out_mine, out_other, gate_mine, gate_other, [previous, squares]
     )
     out_grad_arrived = pairing.swap_partner(out_grad_other)
-    shared_grad = shared_back(grad_low, shared_w, shared_act, shared_slope, [out_grad_mine])
     gate_gm, up_gm, in_grad_mine = expert_call(
         expert_back_kernel,
         "expert_back",
@@ -1483,8 +1529,9 @@
         [act_m, slope_m],
         expert_w,
         2,
-        [shared_grad],
-    )
+        [],
+    )
+    shared_grad = shared_back(grad_low, shared_w, shared_act, shared_slope, [in_grad_mine])
     gate_ga, up_ga, in_grad_arrived = expert_call(
         expert_back_kernel,
         "expert_back",
@@ -1493,7 +1540,7 @@
         [act_a, slope_a],
         expert_w,
         2,
-        [in_grad_mine],
+        [shared_grad],
     )
     in_grad_other = pairing.swap_partner(in_grad_arrived)
 
@@ -1602,6 +1649,7 @@
     expand_terms = pairing.collect(
         expand_pieces[: groups // 2], list(expand_pieces[groups // 2 :].squeeze(1))
     )
+    norm1_part = gain_part(normed_grad_part, normed, first_gain_vector)
     expert_down_gradient = place_experts(bit, down_parts, 0, True, [attention_kept])
     expand_sum = pairing.partner_sum(*expand_terms, 0)
     expand_parts = (*expand_terms, [pairing.swap_partner(expand_sum)])
@@ -1611,7 +1659,7 @@
         first_block(
             latent_grad,
             [attention_kept, expert_down_gradient, up_other_half, gate_up_terms[1][0], shared_sum]
-            + [expand_pieces],
+            + [expand_pieces, norm1_part],
         ),
         "dp",
         [(i + 1, i) for i in range(groups - 1)],
@@ -1625,19 +1673,20 @@
         latent_gain_vector,
         own_cos,
         own_sin,
-        gate_up_terms[1][1:2],
+        [],
     )
     expert_gate_gradient = place_experts(bit, gate_up_parts, 0, False, [grad_projected])
     expert_up_gradient = place_experts(bit, gate_up_parts, 1, False, [grad_projected])
     slice_cols = width // members
+    grad_norm1 = gain_rest(grad_projected, compress_t, own_unit, norm1_part)
     group_grad = pairing.gather_members(
-        grad_projected, [expert_gate_gradient, expert_up_gradient, expand_sum]
+        grad_projected, [expert_gate_gradient, expert_up_gradient, expand_sum, grad_norm1]
     )
     attention_terms = pairing.collect(
         attention_kept, attention_given
     )
     compress_slice = slice_grad(group_grad, normed, member, slice_cols, [])
-    grad_tokens, grad_norm1 = tokens_back(
+    grad_tokens = tokens_back(
         normed_grad,
         grad_projected,
         compress_t,
@@ -1675,7 +1724,7 @@
         shared_parts,
         [(i * padded, (i + 1) * padded, True) for i in range(3)],
         [shared_hidden_width] * 3,
-        [compress_slice],
+        [compress_slice, grad_tokens],
     )
     query_weight_gradient, output_weight_gradient = finish(
         "attention_finish",

time: 817 us -> 817 us (level)
  waiting for transfers between devices: 327 us -> 309 us
  Pallas kernels: 315 us -> 325 us
    ppermute x29, waiting for transfers between devices: 181 us -> 170 us  [swap(): return lax.ppermute(value, ('dp', 'expert'), pairs)]
    ppermute x1, waiting for transfers between devices: 1.65 us -> 10 us  [body(): lax.ppermute(first_block(latent_grad, [attention_kept, expert_down_gradie...]
    unnamed x113 -> x115, local copies, waits for them, and re-layouts: 21 us -> 20.3 us
  transfers between devices with their start and end apart: 59 -> 60, of which waited for: 37 -> 33; matrix products, arithmetic and copies ran while one was open for 7% -> 7% of each run, Pallas kernels for 29% -> 31%
where the time goes in v4:
time: 817 us; the launch traced here: 806 us
  Pallas kernels  325 us (40%)
  waiting for transfers between devices  309 us (38%)
  starting transfers between devices  60.5 us (7%)
  local copies, waits for them, and re-layouts  48.3 us (6%)
  other arithmetic  39.2 us (5%)
  between operations  18.5 us (2%)
    ppermute x29, waiting for transfers between devices, swap(): return lax.ppermute(value, ('dp', 'expert'), pairs)  170 us
    pallas_call x5, Pallas kernels, expert_call(): pl.pallas_call(functools.partial(kernel, count, len(after) + len(held), r...  75.8 us
    pallas_call x4, Pallas kernels, weight_grads(): pl.pallas_call(functools.partial(weight_grad_kernel, count, plan), grid_s...  62.2 us
    ppermute x29, starting transfers between devices, swap(): return lax.ppermute(value, ('dp', 'expert'), pairs)  40 us
    ppermute x10, waiting for transfers between devices, total_all(): value = value + lax.ppermute(value, ('dp', 'expert'), pairs)  37 us
    reduce_scatter x1, waiting for transfers between devices, body(): lax.psum_scatter(branch_part, 'expert', scatter_dimension=0, tiled=True)  25.9 us
    pallas_call x1, Pallas kernels, attend_back(): pl.pallas_call(functools.partial(attend_back_kernel, chunks), grid=(rows...  24 us
    ppermute x1, waiting for transfers between devices, body(): past = lax.ppermute(keys, 'dp', forward)  22 us
  transfers between devices with their start and end apart: 60, of which 33 were waited for; matrix products, arithmetic and copies ran while one was open for 7% of the time, Pallas kernels for 31%

profile of v4, /device:TPU:0, one launch (start us, length us, event | category | flops | bytes accessed | tf_op | source)
XLA Modules:
  0.0 806.1 jit_solution(1330954133738317086)
XLA Ops:
  11.5 7.6 prepare.1
  31.8 5.3 concatenate.36.query_w.refs_1_
  49.6 11.8 %all-gather.7.cloned.1.call-done.normed.refs_0_.right = bf16[1024,2048]{1,0:T(8,128)(2,1)} async-done(((bf16[128,2048]{1,0:T(8,128)(2,1)}), bf16[1024,2048]{1,0:T(8,128)(2,1)}) %all-gather.7.cloned.1.call-update) | async-done | bytes 4194320 | tf_op jit(solution)/shard_map/all_gather | solution.py:1395
  61.4 8.4 %own_keys.1 = (bf16[1024,640]{1,0:T(8,128)(2,1)}, bf16[1024,512]{1,0:T(8,128)(2,1)}) custom-call(bf16[1024,2048]{1,0:T(8,128)(2,1)} %all-gather.7.cloned.1.call-done.normed.refs_0_.right, f32[1024,128]{1,0:T(8,128)} %pad_maximum_fusion.1.cosine, f32[1024,128]{1,0:T(8,128)} %pad_maximum_fusion.2.sine, f32[1,512]{1,0:T(1,128)} %bitcast.98, ...), custom_call_target="tpu_custom_call" | custom-call | flops 1 | bytes 1 | tf_op jit(solution)/shard_map/own_keys/pallas_call | solution.py:139
  73.6 6.3 project_query.1.query_in
  79.9 22.0 %collective-permute-done.refs_0_.refs_1_.refs_3_.refs_5_ = bf16[1024,640]{1,0:T(8,128)(2,1)S(1)} collective-permute-done((bf16[1024,640]{1,0:T(8,128)(2,1)}, bf16[1024,640]{1,0:T(8,128)(2,1)S(1)}, u32[]{:S(2)}, u32[]{:S(2)}) %collective-permute-start) | collective-permute-done | bytes 1310752 | tf_op jit(solution)/shard_map/ppermute | solution.py:1468
  103.2 13.5 %attend.1 = (bf16[1024,256]{1,0:T(8,128)(2,1)}, f32[1024,128]{1,0:T(8,128)}, bf16[1024,2048]{1,0:T(8,128)(2,1)}) custom-call(bf16[1024,384]{1,0:T(8,128)(2,1)} %project_query.1.query_in, s32[1024,128]{1,0:T(8,128)} %broadcast_in_dim.108.low, bf16[256,2048]{1,0:T(8,128)(2,1)} %out_w.3, bf16[1024,640]{1,0:T(8,128)(2,1)} %copy-done, bf16[1024,640]{1,0:T(8,128)(2,1)} %copy-done, ...), custom_call_target="tpu_custom_call" | custom-call | flops 1 | bytes 1 | tf_op jit(solution)/shard_map/attend/pallas_call | solution.py:197
  119.2 48.2 %collective-permute-done.2.refs_0_.refs_2_ = bf16[3,512,1408]{2,1,0:T(8,128)(2,1)} collective-permute-done((bf16[3,512,1408]{2,1,0:T(8,128)(2,1)}, bf16[3,512,1408]{2,1,0:T(8,128)(2,1)}, u32[]{:S(2)}, u32[]{:S(2)}) %collective-permute-start.2) | collective-permute-done | bytes 4325408 | tf_op jit(solution)/shard_map/ppermute | solution.py:1279
  172.4 48.2 %collective-permute-done.3.refs_0_.refs_3_ = bf16[3,512,1408]{2,1,0:T(8,128)(2,1)} collective-permute-done((bf16[3,512,1408]{2,1,0:T(8,128)(2,1)}, bf16[3,512,1408]{2,1,0:T(8,128)(2,1)}, u32[]{:S(2)}, u32[]{:S(2)}) %collective-permute-start.3) | collective-permute-done | bytes 4325408 | tf_op jit(solution)/shard_map/ppermute | solution.py:1279
  220.7 6.2 dispatch.1
  230.5 16.5 %expert.3 = (bf16[512,1408]{1,0:T(8,128)(2,1)}, bf16[512,1408]{1,0:T(8,128)(2,1)}, bf16[512,1408]{1,0:T(8,128)(2,1)}, bf16[512,2048]{1,0:T(8,128)(2,1)}) custom-call(s32[4]{0:T(128)} %pad_add_fusion.1.places, bf16[512,2048]{1,0:T(8,128)(2,1)} %get-tuple-element.95.slot_in.refs_0_, bf16[3,512,1408]{2,1,0:T(8,128)(2,1)} %get-tuple-element.90.refs_0_, ...), custom_call_target="tpu_custom_call" | custom-call | flops 1 | bytes 1 | tf_op jit(solution)/shard_map/expert/pallas_call | solution.py:519
  248.0 11.5 %expert.4 = (bf16[512,1408]{1,0:T(8,128)(2,1)}, bf16[512,1408]{1,0:T(8,128)(2,1)}, bf16[512,1408]{1,0:T(8,128)(2,1)}, bf16[256,2048]{1,0:T(8,128)(2,1)}) custom-call(s32[4]{0:T(128)} %pad_add_fusion.1.places, bf16[256,2048]{1,0:T(8,128)(2,1)} %copy-done.17, bf16[3,512,1408]{2,1,0:T(8,128)(2,1)} %get-tuple-element.90.refs_0_, ...), custom_call_target="tpu_custom_call" | custom-call | flops 1 | bytes 1 | tf_op jit(solution)/shard_map/expert/pallas_call | solution.py:519
  262.6 11.5 %expert.5 = (bf16[512,1408]{1,0:T(8,128)(2,1)}, bf16[512,1408]{1,0:T(8,128)(2,1)}, bf16[512,1408]{1,0:T(8,128)(2,1)}, bf16[256,2048]{1,0:T(8,128)(2,1)}) custom-call(s32[4]{0:T(128)} %pad_add_fusion.1.places, bf16[256,2048]{1,0:T(8,128)(2,1)} %copy-done.18, ...), custom_call_target="tpu_custom_call", output_to_operand_aliasing={{0}: (6, {}), {1}: (7, {}), {2}: (8, {})} | custom-call | flops 1 | bytes 1 | tf_op jit(solution)/shard_map/expert/pallas_call | solution.py:519
  275.8 8.7 %shared_forward.1 = (bf16[1024,384]{1,0:T(8,128)(2,1)}, bf16[1024,384]{1,0:T(8,128)(2,1)}, bf16[1024,384]{1,0:T(8,128)(2,1)}, f32[1024,128]{1,0:T(8,128)}) custom-call(bf16[1024,2048]{1,0:T(8,128)(2,1)} %all-gather.9.cloned.1.call-done.branch.refs_0_, bf16[1280,2048]{1,0:T(8,128)(2,1)} %fusion.7.refs_0_.weights.router.down, ...), custom_call_target="tpu_custom_call" | custom-call | flops 1 | bytes 1 | tf_op jit(solution)/shard_map/shared_forward/pallas_call | solution.py:782
  284.5 4.7 collective-permute-done.7.other_b
  290.2 9.4 %combine.1 = bf16[1024,2048]{1,0:T(8,128)(2,1)} custom-call(s32[2]{0:T(128)} %pad_add_fusion.named, bf16[1024,384]{1,0:T(8,128)(2,1)} %get-tuple-element.102.inner.refs_3_, bf16[1280,2048]{1,0:T(8,128)(2,1)} %fusion.7.refs_0_.weights.router.down, bf16[8,128,128]{2,1,0:T(8,128)(2,1)} %add_convert_fusion.1.refs_3_.slots, ...), custom_call_target="tpu_custom_call" | custom-call | flops 1 | bytes 1 | tf_op jit(solution)/shard_map/combine/pallas_call | solution.py:860
  303.4 3.6 collective-permute-done.14
  308.8 3.8 collective-permute-done.15
  321.0 25.9 %reduce-scatter.8.cloned.1.call-done = bf16[128,2048]{1,0:T(8,128)(2,1)} async-done(((bf16[1024,2048]{1,0:T(8,128)(2,1)}), bf16[128,2048]{1,0:T(8,128)(2,1)}) %reduce-scatter.8.cloned.1.call-update) | async-done | bytes 524304 | tf_op jit(solution)/shard_map/reduce_scatter | solution.py:1510
  360.8 4.7 collective-permute-done.10
  366.8 9.5 %collective-permute-done.11 = f32[8,128]{1,0:T(8,128)S(1)} collective-permute-done((f32[8,128]{1,0:T(8,128)S(1)}, f32[8,128]{1,0:T(8,128)S(1)}, u32[]{:S(2)}, u32[]{:S(2)}) %collective-permute-start.11) | collective-permute-done | bytes 4128 | tf_op jit(solution)/shard_map/ppermute | solution.py:1350
  380.5 15.4 %all-gather.11.cloned.1.call-done.grad.refs_1_ = bf16[1024,2048]{1,0:T(8,128)(2,1)} async-done(((bf16[128,2048]{1,0:T(8,128)(2,1)}), bf16[1024,2048]{1,0:T(8,128)(2,1)}) %all-gather.11.cloned.1.call-update) | async-done | bytes 4194320 | tf_op jit(solution)/shard_map/all_gather | solution.py:1518
  395.9 7.0 out_grads.1
  404.4 18.1 %expert_back.2 = (bf16[512,1408]{1,0:T(8,128)(2,1)}, bf16[512,1408]{1,0:T(8,128)(2,1)}, bf16[512,2048]{1,0:T(8,128)(2,1)}) custom-call(s32[4]{0:T(128)} %pad_add_fusion.1.places, bf16[512,2048]{1,0:T(8,128)(2,1)} %get-tuple-element.107.out_grad.refs_0_, bf16[512,1408]{1,0:T(8,128)(2,1)} %get-tuple-element.108.act, ...), custom_call_target="tpu_custom_call" | custom-call | flops 1 | bytes 1 | tf_op jit(solution)/shard_map/expert_back/pallas_call | solution.py:519
  422.5 6.3 shared_back.1.refs_4_.grads.refs_2_
  430.5 18.2 %expert_back.3 = (bf16[512,1408]{1,0:T(8,128)(2,1)}, bf16[512,1408]{1,0:T(8,128)(2,1)}, bf16[512,2048]{1,0:T(8,128)(2,1)}) custom-call(s32[4]{0:T(128)} %pad_add_fusion.1.places, bf16[512,2048]{1,0:T(8,128)(2,1)} %copy-done.5, bf16[512,1408]{1,0:T(8,128)(2,1)} %get-tuple-element.114.act, bf16[512,1408]{1,0:T(8,128)(2,1)} %get-tuple-element.115.slope, ...), custom_call_target="tpu_custom_call" | custom-call | flops 1 | bytes 1 | tf_op jit(solution)/shard_map/expert_back/pallas_call | solution.py:519
  452.8 13.4 %down_grad.1 = (bf16[2,1,512,1408]{3,2,1,0:T(8,128)(2,1)}, bf16[512,1408]{1,0:T(8,128)(2,1)}, bf16[512,1408]{1,0:T(8,128)(2,1)}) custom-call(s32[4]{0:T(128)} %pad_add_fusion.1.places, bf16[512,2048]{1,0:T(8,128)(2,1)} %get-tuple-element.107.out_grad.refs_0_, bf16[512,2048]{1,0:T(8,128)(2,1)} %copy-done.5, bf16[512,1408]{1,0:T(8,128)(2,1)} %get-tuple-element.117.refs_2_, ...), custom_call_target="tpu_custom_call" | custom-call | flops 1 | bytes 1 | tf_op jit(solution)/shard_map/down_grad/pallas_call | solution.py:597
  480.8 10.4 %combine_back.1.refs_7_ = bf16[1024,2048]{1,0:T(8,128)(2,1)} custom-call(bf16[1024,768]{1,0:T(8,128)(2,1)} %shared_back.1.refs_4_.grads.refs_2_, bf16[1024,128]{1,0:T(8,128)(2,1)} %get-tuple-element.171.logit_grad, bf16[1280,2048]{1,0:T(8,128)(2,1)} %fusion.7.refs_0_.weights.router.down, bf16[1280,2048]{1,0:T(8,128)(2,1)} %fusion.7.refs_0_.weights.router.down, ...), custom_call_target="tpu_custom_call" | custom-call | flops 1 | bytes 1 | tf_op jit(solution)/shard_map/combine_back/pallas_call | solution.py:957
  493.4 24.6 %gate_up_grad.1 = (bf16[2,2,512,1408]{3,2,1,0:T(8,128)(2,1)}, bf16[512,1408]{1,0:T(8,128)(2,1)}, bf16[512,1408]{1,0:T(8,128)(2,1)}, bf16[512,1408]{1,0:T(8,128)(2,1)}, bf16[512,1408]{1,0:T(8,128)(2,1)}) custom-call(s32[4]{0:T(128)} %pad_add_fusion.1.places, bf16[512,2048]{1,0:T(8,128)(2,1)} %get-tuple-element.95.slot_in.refs_0_, ...), custom_call_target="tpu_custom_call" | custom-call | flops 1 | bytes 1 | tf_op jit(solution)/shard_map/gate_up_grad/pallas_call | solution.py:597
  519.4 12.9 %shared_grads.1 = (bf16[2,1,512,1152]{3,2,1,0:T(8,128)(2,1)}, bf16[512,1152]{1,0:T(8,128)(2,1)}, bf16[512,1152]{1,0:T(8,128)(2,1)}) custom-call(s32[4]{0:T(128)} %pad_add_fusion.1.places, bf16[1024,2048]{1,0:T(8,128)(2,1)} %all-gather.9.cloned.1.call-done.branch.refs_0_, bf16[1024,2048]{1,0:T(8,128)(2,1)} %all-gather.11.cloned.1.call-done.grad.refs_1_, ...), custom_call_target="tpu_custom_call" | custom-call | flops 1 | bytes 1 | tf_op jit(solution)/shard_map/shared_grads/pallas_call | solution.py:597
  532.3 9.2 %collective-permute-done.27.refs_2_.arrived = bf16[512,1408]{1,0:T(8,128)(2,1)} collective-permute-done((bf16[512,1408]{1,0:T(8,128)(2,1)}, bf16[512,1408]{1,0:T(8,128)(2,1)}, u32[]{:S(2)}, u32[]{:S(2)}) %collective-permute-start.27) | collective-permute-done | bytes 1441824 | tf_op jit(solution)/shard_map/ppermute | solution.py:1279
  557.2 21.1 %collective-permute-done.32.arrived = bf16[512,1408]{1,0:T(8,128)(2,1)} collective-permute-done((bf16[512,1408]{1,0:T(8,128)(2,1)}, bf16[512,1408]{1,0:T(8,128)(2,1)}, u32[]{:S(2)}, u32[]{:S(2)}) %collective-permute-start.32) | collective-permute-done | bytes 1441824 | tf_op jit(solution)/shard_map/ppermute | solution.py:1279
  581.6 9.2 %all-gather.13.cloned.1.call-done.grad.refs_1_ = bf16[1024,2048]{1,0:T(8,128)(2,1)} async-done(((bf16[128,2048]{1,0:T(8,128)(2,1)}), bf16[1024,2048]{1,0:T(8,128)(2,1)}) %all-gather.13.cloned.1.call-update) | async-done | bytes 4194320 | tf_op jit(solution)/shard_map/all_gather | solution.py:1611
  590.9 24.0 %attend_back.1 = (bf16[1024,384]{1,0:T(8,128)(2,1)}, bf16[1024,2048]{1,0:T(8,128)(2,1)}, bf16[1024,512]{1,0:T(8,128)(2,1)}, bf16[1024,128]{1,0:T(8,128)(2,1)}, b...) custom-call(bf16[1024,2048]{1,0:T(8,128)(2,1)} %all-gather.13.cloned.1.call-done.grad.refs_1_, ...), custom_call_target="tpu_custom_call" | custom-call | flops 1 | bytes 1 | tf_op jit(solution)/shard_map/attend_back/pallas_call | solution.py:311
  614.9 5.7 collective-permute-done.29.refs_1_.arrived
  621.7 5.2 latent_grads.1
  639.7 4.8 gain_part.1.refs_6_.part
  644.5 11.3 %attention_grads.1 = (bf16[2,1,512,640]{3,2,1,0:T(8,128)(2,1)}, bf16[512,640]{1,0:T(8,128)(2,1)}, bf16[512,640]{1,0:T(8,128)(2,1)}) custom-call(s32[4]{0:T(128)} %pad_add_fusion.1.places, bf16[1024,2048]{1,0:T(8,128)(2,1)} %all-gather.7.cloned.1.call-done.normed.refs_0_.right, bf16[1024,2048]{1,0:T(8,128)(2,1)} %all-gather.13.cloned.1.call-done.grad.refs_1_, ...), custom_call_target="tpu_custom_call" | custom-call | flops 1 | bytes 1 | tf_op jit(solution)/shard_map/attention_grads/pallas_call | solution.py:597
  655.8 5.6 place_experts.3.refs_1_
  670.8 10.0 %collective-permute-done.35.back = bf16[128,640]{1,0:T(8,128)(2,1)S(1)} collective-permute-done((bf16[128,640]{1,0:T(8,128)(2,1)}, bf16[128,640]{1,0:T(8,128)(2,1)S(1)}, u32[]{:S(2)}, u32[]{:S(2)}) %collective-permute-start.35) | collective-permute-done | bytes 163872 | tf_op jit(solution)/shard_map/ppermute | solution.py:1658
  698.8 5.3 place_experts.4.refs_4_
  704.1 5.1 place_experts.5.refs_5_
  724.4 5.0 collective-permute-done.42
  732.1 5.6 collective-permute-done.43
  747.9 10.1 %collective-permute-done.45.arrived = bf16[512,640]{1,0:T(8,128)(2,1)} collective-permute-done((bf16[512,640]{1,0:T(8,128)(2,1)}, bf16[512,640]{1,0:T(8,128)(2,1)}, u32[]{:S(2)}, u32[]{:S(2)}) %collective-permute-start.45) | collective-permute-done | bytes 655392 | tf_op jit(solution)/shard_map/ppermute | solution.py:1279
  760.9 9.0 %collective-permute-done.48.other = bf16[128,512]{1,0:T(8,128)(2,1)S(1)} collective-permute-done((bf16[128,512]{1,0:T(8,128)(2,1)S(1)}, bf16[128,512]{1,0:T(8,128)(2,1)S(1)}, u32[]{:S(2)}, u32[]{:S(2)}) %collective-permute-start.48) | collective-permute-done | bytes 131104 | tf_op jit(solution)/shard_map/ppermute | solution.py:1279
  772.3 4.4 tokens_back.1.refs_1_
  782.3 4.4 beside.1.refs_0_
  (329 shorter events, 218.9 us)
Async XLA Ops:
  7.2 54.2 %all-gather.7.cloned.1.call-start = ((), (), s32[]{:S(2)}) async-start(), calls=%async_computation.5 | async-start | bytes 4718592 | tf_op jit(solution)/shard_map/all_gather | solution.py:1395
  11.4 156.0 %reduce-scatter.6.cloned.1.call-start = ((), (), s32[]{:S(2)}) async-start(), calls=%async_computation.6 | async-start | bytes 4718592 | tf_op jit(solution)/shard_map/reduce_scatter | solution.py:1472
  19.0 60.9 %collective-permute-start.1 = (bf16[3,512,1408]{2,1,0:T(8,128)(2,1)}, bf16[3,512,1408]{2,1,0:T(8,128)(2,1)}, u32[]{:S(2)}, u32[]{:S(2)}) collective-permute-start(bf16[3,512,1408]{2,1,0:T(8,128)(2,1)} %get-tuple-element.88), channel_id=1, source_target_pairs={{0,16},{1,9},{2,18},{3,11},{4,20},{5,13},{6,22},{7,15},{8,24},{9,1... | collective-permute-start | bytes 12976136 | tf_op jit(solution)/shard_map/ppermute | solution.py:1279
  69.8 32.1 %collective-permute-start = (bf16[1024,640]{1,0:T(8,128)(2,1)}, bf16[1024,640]{1,0:T(8,128)(2,1)S(1)}, u32[]{:S(2)}, u32[]{:S(2)}) collective-permute-start(bf16[1024,640]{1,0:T(8,128)(2,1)} %get-tuple-element.87.refs_2_.refs_4_.refs_6_.refs_7_), channel_id=1, source_target_pairs={{0,8},{8,16},{16,24},{1,9},{9,17},{17,25},{2,10},{10,18},{18,26},{... | collective-permute-start | bytes 3932168 | tf_op jit(solution)/shard_map/ppermute | solution.py:1468
  116.7 103.9 %all-gather.9.cloned.1.call-start = ((), (), s32[]{:S(2)}) async-start(), calls=%async_computation.7 | async-start | bytes 4718592 | tf_op jit(solution)/shard_map/all_gather | solution.py:1476
  116.8 50.6 %collective-permute-start.2 = (bf16[3,512,1408]{2,1,0:T(8,128)(2,1)}, bf16[3,512,1408]{2,1,0:T(8,128)(2,1)}, u32[]{:S(2)}, u32[]{:S(2)}) collective-permute-start(bf16[3,512,1408]{2,1,0:T(8,128)(2,1)} %get-tuple-element.90.refs_0_), channel_id=1, source_target_pairs={{0,8},{1,17},{2,10},{3,19},{4,12},{5,21},{6,14},{7,23},{8,0},{9,25... | collective-permute-start | bytes 12976136 | tf_op jit(solution)/shard_map/ppermute | solution.py:1279
  170.3 176.6 %reduce-scatter.8.cloned.1.call-start = ((), (), s32[]{:S(2)}) async-start(), calls=%async_computation.8 | async-start | bytes 4718592 | tf_op jit(solution)/shard_map/reduce_scatter | solution.py:1510
  170.4 50.3 %collective-permute-start.3 = (bf16[3,512,1408]{2,1,0:T(8,128)(2,1)}, bf16[3,512,1408]{2,1,0:T(8,128)(2,1)}, u32[]{:S(2)}, u32[]{:S(2)}) collective-permute-start(bf16[3,512,1408]{2,1,0:T(8,128)(2,1)} %collective-permute-done.1.refs_8_.refs_1_), channel_id=1, source_target_pairs={{0,8},{1,17},{2,10},{3,19},{4,12},{5,21},{6,14},{7,23},{8,0},{9,25... | collective-permute-start | bytes 12976136 | tf_op jit(solution)/shard_map/ppermute | solution.py:1279
  226.9 20.1 %collective-permute-start.5 = (bf16[256,2048]{1,0:T(8,128)(2,1)}, bf16[256,2048]{1,0:T(8,128)(2,1)S(1)}, u32[]{:S(2)}, u32[]{:S(2)}) collective-permute-start(bf16[256,2048]{1,0:T(8,128)(2,1)} %get-tuple-element.94), channel_id=1, source_target_pairs={{0,16},{1,9},{2,18},{3,11},{4,20},{5,13},{6,22},{7,15},{8,24},{9,1... | collective-permute-start | bytes 3145736 | tf_op jit(solution)/shard_map/ppermute | solution.py:1279
  229.8 31.7 %collective-permute-start.4 = (bf16[256,2048]{1,0:T(8,128)(2,1)}, bf16[256,2048]{1,0:T(8,128)(2,1)S(1)}, u32[]{:S(2)}, u32[]{:S(2)}) collective-permute-start(bf16[256,2048]{1,0:T(8,128)(2,1)} %get-tuple-element.93), channel_id=1, source_target_pairs={{0,16},{1,9},{2,18},{3,11},{4,20},{5,13},{6,22},{7,15},{8,24},{9,1... | collective-permute-start | bytes 3145736 | tf_op jit(solution)/shard_map/ppermute | solution.py:1279
  259.5 15.3 %collective-permute-start.6 = (bf16[256,2048]{1,0:T(8,128)(2,1)}, bf16[256,2048]{1,0:T(8,128)(2,1)S(1)}, u32[]{:S(2)}, u32[]{:S(2)}) collective-permute-start(bf16[256,2048]{1,0:T(8,128)(2,1)} %get-tuple-element.101), channel_id=1, source_target_pairs={{0,16},{1,9},{2,18},{3,11},{4,20},{5,13},{6,22},{7,15},{8,24},{9,1... | collective-permute-start | bytes 3145736 | tf_op jit(solution)/shard_map/ppermute | solution.py:1279
  274.1 15.1 %collective-permute-start.7 = (bf16[256,2048]{1,0:T(8,128)(2,1)}, bf16[256,2048]{1,0:T(8,128)(2,1)S(1)}, u32[]{:S(2)}, u32[]{:S(2)}) collective-permute-start(bf16[256,2048]{1,0:T(8,128)(2,1)} %get-tuple-element.100.refs_0_), channel_id=1, source_target_pairs={{0,16},{1,9},{2,18},{3,11},{4,20},{5,13},{6,22},{7,15},{8,24},{9,1... | collective-permute-start | bytes 3145736 | tf_op jit(solution)/shard_map/ppermute | solution.py:1279
  299.6 96.3 %all-gather.11.cloned.1.call-start = ((), (), s32[]{:S(2)}) async-start(), calls=%async_computation.9 | async-start | bytes 4718592 | tf_op jit(solution)/shard_map/all_gather | solution.py:1518
  350.4 191.2 %reduce-scatter.10.cloned.1.call-start = ((), (), s32[]{:S(2)}) async-start(), calls=%async_computation.10 | async-start | bytes 4718592 | tf_op jit(solution)/shard_map/reduce_scatter | solution.py:1573
  350.5 30.0 %collective-permute-start.18 = (bf16[1024,512]{1,0:T(8,128)(2,1)}, bf16[1024,512]{1,0:T(8,128)(2,1)S(1)}, u32[]{:S(2)}, u32[]{:S(2)}) collective-permute-start(bf16[1024,512]{1,0:T(8,128)(2,1)} %get-tuple-element.106), channel_id=1, source_target_pairs={{0,8},{8,16},{16,24},{1,9},{9,17},{17,25},{2,10},{10,18},{18,26},{... | collective-permute-start | bytes 3145736 | tf_op jit(solution)/shard_map/ppermute | solution.py:1469
  365.6 10.7 %collective-permute-start.11 = (f32[8,128]{1,0:T(8,128)S(1)}, f32[8,128]{1,0:T(8,128)S(1)}, u32[]{:S(2)}, u32[]{:S(2)}) collective-permute-start(f32[8,128]{1,0:T(8,128)S(1)} %add.213), channel_id=1, source_target_pairs={{0,8},{1,9},{2,10},{3,11},{4,12},{5,13},{6,14},{7,15},{8,0},{9,1},... | collective-permute-start | bytes 12296 | tf_op jit(solution)/shard_map/ppermute | solution.py:1350
  402.9 26.3 %collective-permute-start.19 = (bf16[512,2048]{1,0:T(8,128)(2,1)}, bf16[512,2048]{1,0:T(8,128)(2,1)S(1)}, u32[]{:S(2)}, u32[]{:S(2)}) collective-permute-start(bf16[512,2048]{1,0:T(8,128)(2,1)} %get-tuple-element.113), channel_id=1, source_target_pairs={{0,16},{1,9},{2,18},{3,11},{4,20},{5,13},{6,22},{7,15},{8,24},{9,1... | collective-permute-start | bytes 6291464 | tf_op jit(solution)/shard_map/ppermute | solution.py:1279
  448.8 30.8 %collective-permute-start.20 = (bf16[512,2048]{1,0:T(8,128)(2,1)}, bf16[512,2048]{1,0:T(8,128)(2,1)S(1)}, u32[]{:S(2)}, u32[]{:S(2)}) collective-permute-start(bf16[512,2048]{1,0:T(8,128)(2,1)} %get-tuple-element.116.refs_4_), channel_id=1, source_target_pairs={{0,16},{1,9},{2,18},{3,11},{4,20},{5,13},{6,22},{7,15},{8,24},{9,1... | collective-permute-start | bytes 6291464 | tf_op jit(solution)/shard_map/ppermute | solution.py:1279
  470.1 6.8 collective-permute-start.24
  471.5 7.4 collective-permute-start.23
  471.5 7.4 collective-permute-start.22
  491.2 99.6 %all-gather.13.cloned.1.call-start = ((), (), s32[]{:S(2)}) async-start(), calls=%async_computation.11 | async-start | bytes 4718592 | tf_op jit(solution)/shard_map/all_gather | solution.py:1611
  491.3 41.0 %collective-permute-start.25 = (bf16[512,1408]{1,0:T(8,128)(2,1)}, bf16[512,1408]{1,0:T(8,128)(2,1)S(1)}, u32[]{:S(2)}, u32[]{:S(2)}) collective-permute-start(bf16[512,1408]{1,0:T(8,128)(2,1)} %get-tuple-element.122), channel_id=1, source_target_pairs={{0,8},{1,17},{2,10},{3,19},{4,12},{5,21},{6,14},{7,23},{8,0},{9,25... | collective-permute-start | bytes 4325384 | tf_op jit(solution)/shard_map/ppermute | solution.py:1279
  492.8 39.5 %collective-permute-start.26 = (bf16[512,1408]{1,0:T(8,128)(2,1)}, bf16[512,1408]{1,0:T(8,128)(2,1)S(1)}, u32[]{:S(2)}, u32[]{:S(2)}) collective-permute-start(bf16[512,1408]{1,0:T(8,128)(2,1)} %get-tuple-element.123), channel_id=1, source_target_pairs={{0,8},{1,17},{2,10},{3,19},{4,12},{5,21},{6,14},{7,23},{8,0},{9,25... | collective-permute-start | bytes 4325384 | tf_op jit(solution)/shard_map/ppermute | solution.py:1279
  518.0 23.6 %collective-permute-start.27 = (bf16[512,1408]{1,0:T(8,128)(2,1)}, bf16[512,1408]{1,0:T(8,128)(2,1)}, u32[]{:S(2)}, u32[]{:S(2)}) collective-permute-start(bf16[512,1408]{1,0:T(8,128)(2,1)} %get-tuple-element.128), channel_id=1, source_target_pairs={{0,8},{1,17},{2,10},{3,19},{4,12},{5,21},{6,14},{7,23},{8,0},{9,25... | collective-permute-start | bytes 4325384 | tf_op jit(solution)/shard_map/ppermute | solution.py:1279
  545.0 121.0 %reduce-scatter.14.cloned.1.call-start = ((), (), s32[]{:S(2)}) async-start(), calls=%async_computation.13 | async-start | bytes 2949120 | tf_op jit(solution)/shard_map/reduce_scatter | solution.py:1626
  545.0 33.3 %collective-permute-start.32 = (bf16[512,1408]{1,0:T(8,128)(2,1)}, bf16[512,1408]{1,0:T(8,128)(2,1)}, u32[]{:S(2)}, u32[]{:S(2)}) collective-permute-start(bf16[512,1408]{1,0:T(8,128)(2,1)} %get-tuple-element.140), channel_id=1, source_target_pairs={{0,8},{1,17},{2,10},{3,19},{4,12},{5,21},{6,14},{7,23},{8,0},{9,25... | collective-permute-start | bytes 4325384 | tf_op jit(solution)/shard_map/ppermute | solution.py:1279
  549.8 65.1 %collective-permute-start.30 = (bf16[512,1408]{1,0:T(8,128)(2,1)}, bf16[512,1408]{1,0:T(8,128)(2,1)S(1)}, u32[]{:S(2)}, u32[]{:S(2)}) collective-permute-start(bf16[512,1408]{1,0:T(8,128)(2,1)} %add_pair.6.refs_8_), channel_id=1, source_target_pairs={{0,16},{1,9},{2,18},{3,11},{4,20},{5,13},{6,22},{7,15},{8,24},{9,1... | collective-permute-start | bytes 4325384 | tf_op jit(solution)/shard_map/ppermute | solution.py:1279
  553.7 66.9 %collective-permute-start.31 = (bf16[512,1408]{1,0:T(8,128)(2,1)}, bf16[512,1408]{1,0:T(8,128)(2,1)S(1)}, u32[]{:S(2)}, u32[]{:S(2)}) collective-permute-start(bf16[512,1408]{1,0:T(8,128)(2,1)} %add_pair.7.refs_9_), channel_id=1, source_target_pairs={{0,16},{1,9},{2,18},{3,11},{4,20},{5,13},{6,22},{7,15},{8,24},{9,1... | collective-permute-start | bytes 4325384 | tf_op jit(solution)/shard_map/ppermute | solution.py:1279
  555.2 59.6 %collective-permute-start.28 = (bf16[512,1152]{1,0:T(8,128)(2,1)}, bf16[512,1152]{1,0:T(8,128)(2,1)}, u32[]{:S(2)}, u32[]{:S(2)}) collective-permute-start(bf16[512,1152]{1,0:T(8,128)(2,1)} %get-tuple-element.138), channel_id=1, source_target_pairs={{0,8},{1,17},{2,10},{3,19},{4,12},{5,21},{6,14},{7,23},{8,0},{9,25... | collective-permute-start | bytes 3538952 | tf_op jit(solution)/shard_map/ppermute | solution.py:1279
  555.7 64.8 %collective-permute-start.29 = (bf16[512,1152]{1,0:T(8,128)(2,1)}, bf16[512,1152]{1,0:T(8,128)(2,1)}, u32[]{:S(2)}, u32[]{:S(2)}) collective-permute-start(bf16[512,1152]{1,0:T(8,128)(2,1)} %get-tuple-element.139), channel_id=1, source_target_pairs={{0,8},{1,17},{2,10},{3,19},{4,12},{5,21},{6,14},{7,23},{8,0},{9,25... | collective-permute-start | bytes 3538952 | tf_op jit(solution)/shard_map/ppermute | solution.py:1279
  626.9 145.4 %reduce-scatter.12.cloned.1.call-start = ((), (), s32[]{:S(2)}) async-start(), calls=%async_computation.12 | async-start | bytes 4718592 | tf_op jit(solution)/shard_map/reduce_scatter | solution.py:1634
  627.7 153.7 %all-gather.15.cloned.1.call-start = ((), (), s32[]{:S(2)}) async-start(), calls=%async_computation.14 | async-start | bytes 2875392 | tf_op jit(solution)/shard_map/all_gather | solution.py:1708
  629.7 35.8 %collective-permute-start.34 = (bf16[512,1408]{1,0:T(8,128)(2,1)}, bf16[512,1408]{1,0:T(8,128)(2,1)S(1)}, u32[]{:S(2)}, u32[]{:S(2)}) collective-permute-start(bf16[512,1408]{1,0:T(8,128)(2,1)} %get-tuple-element.144), channel_id=1, source_target_pairs={{0,8},{1,17},{2,10},{3,19},{4,12},{5,21},{6,14},{7,23},{8,0},{9,25... | collective-permute-start | bytes 4325384 | tf_op jit(solution)/shard_map/ppermute | solution.py:1279
  631.2 34.7 %collective-permute-start.33 = (bf16[512,1408]{1,0:T(8,128)(2,1)}, bf16[512,1408]{1,0:T(8,128)(2,1)S(1)}, u32[]{:S(2)}, u32[]{:S(2)}) collective-permute-start(bf16[512,1408]{1,0:T(8,128)(2,1)} %add_pair.8.refs_4_), channel_id=1, source_target_pairs={{0,16},{1,9},{2,18},{3,11},{4,20},{5,13},{6,22},{7,15},{8,24},{9,1... | collective-permute-start | bytes 4325384 | tf_op jit(solution)/shard_map/ppermute | solution.py:1279
  633.3 70.8 %collective-permute-start.39 = (bf16[512,1408]{1,0:T(8,128)(2,1)}, bf16[512,1408]{1,0:T(8,128)(2,1)}, u32[]{:S(2)}, u32[]{:S(2)}) collective-permute-start(bf16[512,1408]{1,0:T(8,128)(2,1)} %get-tuple-element.147), channel_id=1, source_target_pairs={{0,8},{1,17},{2,10},{3,19},{4,12},{5,21},{6,14},{7,23},{8,0},{9,25... | collective-permute-start | bytes 4325384 | tf_op jit(solution)/shard_map/ppermute | solution.py:1279
  668.8 12.0 %collective-permute-start.35 = (bf16[128,640]{1,0:T(8,128)(2,1)}, bf16[128,640]{1,0:T(8,128)(2,1)S(1)}, u32[]{:S(2)}, u32[]{:S(2)}) collective-permute-start(bf16[128,640]{1,0:T(8,128)(2,1)} %first_block.3), channel_id=1, source_target_pairs={{8,0},{16,8},{24,16},{9,1},{17,9},{25,17},{10,2},{18,10},{26,18},{... | collective-permute-start | bytes 491528 | tf_op jit(solution)/shard_map/ppermute | solution.py:1658
  683.6 25.7 %collective-permute-start.38 = (bf16[128,640]{1,0:T(8,128)(2,1)}, bf16[128,640]{1,0:T(8,128)(2,1)S(1)}, u32[]{:S(2)}, u32[]{:S(2)}) collective-permute-start(bf16[128,640]{1,0:T(8,128)(2,1)} %get-tuple-element.145.projected.refs_0_), channel_id=1, source_target_pairs={{0,6},{1,7},{2,4},{3,5},{4,2},{5,3},{6,0},{7,1},{8,14},{9,15},{10,... | collective-permute-start | bytes 491528 | tf_op jit(solution)/shard_map/ppermute | solution.py:1318
  685.2 24.1 %collective-permute-start.37 = (bf16[128,640]{1,0:T(8,128)(2,1)}, bf16[128,640]{1,0:T(8,128)(2,1)S(1)}, u32[]{:S(2)}, u32[]{:S(2)}) collective-permute-start(bf16[128,640]{1,0:T(8,128)(2,1)} %get-tuple-element.145.projected.refs_0_), channel_id=1, source_target_pairs={{0,4},{1,5},{2,6},{3,7},{4,0},{5,1},{6,2},{7,3},{8,12},{9,13},{10,... | collective-permute-start | bytes 491528 | tf_op jit(solution)/shard_map/ppermute | solution.py:1318
  685.5 23.8 %collective-permute-start.36 = (bf16[128,640]{1,0:T(8,128)(2,1)}, bf16[128,640]{1,0:T(8,128)(2,1)S(1)}, u32[]{:S(2)}, u32[]{:S(2)}) collective-permute-start(bf16[128,640]{1,0:T(8,128)(2,1)} %get-tuple-element.145.projected.refs_0_), channel_id=1, source_target_pairs={{0,2},{1,3},{2,0},{3,1},{4,6},{5,7},{6,4},{7,5},{8,10},{9,11},{10,... | collective-permute-start | bytes 491528 | tf_op jit(solution)/shard_map/ppermute | solution.py:1318
  722.4 7.1 collective-permute-start.42
  730.6 7.1 collective-permute-start.43
  738.5 38.2 %collective-permute-start.49 = (bf16[512,1152]{1,0:T(8,128)(2,1)S(1)}, bf16[512,1152]{1,0:T(8,128)(2,1)S(1)}, u32[]{:S(2)}, u32[]{:S(2)}) collective-permute-start(bf16[512,1152]{1,0:T(8,128)(2,1)S(1)} %copy-done.15), channel_id=1, source_target_pairs={{0,16},{1,9},{2,18},{3,11},{4,20},{5,13},{6,22},{7,15},{8,24},{9,1... | collective-permute-start | bytes 3538952 | tf_op jit(solution)/shard_map/ppermute | solution.py:1279
  740.0 18.0 %collective-permute-start.45 = (bf16[512,640]{1,0:T(8,128)(2,1)}, bf16[512,640]{1,0:T(8,128)(2,1)}, u32[]{:S(2)}, u32[]{:S(2)}) collective-permute-start(bf16[512,640]{1,0:T(8,128)(2,1)} %get-tuple-element.151), channel_id=1, source_target_pairs={{0,8},{1,17},{2,10},{3,19},{4,12},{5,21},{6,14},{7,23},{8,0},{9,25... | collective-permute-start | bytes 1966088 | tf_op jit(solution)/shard_map/ppermute | solution.py:1279
  740.6 20.3 %collective-permute-start.47 = (bf16[128,512]{1,0:T(8,128)(2,1)S(1)}, bf16[128,512]{1,0:T(8,128)(2,1)S(1)}, u32[]{:S(2)}, u32[]{:S(2)}) collective-permute-start(bf16[128,512]{1,0:T(8,128)(2,1)S(1)} %bitcast.83), channel_id=1, source_target_pairs={{0,8},{1,17},{2,10},{3,19},{4,12},{5,21},{6,14},{7,23},{8,0},{9,25... | collective-permute-start | bytes 393224 | tf_op jit(solution)/shard_map/ppermute | solution.py:1279
  742.0 27.9 %collective-permute-start.48 = (bf16[128,512]{1,0:T(8,128)(2,1)S(1)}, bf16[128,512]{1,0:T(8,128)(2,1)S(1)}, u32[]{:S(2)}, u32[]{:S(2)}) collective-permute-start(bf16[128,512]{1,0:T(8,128)(2,1)S(1)} %copy-done.38), channel_id=1, source_target_pairs={{0,16},{1,9},{2,18},{3,11},{4,20},{5,13},{6,22},{7,15},{8,24},{9,1... | collective-permute-start | bytes 393224 | tf_op jit(solution)/shard_map/ppermute | solution.py:1279
  745.9 41.7 %collective-permute-start.44 = (bf16[512,640]{1,0:T(8,128)(2,1)}, bf16[512,640]{1,0:T(8,128)(2,1)S(1)}, u32[]{:S(2)}, u32[]{:S(2)}) collective-permute-start(bf16[512,640]{1,0:T(8,128)(2,1)} %get-tuple-element.150), channel_id=1, source_target_pairs={{0,8},{1,17},{2,10},{3,19},{4,12},{5,21},{6,14},{7,23},{8,0},{9,25... | collective-permute-start | bytes 1966088 | tf_op jit(solution)/shard_map/ppermute | solution.py:1279
  760.3 27.2 %collective-permute-start.46 = (bf16[512,640]{1,0:T(8,128)(2,1)}, bf16[512,640]{1,0:T(8,128)(2,1)}, u32[]{:S(2)}, u32[]{:S(2)}) collective-permute-start(bf16[512,640]{1,0:T(8,128)(2,1)} %add_pair.11), channel_id=1, source_target_pairs={{0,16},{1,9},{2,18},{3,11},{4,20},{5,13},{6,22},{7,15},{8,24},{9,1... | collective-permute-start | bytes 1966088 | tf_op jit(solution)/shard_map/ppermute | solution.py:1279
  (67 other events, 427.2 us)
Sparse Core Ops, SparseCore 0:
  11.5 49.8 all-gather.6
  116.8 49.6 reduce-scatter.5
  170.4 46.4 all-gather.8
  299.7 47.1 reduce-scatter.7
  350.5 45.2 all-gather.10
  491.4 48.5 reduce-scatter.9
  545.1 45.7 all-gather.12
  627.0 36.1 reduce-scatter.13
  666.1 59.6 reduce-scatter.11
  738.6 32.1 all-gather.14
